TPU v7x, 32 devices: a whole 2x2x4 slice. The times are simulated.
32 devices in a mesh: dp: 8 (over z, y), mp: 4 (over x, core).
Axes of the slice: x: 2, y: 2, z: 4, core: 2. Of those that a mesh axis runs over, the one named last changes fastest.
Arguments:
- patches: bfloat16 [192, 49, 3072], P(('dp', 'mp')), may hold values from -6 to 6
- keep_list: int32 [192, 49], P(('dp', 'mp')), may hold values from 0 to 48, each once within a row
- keep_count: int32 [192], P(('dp', 'mp')), may hold values from 24 to 49, as said below
- labels: int32 [192], P(('dp', 'mp')), may hold values from 0 to 999
- patch_weight: float32 [3072, 1024], P(('dp', 'mp')), may hold values from -0.109375 to 0.109375
- vector_table: float32 [66, 1024], replicated, may hold values from -2 to 2
- head_table: float32 [1025, 1000], replicated, may hold values from -0.1875 to 0.1875
- joint_weight: float32 [2, 1024, 3, 1024], P(None, 'dp', None, 'mp'), may hold values from -0.1875 to 0.1875
- shift_table: float32 [2, 2, 1024], replicated, may hold values from -4 to 4
- output_weight: float32 [2, 1024, 1024], P(None, 'mp', 'dp'), may hold values from -0.5 to 0.5
- expand_weight: float32 [2, 1024, 4096], P(None, 'dp', 'mp'), may hold values from -0.1875 to 0.1875
- raise_table: float32 [2, 4096], replicated, may hold values from -4 to 4
- shrink_weight: float32 [2, 4096, 1024], P(None, 'mp', 'dp'), may hold values from -0.09375 to 0.09375
- patch_first: float32 [3072, 1024], P(('dp', 'mp')), may hold values from -5.722046e-06 to 5.722046e-06
- vector_first: float32 [66, 1024], replicated, may hold values from -5.722046e-06 to 5.722046e-06
- head_first: float32 [1025, 1000], replicated, may hold values from -5.722046e-06 to 5.722046e-06
- joint_first: float32 [2, 1024, 3, 1024], P(None, 'dp', None, 'mp'), may hold values from -5.722046e-06 to 5.722046e-06
- shift_first: float32 [2, 2, 1024], replicated, may hold values from -5.722046e-06 to 5.722046e-06
- output_first: float32 [2, 1024, 1024], P(None, 'mp', 'dp'), may hold values from -5.722046e-06 to 5.722046e-06
- expand_first: float32 [2, 1024, 4096], P(None, 'dp', 'mp'), may hold values from -5.722046e-06 to 5.722046e-06
- raise_first: float32 [2, 4096], replicated, may hold values from -5.722046e-06 to 5.722046e-06
- shrink_first: float32 [2, 4096, 1024], P(None, 'mp', 'dp'), may hold values from -5.722046e-06 to 5.722046e-06
- patch_second: float32 [3072, 1024], P(('dp', 'mp')), may hold values from 3.53544e-13 to 2.8555476e-12
- vector_second: float32 [66, 1024], replicated, may hold values from 3.53544e-13 to 2.8555476e-12
- head_second: float32 [1025, 1000], replicated, may hold values from 3.53544e-13 to 2.8555476e-12
- joint_second: float32 [2, 1024, 3, 1024], P(None, 'dp', None, 'mp'), may hold values from 3.53544e-13 to 2.8555476e-12
- shift_second: float32 [2, 2, 1024], replicated, may hold values from 3.53544e-13 to 2.8555476e-12
- output_second: float32 [2, 1024, 1024], P(None, 'mp', 'dp'), may hold values from 3.53544e-13 to 2.8555476e-12
- expand_second: float32 [2, 1024, 4096], P(None, 'dp', 'mp'), may hold values from 3.53544e-13 to 2.8555476e-12
- raise_second: float32 [2, 4096], replicated, may hold values from 3.53544e-13 to 2.8555476e-12
- shrink_second: float32 [2, 4096, 1024], P(None, 'mp', 'dp'), may hold values from 3.53544e-13 to 2.8555476e-12
Outputs:
- loss_total: float32 [], replicated
- gradient_norm: float32 [], replicated
- patch_update: float32 [3072, 1024], P(('dp', 'mp'))
- patch_momentum: float32 [3072, 1024], P(('dp', 'mp'))
- patch_variance: float32 [3072, 1024], P(('dp', 'mp'))
- vector_update: float32 [66, 1024], replicated
- vector_momentum: float32 [66, 1024], replicated
- vector_variance: float32 [66, 1024], replicated
- head_update: float32 [1025, 1000], replicated
- head_momentum: float32 [1025, 1000], replicated
- head_variance: float32 [1025, 1000], replicated
- joint_update: float32 [2, 1024, 3, 1024], P(None, 'dp', None, 'mp')
- joint_momentum: float32 [2, 1024, 3, 1024], P(None, 'dp', None, 'mp')
- joint_variance: float32 [2, 1024, 3, 1024], P(None, 'dp', None, 'mp')
- shift_update: float32 [2, 2, 1024], replicated
- shift_momentum: float32 [2, 2, 1024], replicated
- shift_variance: float32 [2, 2, 1024], replicated
- output_update: float32 [2, 1024, 1024], P(None, 'mp', 'dp')
- output_momentum: float32 [2, 1024, 1024], P(None, 'mp', 'dp')
- output_variance: float32 [2, 1024, 1024], P(None, 'mp', 'dp')
- expand_update: float32 [2, 1024, 4096], P(None, 'dp', 'mp')
- expand_momentum: float32 [2, 1024, 4096], P(None, 'dp', 'mp')
- expand_variance: float32 [2, 1024, 4096], P(None, 'dp', 'mp')
- raise_update: float32 [2, 4096], replicated
- raise_momentum: float32 [2, 4096], replicated
- raise_variance: float32 [2, 4096], replicated
- shrink_update: float32 [2, 4096, 1024], P(None, 'mp', 'dp')
- shrink_momentum: float32 [2, 4096, 1024], P(None, 'mp', 'dp')
- shrink_variance: float32 [2, 4096, 1024], P(None, 'mp', 'dp')
Inputs may be any that keep to these rules, and one draw needn't show every extreme that they name: `keep_list`: each row is an ordering of the patch numbers; the first keep_count entries of a row are the kept patches. `keep_count`: some image keeps all 49 patches and some exactly 24.
All inputs are finite; a program needn't handle non-finite values.
Results may differ from a plain program's by a relative error of at most 0.012.
Values may be sent and summed in bfloat16 or wider, within the bound.
No kernel may reach another device: no remote copies, remote signals or barrier semaphores. Data moves between devices by JAX's collectives and lax.ppermute only.
A program may use at most 256 MiB of HBM per device.

v0:
```python
import jax
import jax.numpy as jnp
from jax import lax
from jax.sharding import PartitionSpec as P

HEAD_DIM = 64
FF = 4096
CLASSES = 1000
PATCHES = 49
LAYERS = 2
STEP = 10
SLOTS = 50


group_rates = (0.01, 0.2, 0.01, 0.01, 0.1, 0.03, 0.01, 0.1, 0.01)
beta_one = 0.9
beta_two = 0.95
adam_eps = 1e-08
decay_rate = 0.1
clip_limit = 0.02
norm_eps = 1e-06
highest = lax.Precision.HIGHEST


def layer_norm(values, gain_row, shift_row):
    centre = values - jnp.mean(values, -1, keepdims=True)
    spread = jnp.mean(centre * centre, -1, keepdims=True)
    return centre * lax.rsqrt(spread + norm_eps) * gain_row + shift_row


def product(form, left, right):
    return jnp.einsum(form, left, right, preferred_element_type=jnp.float32)


def adamw(weight, moment_one, moment_two, gradient, rate):
    first_new = beta_one * moment_one + (1.0 - beta_one) * gradient
    second_new = beta_two * moment_two + (1.0 - beta_two) * gradient * gradient
    corrected = first_new / (1.0 - beta_one**STEP)
    scaled = second_new / (1.0 - beta_two**STEP)
    weight_new = weight - rate * (corrected / (jnp.sqrt(scaled) + adam_eps) + decay_rate * weight)
    return (weight_new, first_new, second_new)


def attention_scores(query_rows, key_rows, key_live):
    scores = product("nqhe,nkhe->nhqk", query_rows, key_rows) * 0.125
    return jnp.where(key_live[:, None, None, :], scores, -1e30)


def layer_forward(
    stream, key_share, layer_index, weights_now, vector_table, shift_table, raise_table
):
    joint, output, expand, shrink = weights_now
    row_base = SLOTS + 4 + 6 * layer_index
    local_width = joint.shape[2]
    local_hidden = expand.shape[1]
    heads_here = local_width // HEAD_DIM
    model_index = lax.axis_index("mp")
    shift_here = lax.dynamic_slice_in_dim(
        shift_table[layer_index], model_index * local_width, local_width, 1
    )
    raise_here = lax.dynamic_slice_in_dim(
        raise_table[layer_index], model_index * local_hidden, local_hidden, 0
    )
    normed = layer_norm(stream, vector_table[row_base], vector_table[row_base + 1]).astype(
        jnp.bfloat16
    )
    normed_all, key_all = (
        lax.all_gather(normed, "mp", axis=0, tiled=True),
        lax.all_gather(key_share, "mp", axis=0, tiled=True),
    )
    group_images = normed_all.shape[0]
    key_live = key_all > 0
    joined = product("ntd,dke->ntke", normed_all, joint)
    head_shape = (group_images, SLOTS, heads_here, HEAD_DIM)
    query_rows = (joined[:, :, 0] + shift_here[0]).astype(jnp.bfloat16).reshape(head_shape)
    key_rows = joined[:, :, 1].astype(jnp.bfloat16).reshape(head_shape)
    value_rows = (joined[:, :, 2] + shift_here[1]).astype(jnp.bfloat16).reshape(head_shape)
    scores = attention_scores(query_rows, key_rows, key_live)
    summary = jax.nn.logsumexp(scores, -1, keepdims=True)
    attention = jax.nn.softmax(scores, -1).astype(jnp.bfloat16)
    mixed_heads = (
        product("nhqk,nkhe->nqhe", attention, value_rows)
        .astype(jnp.bfloat16)
        .reshape(group_images, SLOTS, local_width)
    )
    attention_out = lax.psum_scatter(
        product("nte,ed->ntd", mixed_heads, output), "mp", scatter_dimension=0, tiled=True
    )
    middle = stream + attention_out + vector_table[row_base + 4]
    normed_two = layer_norm(middle, vector_table[row_base + 2], vector_table[row_base + 3]).astype(
        jnp.bfloat16
    )
    normed_two_all = lax.all_gather(normed_two, "mp", axis=0, tiled=True)
    hidden = product("ntd,df->ntf", normed_two_all, expand) + raise_here
    active = jax.nn.gelu(hidden).astype(jnp.bfloat16)
    result = (
        middle
        + lax.psum_scatter(
            product("ntf,fd->ntd", active, shrink), "mp", scatter_dimension=0, tiled=True
        )
        + vector_table[row_base + 5]
    )
    return (
        result,
        (
            stream,
            normed_all,
            key_live,
            query_rows,
            key_rows,
            value_rows,
            summary,
            mixed_heads,
            middle,
            normed_two_all,
            hidden,
            active,
        ),
    )


def layer_backward(grad_out, kept_values, layer_index, weights_now, vector_table):
    joint, output, expand, shrink = weights_now
    (
        stream,
        normed_all,
        key_live,
        query_rows,
        key_rows,
        value_rows,
        summary,
        mixed_heads,
        middle,
        normed_two_all,
        hidden,
        active,
    ) = kept_values
    row_base = SLOTS + 4 + 6 * layer_index
    model_width = vector_table.shape[1]
    local_width = joint.shape[2]
    local_hidden = expand.shape[1]
    group_images = normed_all.shape[0]
    model_index = lax.axis_index("mp")
    down_low = lax.all_gather(grad_out.astype(jnp.bfloat16), "mp", axis=0, tiled=True)
    shrink_grad = product("ntf,ntd->fd", active, down_low)
    active_grad = product("ntd,fd->ntf", down_low, shrink)
    unused, gelu_pull = jax.vjp(jax.nn.gelu, hidden)
    hidden_grad = gelu_pull(active_grad)[0]
    raise_grad = jnp.sum(hidden_grad, (0, 1))
    hidden_low = hidden_grad.astype(jnp.bfloat16)
    expand_grad = product("ntd,ntf->df", normed_two_all, hidden_low)
    normed_two_grad = lax.psum_scatter(
        product("ntf,df->ntd", hidden_low, expand), "mp", scatter_dimension=0, tiled=True
    )
    unused, second_pull = jax.vjp(
        layer_norm, middle, vector_table[row_base + 2], vector_table[row_base + 3]
    )
    middle_part, gain_two, shift_two = second_pull(normed_two_grad)
    middle_grad = grad_out + middle_part
    up_low = lax.all_gather(middle_grad.astype(jnp.bfloat16), "mp", axis=0, tiled=True)
    output_grad = product("nte,ntd->ed", mixed_heads, up_low)
    mixed_grad = (
        product("ntd,ed->nte", up_low, output).astype(jnp.bfloat16).reshape(query_rows.shape)
    )
    scores = attention_scores(query_rows, key_rows, key_live)
    attention = jnp.exp(scores - summary)
    value_grad = product("nhqk,nqhe->nkhe", attention.astype(jnp.bfloat16), mixed_grad)
    attention_grad = product("nqhe,nkhe->nhqk", mixed_grad, value_rows)
    score_grad = (
        attention
        * (attention_grad - jnp.sum(attention_grad * attention, -1, keepdims=True))
        * 0.125
    ).astype(jnp.bfloat16)
    query_grad = product("nhqk,nkhe->nqhe", score_grad, key_rows)
    key_grad = product("nhqk,nqhe->nkhe", score_grad, query_rows)
    flat_shape = (group_images, SLOTS, local_width)
    shift_local = jnp.stack(
        [
            jnp.sum(query_grad, (0, 1)).reshape(local_width),
            jnp.sum(value_grad, (0, 1)).reshape(local_width),
        ]
    )
    shift_grad = lax.dynamic_update_slice_in_dim(
        jnp.zeros((2, model_width), jnp.float32), shift_local, model_index * local_width, 1
    )
    raise_full = lax.dynamic_update_slice_in_dim(
        jnp.zeros((FF,), jnp.float32), raise_grad, model_index * local_hidden, 0
    )
    joined_grad = jnp.stack(
        [
            query_grad.reshape(flat_shape),
            key_grad.reshape(flat_shape),
            value_grad.reshape(flat_shape),
        ],
        2,
    ).astype(jnp.bfloat16)
    joint_grad = product("ntd,ntke->dke", normed_all, joined_grad)
    normed_grad = lax.psum_scatter(
        product("ntke,dke->ntd", joined_grad, joint), "mp", scatter_dimension=0, tiled=True
    )
    unused, first_pull = jax.vjp(
        layer_norm, stream, vector_table[row_base], vector_table[row_base + 1]
    )
    stream_part, gain_one, shift_one = first_pull(normed_grad)
    vector_rows = jnp.stack(
        [
            gain_one,
            shift_one,
            gain_two,
            shift_two,
            jnp.sum(middle_grad, (0, 1)),
            jnp.sum(grad_out, (0, 1)),
        ]
    )
    return (
        middle_grad + stream_part,
        (joint_grad, output_grad, expand_grad, shrink_grad, shift_grad, raise_full, vector_rows),
    )


def on_device(
    patches,
    keep_list,
    keep_count,
    labels,
    patch_weight,
    vector_table,
    head_table,
    joint_weight,
    shift_table,
    output_weight,
    expand_weight,
    raise_table,
    shrink_weight,
    patch_first,
    vector_first,
    head_first,
    joint_first,
    shift_first,
    output_first,
    expand_first,
    raise_first,
    shrink_first,
    patch_second,
    vector_second,
    head_second,
    joint_second,
    shift_second,
    output_second,
    expand_second,
    raise_second,
    shrink_second,
):
    share_images = patches.shape[0]
    model_width = vector_table.shape[1]
    total_images = share_images * lax.axis_size("dp") * lax.axis_size("mp")
    patch_full = lax.all_gather(patch_weight.astype(jnp.bfloat16), ("dp", "mp"), axis=0, tiled=True)

    def fetch_layers(joint_part, output_part, expand_part, shrink_part):
        return (
            lax.all_gather(joint_part.astype(jnp.bfloat16), "dp", axis=1, tiled=True),
            lax.all_gather(output_part.astype(jnp.bfloat16), "dp", axis=2, tiled=True),
            lax.all_gather(expand_part.astype(jnp.bfloat16), "dp", axis=1, tiled=True),
            lax.all_gather(shrink_part.astype(jnp.bfloat16), "dp", axis=2, tiled=True),
        )

    def layer_weights(layer_index):
        fresh = fetch_layers(
            joint_weight[layer_index : layer_index + 1],
            output_weight[layer_index : layer_index + 1],
            expand_weight[layer_index : layer_index + 1],
            shrink_weight[layer_index : layer_index + 1],
        )
        return tuple((member[0] for member in fresh))

    patch_ids = jnp.arange(PATCHES, dtype=jnp.int32)
    kept_slot = patch_ids[None, :] < keep_count[:, None]
    selector = ((keep_list[:, :, None] == patch_ids[None, None, :]) & kept_slot[:, :, None]).astype(
        jnp.float32
    )
    chosen = product("nsp,npc->nsc", selector.astype(jnp.bfloat16), patches).astype(jnp.bfloat16)
    slot_bias = kept_slot[:, :, None].astype(jnp.float32) * vector_table[SLOTS + 1]
    placed = jnp.einsum("nsp,pd->nsd", selector, vector_table[1:SLOTS], precision=highest)
    tokens = product("nsc,cd->nsd", chosen, patch_full) + slot_bias + placed
    leading = jnp.broadcast_to(
        vector_table[SLOTS] + vector_table[0], (share_images, 1, model_width)
    )
    stream = jnp.concatenate([leading, tokens], 1)
    key_share = (jnp.arange(SLOTS, dtype=jnp.int32)[None, :] <= keep_count[:, None]).astype(
        jnp.bfloat16
    )
    saved_layers = []
    for layer_index in range(LAYERS):
        stream, kept_values = layer_forward(
            stream,
            key_share,
            layer_index,
            layer_weights(layer_index),
            vector_table,
            shift_table,
            raise_table,
        )
        saved_layers.append(kept_values)
    final_out, final_pull = jax.vjp(
        layer_norm, stream[:, 0], vector_table[SLOTS + 2], vector_table[SLOTS + 3]
    )
    final_low = final_out.astype(jnp.bfloat16)
    head_low = head_table[:model_width].astype(jnp.bfloat16)
    logits = (
        jnp.dot(final_low, head_low, preferred_element_type=jnp.float32) + head_table[model_width]
    )
    target_hot = (labels[:, None] == jnp.arange(CLASSES, dtype=jnp.int32)[None, :]).astype(
        jnp.float32
    )
    loss_local = jnp.sum(jax.nn.logsumexp(logits, -1) - jnp.sum(logits * target_hot, -1))
    logit_grad = (jax.nn.softmax(logits, -1) - target_hot) / total_images
    logit_low = logit_grad.astype(jnp.bfloat16)
    head_grad = jnp.concatenate(
        [product("nd,nc->dc", final_low, logit_low), jnp.sum(logit_grad, 0)[None]], 0
    )
    final_grad = product("nc,dc->nd", logit_low, head_low)
    lead_grad, gain_final, shift_final = final_pull(final_grad)
    back_stream = jnp.zeros_like(stream).at[:, 0].set(lead_grad)
    layer_parts = [None] * LAYERS
    for layer_index in reversed(range(LAYERS)):
        back_stream, layer_parts[layer_index] = layer_backward(
            back_stream,
            saved_layers[layer_index],
            layer_index,
            layer_weights(layer_index),
            vector_table,
        )
    stacked = [jnp.stack([parts[position] for parts in layer_parts]) for position in range(7)]
    token_grad = back_stream[:, 1:]
    lead_total = jnp.sum(back_stream[:, 0], 0)
    bias_grad = jnp.sum(kept_slot[:, :, None].astype(jnp.float32) * token_grad, (0, 1))
    place_grad = jnp.einsum("nsp,nsd->pd", selector, token_grad, precision=highest)
    patch_grad = product("nsc,nsd->cd", chosen, token_grad.astype(jnp.bfloat16))
    vector_grad = jnp.concatenate(
        [
            lead_total[None],
            place_grad,
            lead_total[None],
            bias_grad[None],
            gain_final[None],
            shift_final[None],
            stacked[6].reshape(6 * LAYERS, model_width),
        ],
        0,
    )
    joint_sum, output_sum, expand_sum, shrink_sum = (
        lax.psum_scatter(stacked[0], "dp", scatter_dimension=1, tiled=True),
        lax.psum_scatter(stacked[1], "dp", scatter_dimension=2, tiled=True),
        lax.psum_scatter(stacked[2], "dp", scatter_dimension=1, tiled=True),
        lax.psum_scatter(stacked[3], "dp", scatter_dimension=2, tiled=True),
    )
    patch_sum = lax.psum_scatter(patch_grad, ("dp", "mp"), scatter_dimension=0, tiled=True)
    vector_sum, head_sum, shift_sum, raise_sum, loss_total = lax.psum(
        (vector_grad, head_grad, stacked[4], stacked[5], loss_local), ("dp", "mp")
    )
    sharded_sq = jnp.zeros((), jnp.float32)
    for member in (patch_sum, joint_sum, output_sum, expand_sum, shrink_sum):
        sharded_sq = sharded_sq + jnp.sum(member * member)
    shared_sq = jnp.zeros((), jnp.float32)
    for member in (vector_sum, head_sum, shift_sum, raise_sum):
        shared_sq = shared_sq + jnp.sum(member * member)
    lead_device = (lax.axis_index("dp") == 0) & (lax.axis_index("mp") == 0)
    total_sq = lax.psum(sharded_sq + jnp.where(lead_device, shared_sq, 0.0), ("dp", "mp"))
    gradient_norm = jnp.sqrt(total_sq)
    factor = jnp.minimum(1.0, clip_limit / (gradient_norm + norm_eps))
    weights_in = (
        patch_weight,
        vector_table,
        head_table,
        joint_weight,
        shift_table,
        output_weight,
        expand_weight,
        raise_table,
        shrink_weight,
    )
    firsts = (
        patch_first,
        vector_first,
        head_first,
        joint_first,
        shift_first,
        output_first,
        expand_first,
        raise_first,
        shrink_first,
    )
    seconds = (
        patch_second,
        vector_second,
        head_second,
        joint_second,
        shift_second,
        output_second,
        expand_second,
        raise_second,
        shrink_second,
    )
    reduced = (
        patch_sum,
        vector_sum,
        head_sum,
        joint_sum,
        shift_sum,
        output_sum,
        expand_sum,
        raise_sum,
        shrink_sum,
    )
    updated = [
        adamw(weight, moment_one, moment_two, gradient * factor, rate)
        for weight, moment_one, moment_two, gradient, rate in zip(
            weights_in, firsts, seconds, reduced, group_rates
        )
    ]
    return (
        loss_total,
        gradient_norm,
        updated[0][0],
        updated[0][1],
        updated[0][2],
        updated[1][0],
        updated[1][1],
        updated[1][2],
        updated[2][0],
        updated[2][1],
        updated[2][2],
        updated[3][0],
        updated[3][1],
        updated[3][2],
        updated[4][0],
        updated[4][1],
        updated[4][2],
        updated[5][0],
        updated[5][1],
        updated[5][2],
        updated[6][0],
        updated[6][1],
        updated[6][2],
        updated[7][0],
        updated[7][1],
        updated[7][2],
        updated[8][0],
        updated[8][1],
        updated[8][2],
    )


def solution(mesh):
    in_specs = (
        P(("dp", "mp"), None, None),
        P(("dp", "mp"), None),
        P(("dp", "mp")),
        P(("dp", "mp")),
        P(("dp", "mp"), None),
        P(),
        P(),
        P(None, "dp", None, "mp"),
        P(),
        P(None, "mp", "dp"),
        P(None, "dp", "mp"),
        P(),
        P(None, "mp", "dp"),
        P(("dp", "mp"), None),
        P(),
        P(),
        P(None, "dp", None, "mp"),
        P(),
        P(None, "mp", "dp"),
        P(None, "dp", "mp"),
        P(),
        P(None, "mp", "dp"),
        P(("dp", "mp"), None),
        P(),
        P(),
        P(None, "dp", None, "mp"),
        P(),
        P(None, "mp", "dp"),
        P(None, "dp", "mp"),
        P(),
        P(None, "mp", "dp"),
    )
    out_specs = (
        P(),
        P(),
        P(("dp", "mp"), None),
        P(("dp", "mp"), None),
        P(("dp", "mp"), None),
        P(),
        P(),
        P(),
        P(),
        P(),
        P(),
        P(None, "dp", None, "mp"),
        P(None, "dp", None, "mp"),
        P(None, "dp", None, "mp"),
        P(),
        P(),
        P(),
        P(None, "mp", "dp"),
        P(None, "mp", "dp"),
        P(None, "mp", "dp"),
        P(None, "dp", "mp"),
        P(None, "dp", "mp"),
        P(None, "dp", "mp"),
        P(),
        P(),
        P(),
        P(None, "mp", "dp"),
        P(None, "mp", "dp"),
        P(None, "mp", "dp"),
    )
    return jax.shard_map(
        on_device, mesh=mesh, in_specs=in_specs, out_specs=out_specs, check_vma=False
    )
```

profile of v0, /device:TPU:0, one launch (start us, length us, event | category | flops | bytes accessed | tf_op | source)
XLA Modules:
  0.0 2217.2 jit_solution(17241962619185036164)
XLA Ops:
  15.3 68.5 %all-gather.17.cloned.1.call-done = bf16[3072,1024]{1,0:T(8,128)(2,1)} async-done(((bf16[96,1024]{1,0:T(8,128)(2,1)}), bf16[3072,1024]{1,0:T(8,128)(2,1)}) %all-gather.17.cloned.1.call-update) | async-done | bytes 6291472 | tf_op jit(solution)/shard_map/all_gather | solution.py:257
  101.1 31.3 %all_gather.67 = bf16[1,256,1024]{2,1,0:T(8,128)(2,1)} all-gather(bf16[1,256,128]{2,1,0:T(8,128)(2,1)S(1)} %get-tuple-element.287), channel_id=1, replica_groups=mesh['dp'=8,'mp'=4] {'dp'}, dimensions={2}, use_global_device_ids=true | all-gather | bytes 589824 | tf_op jit(solution)/shard_map/all_gather | solution.py:262
  134.9 27.2 %all-gather.19.cloned.1.call-done = bf16[24,50,1024]{2,1,0:T(8,128)(2,1)} async-done(((bf16[6,50,1024]{2,1,0:T(8,128)(2,1)}), bf16[24,50,1024]{2,1,0:T(8,128)(2,1)}) %all-gather.19.cloned.1.call-update) | async-done | bytes 2457616 | tf_op jit(solution)/shard_map/all_gather | solution.py:68
  199.9 50.7 %reduce-scatter.14.cloned.1.call-done = f32[6,50,1024]{2,1,0:T(8,128)} async-done(((f32[24,50,1024]{2,1,0:T(8,128)}), f32[6,50,1024]{2,1,0:T(8,128)}) %reduce-scatter.14.cloned.1.call-update) | async-done | bytes 1228816 | tf_op jit(solution)/shard_map/reduce_scatter | solution.py:86
  257.1 45.5 %all-gather.25.cloned.1.call-done = bf16[1,1024,1024]{2,1,0:T(8,128)(2,1)} async-done(((bf16[1,128,1024]{2,1,0:T(8,128)(2,1)}), bf16[1,1024,1024]{2,1,0:T(8,128)(2,1)}) %all-gather.25.cloned.1.call-update) | async-done | bytes 2097168 | tf_op jit(solution)/shard_map/all_gather | solution.py:263
  337.4 46.1 %all-gather.27.cloned.1.call-done = bf16[1,1024,1024]{2,1,0:T(8,128)(2,1)} async-done(((bf16[1,1024,128]{2,1,0:T(8,128)(2,1)}), bf16[1,1024,1024]{2,1,0:T(8,128)(2,1)}) %all-gather.27.cloned.1.call-update) | async-done | bytes 2097168 | tf_op jit(solution)/shard_map/all_gather | solution.py:264
  393.9 50.7 %reduce-scatter.16.cloned.1.call-done = f32[6,50,1024]{2,1,0:T(8,128)} async-done(((f32[24,50,1024]{2,1,0:T(8,128)}), f32[6,50,1024]{2,1,0:T(8,128)}) %reduce-scatter.16.cloned.1.call-update) | async-done | bytes 1228816 | tf_op jit(solution)/shard_map/reduce_scatter | solution.py:98
  451.2 31.2 %all_gather.73 = bf16[1,256,1024]{2,1,0:T(8,128)(2,1)} all-gather(bf16[1,256,128]{2,1,0:T(8,128)(2,1)S(1)} %copy-done.75), channel_id=1, replica_groups=mesh['dp'=8,'mp'=4] {'dp'}, dimensions={2}, use_global_device_ids=true | all-gather | bytes 589824 | tf_op jit(solution)/shard_map/all_gather | solution.py:262
  559.4 52.5 %reduce-scatter.18.cloned.1.call-done = f32[6,50,1024]{2,1,0:T(8,128)} async-done(((f32[24,50,1024]{2,1,0:T(8,128)}), f32[6,50,1024]{2,1,0:T(8,128)}) %reduce-scatter.18.cloned.1.call-update) | async-done | bytes 1228816 | tf_op jit(solution)/shard_map/reduce_scatter | solution.py:86
  621.7 42.3 %all-gather.35.cloned.1.call-done = bf16[1,1024,1024]{2,1,0:T(8,128)(2,1)} async-done(((bf16[1,128,1024]{2,1,0:T(8,128)(2,1)}), bf16[1,1024,1024]{2,1,0:T(8,128)(2,1)}) %all-gather.35.cloned.1.call-update) | async-done | bytes 2097168 | tf_op jit(solution)/shard_map/all_gather | solution.py:263
  664.0 27.0 %all-gather.33.cloned.1.call-done = bf16[24,50,1024]{2,1,0:T(8,128)(2,1)} async-done(((bf16[6,50,1024]{2,1,0:T(8,128)(2,1)}), bf16[24,50,1024]{2,1,0:T(8,128)(2,1)}) %all-gather.33.cloned.1.call-update) | async-done | bytes 2457616 | tf_op jit(solution)/shard_map/all_gather | solution.py:93
  698.9 45.8 %all-gather.37.cloned.1.call-done = bf16[1,1024,1024]{2,1,0:T(8,128)(2,1)} async-done(((bf16[1,1024,128]{2,1,0:T(8,128)(2,1)}), bf16[1,1024,1024]{2,1,0:T(8,128)(2,1)}) %all-gather.37.cloned.1.call-update) | async-done | bytes 2097168 | tf_op jit(solution)/shard_map/all_gather | solution.py:264
  754.4 51.4 %reduce-scatter.20.cloned.1.call-done = f32[6,50,1024]{2,1,0:T(8,128)} async-done(((f32[24,50,1024]{2,1,0:T(8,128)}), f32[6,50,1024]{2,1,0:T(8,128)}) %reduce-scatter.20.cloned.1.call-update) | async-done | bytes 1228816 | tf_op jit(solution)/shard_map/reduce_scatter | solution.py:98
  858.7 53.2 %reduce-scatter.22.cloned.1.call-done = f32[6,50,1024]{2,1,0:T(8,128)} async-done(((f32[24,50,1024]{2,1,0:T(8,128)}), f32[6,50,1024]{2,1,0:T(8,128)}) %reduce-scatter.22.cloned.1.call-update) | async-done | bytes 1228816 | tf_op jit(solution)/shard_map/reduce_scatter | solution.py:152
  1010.9 53.2 %reduce-scatter.24.cloned.1.call-done = f32[6,50,1024]{2,1,0:T(8,128)} async-done(((f32[24,50,1024]{2,1,0:T(8,128)}), f32[6,50,1024]{2,1,0:T(8,128)}) %reduce-scatter.24.cloned.1.call-update) | async-done | bytes 1228816 | tf_op jit(solution)/shard_map/reduce_scatter | solution.py:198
  1122.3 53.2 %reduce-scatter.26.cloned.1.call-done = f32[6,50,1024]{2,1,0:T(8,128)} async-done(((f32[24,50,1024]{2,1,0:T(8,128)}), f32[6,50,1024]{2,1,0:T(8,128)}) %reduce-scatter.26.cloned.1.call-update) | async-done | bytes 1228816 | tf_op jit(solution)/shard_map/reduce_scatter | solution.py:152
  1368.8 39.9 %all-reduce.2 = (f32[2,2,1024]{2,1,0:T(2,128)S(1)}, f32[2,4096]{1,0:T(2,128)S(1)}) all-reduce(f32[2,2,1024]{2,1,0:T(2,128)S(1)} %pad_maximum_fusion.8, f32[2,4096]{1,0:T(2,128)S(1)} %pad_maximum_fusion.7), channel_id=1, replica_groups=mesh['dp'=8,'mp'=4] {'dp','mp'}, use_global_device_ids=true, to_apply=%region_77.78 | all-reduce | flops 12288 | bytes 98304 | tf_op jit(solution)/shard_map/psum | solution.py:358
  1410.0 50.1 %reduce-scatter.38.cloned.1.call-done = f32[2,1024,128]{2,1,0:T(8,128)} async-done(((f32[2,1024,1024]{2,1,0:T(8,128)}), f32[2,1024,128]{2,1,0:T(8,128)}) %reduce-scatter.38.cloned.1.call-update) | async-done | bytes 1048592 | tf_op jit(solution)/shard_map/reduce_scatter | solution.py:355
  1462.2 150.0 %reduce-scatter.36.cloned.1.call-done = f32[2,128,1024]{2,1,0:T(8,128)} async-done(((f32[2,1024,1024]{2,1,0:T(8,128)}), f32[2,128,1024]{2,1,0:T(8,128)}) %reduce-scatter.36.cloned.1.call-update) | async-done | bytes 1048592 | tf_op jit(solution)/shard_map/reduce_scatter | solution.py:354
  1614.3 69.0 %reduce-scatter.34.cloned.1.call-done = f32[2,256,128]{2,1,0:T(8,128)} async-done(((f32[2,256,1024]{2,1,0:T(8,128)}), f32[2,256,128]{2,1,0:T(8,128)}) %reduce-scatter.34.cloned.1.call-update) | async-done | bytes 262160 | tf_op jit(solution)/shard_map/reduce_scatter | solution.py:353
  1685.0 149.0 %all-reduce.6.cloned.1.call-done = (f32[66,1024]{1,0:T(8,128)}, f32[1025,1000]{0,1:T(8,128)}) async-done(((f32[66,1024]{1,0:T(8,128)}, f32[1025,1000]{0,1:T(8,128)}), (f32[66,1024]{1,0:T(8,128)}, f32[1025,1000]{0,1:T(8,128)})) %all-reduce.6.cloned.1.call-update) | async-done | bytes 4370352 | tf_op jit(solution)/shard_map/psum | solution.py:358
  1842.3 112.7 %reduce-scatter.32.cloned.1.call-done = f32[2,128,3,256]{3,1,2,0:T(8,128)} async-done(((f32[2,1024,3,256]{3,1,2,0:T(8,128)}), f32[2,128,3,256]{3,1,2,0:T(8,128)}) %reduce-scatter.32.cloned.1.call-update) | async-done | bytes 786448 | tf_op jit(solution)/shard_map/reduce_scatter | solution.py:352
  1957.0 158.7 %reduce-scatter.30.cloned.1.call-done = f32[96,1024]{1,0:T(8,128)} async-done(((f32[3072,1024]{1,0:T(8,128)}), f32[96,1024]{1,0:T(8,128)}) %reduce-scatter.30.cloned.1.call-update) | async-done | bytes 393232 | tf_op jit(solution)/shard_map/reduce_scatter | solution.py:357
  2126.1 40.2 %all-reduce.1 = (f32[]{:T(128)}, f32[]{:T(128)}) all-reduce(f32[]{:T(128)} %subtract_reduce_fusion, f32[]{:T(128)S(6)} %add.589), channel_id=1, replica_groups=mesh['dp'=8,'mp'=4] {'dp','mp'}, use_global_device_ids=true, to_apply=%region_22.23 | all-reduce | flops 2 | bytes 16 | tf_op jit(solution)/shard_map/psum | solution.py:358
  (651 shorter events, 693.6 us)
Async XLA Ops:
  9.1 125.7 %all-gather.21.cloned.1.call-start = ((), (), s32[]{:S(2)}) async-start(), calls=%async_computation.15 | async-start | bytes 1769472 | tf_op jit(solution)/shard_map/all_gather | solution.py:261
  11.2 150.9 %all-gather.19.cloned.1.call-start = ((), (), s32[]{:S(2)}) async-start(), calls=%async_computation.14 | async-start | bytes 3440640 | tf_op jit(solution)/shard_map/all_gather | solution.py:68
  94.3 156.2 %reduce-scatter.14.cloned.1.call-start = ((), (), s32[]{:S(2)}) async-start(), calls=%async_computation.16 | async-start | bytes 6881280 | tf_op jit(solution)/shard_map/reduce_scatter | solution.py:86
  197.3 105.4 %all-gather.25.cloned.1.call-start = ((), (), s32[]{:S(2)}) async-start(), calls=%async_computation.18 | async-start | bytes 2359296 | tf_op jit(solution)/shard_map/all_gather | solution.py:263
  199.4 130.1 %all-gather.23.cloned.1.call-start = ((), (), s32[]{:S(2)}) async-start(), calls=%async_computation.17 | async-start | bytes 3440640 | tf_op jit(solution)/shard_map/all_gather | solution.py:93
  255.4 128.0 %all-gather.27.cloned.1.call-start = ((), (), s32[]{:S(2)}) async-start(), calls=%async_computation.19 | async-start | bytes 2359296 | tf_op jit(solution)/shard_map/all_gather | solution.py:264
  256.4 188.1 %reduce-scatter.16.cloned.1.call-start = ((), (), s32[]{:S(2)}) async-start(), calls=%async_computation.20 | async-start | bytes 6881280 | tf_op jit(solution)/shard_map/reduce_scatter | solution.py:98
  393.1 101.6 %all-gather.31.cloned.1.call-start = ((), (), s32[]{:S(2)}) async-start(), calls=%async_computation.22 | async-start | bytes 1769472 | tf_op jit(solution)/shard_map/all_gather | solution.py:261
  393.8 127.3 %all-gather.29.cloned.1.call-start = ((), (), s32[]{:S(2)}) async-start(), calls=%async_computation.21 | async-start | bytes 3440640 | tf_op jit(solution)/shard_map/all_gather | solution.py:68
  449.9 162.0 %reduce-scatter.18.cloned.1.call-start = ((), (), s32[]{:S(2)}) async-start(), calls=%async_computation.23 | async-start | bytes 6881280 | tf_op jit(solution)/shard_map/reduce_scatter | solution.py:86
  558.6 105.4 %all-gather.35.cloned.1.call-start = ((), (), s32[]{:S(2)}) async-start(), calls=%async_computation.25 | async-start | bytes 2359296 | tf_op jit(solution)/shard_map/all_gather | solution.py:263
  559.2 131.9 %all-gather.33.cloned.1.call-start = ((), (), s32[]{:S(2)}) async-start(), calls=%async_computation.24 | async-start | bytes 3440640 | tf_op jit(solution)/shard_map/all_gather | solution.py:93
  620.4 124.4 %all-gather.37.cloned.1.call-start = ((), (), s32[]{:S(2)}) async-start(), calls=%async_computation.26 | async-start | bytes 2359296 | tf_op jit(solution)/shard_map/all_gather | solution.py:264
  620.9 184.9 %reduce-scatter.20.cloned.1.call-start = ((), (), s32[]{:S(2)}) async-start(), calls=%async_computation.27 | async-start | bytes 6881280 | tf_op jit(solution)/shard_map/reduce_scatter | solution.py:98
  815.3 96.6 %reduce-scatter.22.cloned.1.call-start = ((), (), s32[]{:S(2)}) async-start(), calls=%async_computation.29 | async-start | bytes 6881280 | tf_op jit(solution)/shard_map/reduce_scatter | solution.py:152
  925.6 138.6 %reduce-scatter.24.cloned.1.call-start = ((), (), s32[]{:S(2)}) async-start(), calls=%async_computation.31 | async-start | bytes 6881280 | tf_op jit(solution)/shard_map/reduce_scatter | solution.py:198
  1077.1 98.4 %reduce-scatter.26.cloned.1.call-start = ((), (), s32[]{:S(2)}) async-start(), calls=%async_computation.33 | async-start | bytes 6881280 | tf_op jit(solution)/shard_map/reduce_scatter | solution.py:152
  1186.2 120.3 %reduce-scatter.28.cloned.1.call-start = ((), (), s32[]{:S(2)}) async-start(), calls=%async_computation.35 | async-start | bytes 6881280 | tf_op jit(solution)/shard_map/reduce_scatter | solution.py:198
  1253.2 206.9 %reduce-scatter.38.cloned.1.call-start = ((), (), s32[]{:S(2)}) async-start(), calls=%async_computation.40 | async-start | bytes 9437184 | tf_op jit(solution)/shard_map/reduce_scatter | solution.py:355
  1271.2 341.0 %reduce-scatter.36.cloned.1.call-start = ((), (), s32[]{:S(2)}) async-start(), calls=%async_computation.39 | async-start | bytes 9437184 | tf_op jit(solution)/shard_map/reduce_scatter | solution.py:354
  1286.6 396.7 %reduce-scatter.34.cloned.1.call-start = ((), (), s32[]{:S(2)}) async-start(), calls=%async_computation.38 | async-start | bytes 2359296 | tf_op jit(solution)/shard_map/reduce_scatter | solution.py:353
  1295.0 539.0 %all-reduce.6.cloned.1.call-start = ((), (), s32[]{:S(2)}) async-start(), calls=%async_computation.41 | async-start | bytes 9805824 | tf_op jit(solution)/shard_map/psum | solution.py:358
  1322.0 633.0 %reduce-scatter.32.cloned.1.call-start = ((), (), s32[]{:S(2)}) async-start(), calls=%async_computation.37 | async-start | bytes 7077888 | tf_op jit(solution)/shard_map/reduce_scatter | solution.py:352
  1334.5 781.1 %reduce-scatter.30.cloned.1.call-start = ((), (), s32[]{:S(2)}) async-start(), calls=%async_computation.36 | async-start | bytes 12976128 | tf_op jit(solution)/shard_map/reduce_scatter | solution.py:357
  (159 other events, 2483.7 us)
Sparse Core Ops, SparseCore 0:
  11.5 72.1 all-gather.16
  86.5 48.3 all-gather.20
  197.4 53.1 reduce-scatter.13
  253.3 49.2 all-gather.24
  332.3 51.0 all-gather.26
  393.2 51.3 reduce-scatter.15
  447.3 47.3 all-gather.30
  558.7 53.1 reduce-scatter.17
  614.7 49.2 all-gather.34
  693.7 51.0 all-gather.36
  754.4 51.3 reduce-scatter.19
  858.8 53.1 reduce-scatter.21
  925.7 26.2 all-gather.40
  1011.0 53.1 reduce-scatter.23
  1077.2 26.2 all-gather.42
  1122.3 53.1 reduce-scatter.25
  1186.4 26.2 all-gather.44
  1253.3 53.1 reduce-scatter.27
  1310.0 150.0 reduce-scatter.37
  1464.2 148.0 reduce-scatter.35
  1616.2 67.1 reduce-scatter.33
  1689.5 144.4 all-reduce.5
  1837.6 117.3 reduce-scatter.31
  1961.1 154.5 reduce-scatter.29
  (5 shorter events, 125.0 us)
where the time goes:
time: 2230 us; the launch traced here: 2220 us
  waiting for transfers between devices  1540 us (69%)
  matrix products  209 us (9%)
  local copies, waits for them, and re-layouts  152 us (7%)
  blocking collectives  148 us (7%)
  other arithmetic  145 us (7%)
  between operations  24.2 us (1%)
    dot_general x41, matrix products, product(): return jnp.einsum(form, left, right, preferred_element_type=jnp.float32)  204 us
    reduce_scatter x1, waiting for transfers between devices, on_device(): lax.psum_scatter(patch_grad, ('dp', 'mp'), scatter_dimension=0, tiled=True)  159 us
    reduce_scatter x1, waiting for transfers between devices, on_device(): lax.psum_scatter(stacked[2], 'dp', scatter_dimension=1, tiled=True)  150 us
    psum x1, waiting for transfers between devices, on_device(): lax.psum((vector_grad, head_grad, stacked[4], stacked[5], loss_local), ('...  149 us
    reduce_scatter x1, waiting for transfers between devices, on_device(): lax.psum_scatter(stacked[0], 'dp', scatter_dimension=1, tiled=True)  113 us
    reduce_scatter x2, waiting for transfers between devices, layer_backward(): lax.psum_scatter(product('ntf,df->ntd', hidden_low, expand), 'mp', scatte...  106 us
    reduce_scatter x2, waiting for transfers between devices, layer_forward(): lax.psum_scatter(product('nte,ed->ntd', mixed_heads, output), 'mp', scatt...  103 us
    reduce_scatter x2, waiting for transfers between devices, layer_forward(): lax.psum_scatter(product('ntf,fd->ntd', active, shrink), 'mp', scatter_di...  102 us
  transfers between devices with their start and end apart: 29, of which 29 were waited for; matrix products, arithmetic and copies ran while one was open for 8% of the time, Pallas kernels for 0%

commit v1 on v0

--- a/solution.py
+++ b/solution.py
@@ -44,6 +44,88 @@
 def attention_scores(query_rows, key_rows, key_live):
     scores = product("nqhe,nkhe->nhqk", query_rows, key_rows) * 0.125
     return jnp.where(key_live[:, None, None, :], scores, -1e30)
+
+AXES = ("dp", "mp")
+
+
+def swap(values, mask):
+    count = lax.axis_size("dp") * lax.axis_size("mp")
+    return lax.ppermute(values, AXES, [(n, n ^ mask) for n in range(count)])
+
+
+def device_index():
+    return lax.axis_index("dp") * lax.axis_size("mp") + lax.axis_index("mp")
+
+
+def bit_masks():
+    model, data = lax.axis_size("mp"), lax.axis_size("dp")
+    wide = 1 << ((data.bit_length() - 1) // 2)
+    z_masks = [m for m in (model * wide << b for b in range(16)) if m < model * data]
+    y_masks = [m for m in (model << b for b in range(16)) if m < model * wide]
+    x_masks = [m for m in (2 << b for b in range(16)) if m < model]
+    return (z_masks, y_masks, x_masks, [1])
+
+
+def offsets(masks):
+    table = [0]
+    for mask in masks:
+        table = table + [entry ^ mask for entry in table]
+    return table
+
+
+def gather_blocks(values, masks):
+    blocks = values[None]
+    for mask in masks:
+        blocks = jnp.concatenate([blocks, swap(blocks, mask)], 0)
+    return blocks
+
+
+def from_position(masks, shift):
+    table = offsets(masks)
+    inverse = [0] * len(table)
+    for place, entry in enumerate(table):
+        inverse[entry >> shift] = place
+    here = (device_index() & sum(masks)) >> shift
+    return jnp.take(jnp.array(inverse, jnp.int32), jnp.arange(len(table)) ^ here)
+
+
+def to_position(masks, shift):
+    here = (device_index() & sum(masks)) >> shift
+    return jnp.array([entry >> shift for entry in offsets(masks)], jnp.int32) ^ here
+
+
+def gather_ordered(values, masks, shift):
+    return jnp.take(gather_blocks(values, masks), from_position(masks, shift), axis=0)
+
+
+def reduce_blocks(blocks, masks):
+    for mask in reversed(masks):
+        half = blocks.shape[0] // 2
+        blocks = blocks[:half] + swap(blocks[half:].astype(jnp.bfloat16), mask).astype(jnp.float32)
+    return blocks[0]
+
+
+def reduce_ordered(blocks, masks, shift):
+    return reduce_blocks(jnp.take(blocks, to_position(masks, shift), axis=0), masks)
+
+
+def sum_all(values):
+    for masks in reversed(bit_masks()):
+        for mask in masks:
+            values = jax.tree.map(lambda v: v + swap(v, mask), values)
+    return values
+
+
+def group_gather(values):
+    z_masks, y_masks, x_masks, c_masks = bit_masks()
+    blocks = gather_blocks(values, x_masks + c_masks)
+    return blocks.reshape((-1,) + values.shape[1:])
+
+
+def group_reduce(values):
+    z_masks, y_masks, x_masks, c_masks = bit_masks()
+    model = lax.axis_size("mp")
+    return reduce_blocks(values.reshape((model, -1) + values.shape[1:]), x_masks + c_masks)
 
 
 def layer_forward(
@@ -65,8 +147,8 @@
         jnp.bfloat16
     )
     normed_all, key_all = (
-        lax.all_gather(normed, "mp", axis=0, tiled=True),
-        lax.all_gather(key_share, "mp", axis=0, tiled=True),
+        group_gather(normed),
+        group_gather(key_share),
     )
     group_images = normed_all.shape[0]
     key_live = key_all > 0
@@ -83,21 +165,17 @@
         .astype(jnp.bfloat16)
         .reshape(group_images, SLOTS, local_width)
     )
-    attention_out = lax.psum_scatter(
-        product("nte,ed->ntd", mixed_heads, output), "mp", scatter_dimension=0, tiled=True
-    )
+    attention_out = group_reduce(product("nte,ed->ntd", mixed_heads, output))
     middle = stream + attention_out + vector_table[row_base + 4]
     normed_two = layer_norm(middle, vector_table[row_base + 2], vector_table[row_base + 3]).astype(
         jnp.bfloat16
     )
-    normed_two_all = lax.all_gather(normed_two, "mp", axis=0, tiled=True)
+    normed_two_all = group_gather(normed_two)
     hidden = product("ntd,df->ntf", normed_two_all, expand) + raise_here
     active = jax.nn.gelu(hidden).astype(jnp.bfloat16)
     result = (
         middle
-        + lax.psum_scatter(
-            product("ntf,fd->ntd", active, shrink), "mp", scatter_dimension=0, tiled=True
-        )
+        + group_reduce(product("ntf,fd->ntd", active, shrink))
         + vector_table[row_base + 5]
     )
     return (
@@ -141,7 +219,7 @@
     local_hidden = expand.shape[1]
     group_images = normed_all.shape[0]
     model_index = lax.axis_index("mp")
-    down_low = lax.all_gather(grad_out.astype(jnp.bfloat16), "mp", axis=0, tiled=True)
+    down_low = group_gather(grad_out.astype(jnp.bfloat16))
     shrink_grad = product("ntf,ntd->fd", active, down_low)
     active_grad = product("ntd,fd->ntf", down_low, shrink)
     unused, gelu_pull = jax.vjp(jax.nn.gelu, hidden)
@@ -149,15 +227,13 @@
     raise_grad = jnp.sum(hidden_grad, (0, 1))
     hidden_low = hidden_grad.astype(jnp.bfloat16)
     expand_grad = product("ntd,ntf->df", normed_two_all, hidden_low)
-    normed_two_grad = lax.psum_scatter(
-        product("ntf,df->ntd", hidden_low, expand), "mp", scatter_dimension=0, tiled=True
-    )
+    normed_two_grad = group_reduce(product("ntf,df->ntd", hidden_low, expand))
     unused, second_pull = jax.vjp(
         layer_norm, middle, vector_table[row_base + 2], vector_table[row_base + 3]
     )
     middle_part, gain_two, shift_two = second_pull(normed_two_grad)
     middle_grad = grad_out + middle_part
-    up_low = lax.all_gather(middle_grad.astype(jnp.bfloat16), "mp", axis=0, tiled=True)
+    up_low = group_gather(middle_grad.astype(jnp.bfloat16))
     output_grad = product("nte,ntd->ed", mixed_heads, up_low)
     mixed_grad = (
         product("ntd,ed->nte", up_low, output).astype(jnp.bfloat16).reshape(query_rows.shape)
@@ -195,9 +271,7 @@
         2,
     ).astype(jnp.bfloat16)
     joint_grad = product("ntd,ntke->dke", normed_all, joined_grad)
-    normed_grad = lax.psum_scatter(
-        product("ntke,dke->ntd", joined_grad, joint), "mp", scatter_dimension=0, tiled=True
-    )
+    normed_grad = group_reduce(product("ntke,dke->ntd", joined_grad, joint))
     unused, first_pull = jax.vjp(
         layer_norm, stream, vector_table[row_base], vector_table[row_base + 1]
     )
@@ -254,24 +328,25 @@
     share_images = patches.shape[0]
     model_width = vector_table.shape[1]
     total_images = share_images * lax.axis_size("dp") * lax.axis_size("mp")
-    patch_full = lax.all_gather(patch_weight.astype(jnp.bfloat16), ("dp", "mp"), axis=0, tiled=True)
-
-    def fetch_layers(joint_part, output_part, expand_part, shrink_part):
+    z_masks, y_masks, x_masks, c_masks = bit_masks()
+    dp_masks = z_masks + y_masks
+    all_masks = dp_masks + x_masks + c_masks
+    dp_shift = lax.axis_size("mp").bit_length() - 1
+    patch_full = gather_ordered(patch_weight.astype(jnp.bfloat16), all_masks, 0).reshape(-1, model_width)
+
+    def layer_weights(layer_index):
+        def over_rows(shard):
+            blocks = gather_ordered(shard.astype(jnp.bfloat16), dp_masks, dp_shift)
+            return blocks.reshape((-1,) + shard.shape[1:])
+
         return (
-            lax.all_gather(joint_part.astype(jnp.bfloat16), "dp", axis=1, tiled=True),
-            lax.all_gather(output_part.astype(jnp.bfloat16), "dp", axis=2, tiled=True),
-            lax.all_gather(expand_part.astype(jnp.bfloat16), "dp", axis=1, tiled=True),
-            lax.all_gather(shrink_part.astype(jnp.bfloat16), "dp", axis=2, tiled=True),
+            over_rows(joint_weight[layer_index]),
+            over_rows(output_weight[layer_index].T).T,
+            over_rows(expand_weight[layer_index]),
+            over_rows(shrink_weight[layer_index].T).T,
         )
 
-    def layer_weights(layer_index):
-        fresh = fetch_layers(
-            joint_weight[layer_index : layer_index + 1],
-            output_weight[layer_index : layer_index + 1],
-            expand_weight[layer_index : layer_index + 1],
-            shrink_weight[layer_index : layer_index + 1],
-        )
-        return tuple((member[0] for member in fresh))
+    weights_of = [layer_weights(layer_index) for layer_index in range(LAYERS)]
 
     patch_ids = jnp.arange(PATCHES, dtype=jnp.int32)
     kept_slot = patch_ids[None, :] < keep_count[:, None]
@@ -295,7 +370,7 @@
             stream,
             key_share,
             layer_index,
-            layer_weights(layer_index),
+            weights_of[layer_index],
             vector_table,
             shift_table,
             raise_table,
@@ -315,8 +390,14 @@
     loss_local = jnp.sum(jax.nn.logsumexp(logits, -1) - jnp.sum(logits * target_hot, -1))
     logit_grad = (jax.nn.softmax(logits, -1) - target_hot) / total_images
     logit_low = logit_grad.astype(jnp.bfloat16)
-    head_grad = jnp.concatenate(
-        [product("nd,nc->dc", final_low, logit_low), jnp.sum(logit_grad, 0)[None]], 0
+    final_every = gather_ordered(final_low, all_masks, 0).reshape(-1, model_width)
+    logit_every = gather_ordered(logit_grad, all_masks, 0).reshape(-1, CLASSES)
+    head_sum = jnp.concatenate(
+        [
+            product("nd,nc->dc", final_every, logit_every.astype(jnp.bfloat16)),
+            jnp.sum(logit_every, 0)[None],
+        ],
+        0,
     )
     final_grad = product("nc,dc->nd", logit_low, head_low)
     lead_grad, gain_final, shift_final = final_pull(final_grad)
@@ -327,10 +408,12 @@
             back_stream,
             saved_layers[layer_index],
             layer_index,
-            layer_weights(layer_index),
+            weights_of[layer_index],
             vector_table,
         )
-    stacked = [jnp.stack([parts[position] for parts in layer_parts]) for position in range(7)]
+    stacked = {
+        position: jnp.stack([parts[position] for parts in layer_parts]) for position in (4, 5, 6)
+    }
     token_grad = back_stream[:, 1:]
     lead_total = jnp.sum(back_stream[:, 0], 0)
     bias_grad = jnp.sum(kept_slot[:, :, None].astype(jnp.float32) * token_grad, (0, 1))
@@ -348,15 +431,18 @@
         ],
         0,
     )
-    joint_sum, output_sum, expand_sum, shrink_sum = (
-        lax.psum_scatter(stacked[0], "dp", scatter_dimension=1, tiled=True),
-        lax.psum_scatter(stacked[1], "dp", scatter_dimension=2, tiled=True),
-        lax.psum_scatter(stacked[2], "dp", scatter_dimension=1, tiled=True),
-        lax.psum_scatter(stacked[3], "dp", scatter_dimension=2, tiled=True),
-    )
-    patch_sum = lax.psum_scatter(patch_grad, ("dp", "mp"), scatter_dimension=0, tiled=True)
-    vector_sum, head_sum, shift_sum, raise_sum, loss_total = lax.psum(
-        (vector_grad, head_grad, stacked[4], stacked[5], loss_local), ("dp", "mp")
+    def scatter_rows(grads):
+        blocks = grads.reshape((lax.axis_size("dp"), -1) + grads.shape[1:])
+        return reduce_ordered(blocks, dp_masks, dp_shift)
+
+    joint_sum = jnp.stack([scatter_rows(parts[0]) for parts in layer_parts])
+    output_sum = jnp.stack([scatter_rows(parts[1].T).T for parts in layer_parts])
+    expand_sum = jnp.stack([scatter_rows(parts[2]) for parts in layer_parts])
+    shrink_sum = jnp.stack([scatter_rows(parts[3].T).T for parts in layer_parts])
+    patch_blocks = patch_grad.reshape(lax.axis_size("dp") * lax.axis_size("mp"), -1, model_width)
+    patch_sum = reduce_ordered(patch_blocks, all_masks, 0)
+    vector_sum, shift_sum, raise_sum, loss_total = sum_all(
+        (vector_grad, stacked[4], stacked[5], loss_local)
     )
     sharded_sq = jnp.zeros((), jnp.float32)
     for member in (patch_sum, joint_sum, output_sum, expand_sum, shrink_sum):
@@ -365,7 +451,7 @@
     for member in (vector_sum, head_sum, shift_sum, raise_sum):
         shared_sq = shared_sq + jnp.sum(member * member)
     lead_device = (lax.axis_index("dp") == 0) & (lax.axis_index("mp") == 0)
-    total_sq = lax.psum(sharded_sq + jnp.where(lead_device, shared_sq, 0.0), ("dp", "mp"))
+    total_sq = sum_all(sharded_sq + jnp.where(lead_device, shared_sq, 0.0))
     gradient_norm = jnp.sqrt(total_sq)
     factor = jnp.minimum(1.0, clip_limit / (gradient_norm + norm_eps))
     weights_in = (

time: 2230 us -> 1530 us (0.69)
  waiting for transfers between devices: 1540 us -> 512 us
  local copies, waits for them, and re-layouts: 152 us -> 403 us
  other arithmetic: 145 us -> 297 us
  blocking collectives: 148 us -> 0 us
  starting transfers between devices: 3.19 us -> 130 us
  matrix products: 209 us -> 157 us
    reduce_scatter x13 -> x0, waiting for transfers between devices: 910 us -> none  [the longest x1 159 us: on_device(): lax.psum_scatter(patch_grad, ('dp', 'mp'), scatter_dimension=0, tiled=True)]
    ppermute x0 -> x127, waiting for transfers between devices: none -> 512 us  [swap(): return lax.ppermute(values, AXES, [(n, n ^ mask) for n in range(count)])]
    all_gather x15 -> x0, waiting for transfers between devices: 475 us -> none  [the longest x2 91.9 us: fetch_layers(): lax.all_gather(shrink_part.astype(jnp.bfloat16), 'dp', axis=2, tiled=True)]
    psum x1 -> x0, waiting for transfers between devices: 149 us -> none  [on_device(): lax.psum((vector_grad, head_grad, stacked[4], stacked[5], loss_local), ('...]
    ppermute x0 -> x127, starting transfers between devices: none -> 130 us  [swap(): return lax.ppermute(values, AXES, [(n, n ^ mask) for n in range(count)])]
    psum x2 -> x0, blocking collectives: 80.1 us -> none  [on_device(): lax.psum((vector_grad, head_grad, stacked[4], stacked[5], loss_local), ('...]
    concatenate x1 -> x50, other arithmetic: 2.52 us -> 80 us  [gather_blocks(): blocks = jnp.concatenate([blocks, swap(blocks, mask)], 0)]
    gather x0 -> x22, local copies, waits for them, and re-layouts: none -> 71.4 us  [the longest x9 41.7 us: reduce_ordered(): jnp.take(blocks, to_position(masks, shift), axis=0)]
  transfers between devices with their start and end apart: 29 -> 127, of which waited for: 29 -> 64; matrix products, arithmetic and copies ran while one was open for 8% -> 38% of each run, Pallas kernels for 0% -> 0%
where the time goes in v1:
time: 1530 us; the launch traced here: 1520 us
  waiting for transfers between devices  512 us (33%)
  local copies, waits for them, and re-layouts  403 us (26%)
  other arithmetic  297 us (19%)
  matrix products  157 us (10%)
  starting transfers between devices  130 us (8%)
  between operations  21 us (1%)
    ppermute x127, waiting for transfers between devices, swap(): return lax.ppermute(values, AXES, [(n, n ^ mask) for n in range(count)])  512 us
    dot_general x41, matrix products, product(): return jnp.einsum(form, left, right, preferred_element_type=jnp.float32)  153 us
    ppermute x127, starting transfers between devices, swap(): return lax.ppermute(values, AXES, [(n, n ^ mask) for n in range(count)])  130 us
    unnamed x631, local copies, waits for them, and re-layouts  100 us
    concatenate x50, other arithmetic, gather_blocks(): blocks = jnp.concatenate([blocks, swap(blocks, mask)], 0)  80 us
    dot_general x12, local copies, waits for them, and re-layouts, product(): return jnp.einsum(form, left, right, preferred_element_type=jnp.float32)  49.9 us
    gather x9, local copies, waits for them, and re-layouts, reduce_ordered(): jnp.take(blocks, to_position(masks, shift), axis=0)  41.7 us
    add x32, other arithmetic, reduce_blocks(): blocks[:half]  36 us
  transfers between devices with their start and end apart: 127, of which 64 were waited for; matrix products, arithmetic and copies ran while one was open for 38% of the time, Pallas kernels for 0%

profile of v1, /device:TPU:0, one launch (start us, length us, event | category | flops | bytes accessed | tf_op | source)
XLA Modules:
  0.0 1519.8 jit_solution(1390948170639390099)
XLA Ops:
  13.3 16.9 %collective-permute-done.1 = bf16[2,96,1024]{2,1,0:T(8,128)(2,1)S(1)} collective-permute-done((bf16[2,96,1024]{2,1,0:T(8,128)(2,1)S(1)}, bf16[2,96,1024]{2,1,0:T(8,128)(2,1)S(1)}, u32[]{:S(2)}, u32[]{:S(2)}) %collective-permute-start.1) | collective-permute-done | bytes 393248 | tf_op jit(solution)/shard_map/ppermute | solution.py:53
  31.7 17.2 %collective-permute-done.2 = bf16[4,96,1024]{2,1,0:T(8,128)(2,1)S(1)} collective-permute-done((bf16[4,96,1024]{2,1,0:T(8,128)(2,1)S(1)}, bf16[4,96,1024]{2,1,0:T(8,128)(2,1)S(1)}, u32[]{:S(2)}, u32[]{:S(2)}) %collective-permute-start.2) | collective-permute-done | bytes 786464 | tf_op jit(solution)/shard_map/ppermute | solution.py:53
  56.3 27.2 %collective-permute-done.3 = bf16[8,96,1024]{2,1,0:T(8,128)(2,1)S(1)} collective-permute-done((bf16[8,96,1024]{2,1,0:T(8,128)(2,1)S(1)}, bf16[8,96,1024]{2,1,0:T(8,128)(2,1)S(1)}, u32[]{:S(2)}, u32[]{:S(2)}) %collective-permute-start.3) | collective-permute-done | bytes 1572896 | tf_op jit(solution)/shard_map/ppermute | solution.py:53
  185.5 12.7 collective-permute-done.31
  261.5 16.7 %collective-permute-done.22 = bf16[1,128,1024]{2,1,0:T(8,128)(2,1)S(1)} collective-permute-done((bf16[1,128,1024]{2,1,0:T(8,128)(2,1)S(1)}, bf16[1,128,1024]{2,1,0:T(8,128)(2,1)S(1)}, u32[]{:S(2)}, u32[]{:S(2)}) %collective-permute-start.22) | collective-permute-done | bytes 262176 | tf_op jit(solution)/shard_map/ppermute | solution.py:53
  299.0 34.2 %collective-permute-done.23 = bf16[2,128,1024]{2,1,0:T(8,128)(2,1)S(1)} collective-permute-done((bf16[2,128,1024]{2,1,0:T(8,128)(2,1)S(1)}, bf16[2,128,1024]{2,1,0:T(8,128)(2,1)S(1)}, u32[]{:S(2)}, u32[]{:S(2)}) %collective-permute-start.23) | collective-permute-done | bytes 524320 | tf_op jit(solution)/shard_map/ppermute | solution.py:53
  442.4 16.0 %collective-permute-done.26 = bf16[1,6,50,1024]{3,2,1,0:T(8,128)(2,1)S(1)} collective-permute-done((bf16[1,6,50,1024]{3,2,1,0:T(8,128)(2,1)S(1)}, bf16[1,6,50,1024]{3,2,1,0:T(8,128)(2,1)S(1)}, u32[]{:S(2)}, u32[]{:S(2)}) %collective-permute-start.26) | collective-permute-done | bytes 614432 | tf_op jit(solution)/shard_map/ppermute | solution.py:53
  467.7 15.1 collective-permute-done.27
  523.9 16.2 %collective-permute-done.36 = bf16[1,6,50,1024]{3,2,1,0:T(8,128)(2,1)S(1)} collective-permute-done((bf16[1,6,50,1024]{3,2,1,0:T(8,128)(2,1)S(1)}, bf16[1,6,50,1024]{3,2,1,0:T(8,128)(2,1)S(1)}, u32[]{:S(2)}, u32[]{:S(2)}) %collective-permute-start.36) | collective-permute-done | bytes 614432 | tf_op jit(solution)/shard_map/ppermute | solution.py:53
  547.3 15.4 %collective-permute-done.37 = bf16[1,6,50,1024]{3,2,1,0:T(8,128)(2,1)S(1)} collective-permute-done((bf16[1,6,50,1024]{3,2,1,0:T(8,128)(2,1)S(1)}, bf16[1,6,50,1024]{3,2,1,0:T(8,128)(2,1)S(1)}, u32[]{:S(2)}, u32[]{:S(2)}) %collective-permute-start.37) | collective-permute-done | bytes 614432 | tf_op jit(solution)/shard_map/ppermute | solution.py:53
  587.4 16.0 %collective-permute-done.46 = bf16[1,6,50,1024]{3,2,1,0:T(8,128)(2,1)S(1)} collective-permute-done((bf16[1,6,50,1024]{3,2,1,0:T(8,128)(2,1)S(1)}, bf16[1,6,50,1024]{3,2,1,0:T(8,128)(2,1)S(1)}, u32[]{:S(2)}, u32[]{:S(2)}) %collective-permute-start.46) | collective-permute-done | bytes 614432 | tf_op jit(solution)/shard_map/ppermute | solution.py:53
  609.0 15.1 collective-permute-done.52
  655.6 16.2 %collective-permute-done.55 = bf16[1,6,50,1024]{3,2,1,0:T(8,128)(2,1)} collective-permute-done((bf16[1,6,50,1024]{3,2,1,0:T(8,128)(2,1)}, bf16[1,6,50,1024]{3,2,1,0:T(8,128)(2,1)}, u32[]{:S(2)}, u32[]{:S(2)}) %collective-permute-start.55) | collective-permute-done | bytes 614432 | tf_op jit(solution)/shard_map/ppermute | solution.py:53
  995.3 11.9 broadcast_select_fusion.2
  1011.9 22.6 %collective-permute-done.119 = f32[2,4096]{1,0:T(2,128)S(1)} collective-permute-done((f32[2,4096]{1,0:T(2,128)S(1)}, f32[2,4096]{1,0:T(2,128)S(1)}, u32[]{:S(2)}, u32[]{:S(2)}) %collective-permute-start.119) | collective-permute-done | bytes 32800 | tf_op jit(solution)/shard_map/ppermute | solution.py:53
  1086.2 19.2 %collective-permute-done.85 = bf16[4,128,1024]{2,1,0:T(8,128)(2,1)} collective-permute-done((bf16[4,128,1024]{2,1,0:T(8,128)(2,1)}, bf16[4,128,1024]{2,1,0:T(8,128)(2,1)}, u32[]{:S(2)}, u32[]{:S(2)}) %collective-permute-start.85) | collective-permute-done | bytes 1048608 | tf_op jit(solution)/shard_map/ppermute | solution.py:53
  1110.9 14.6 collective-permute-done.88
  1133.8 14.6 collective-permute-done.86
  1149.4 10.1 collective-permute-done.89
  1270.1 10.5 gather_fusion.1
  1280.7 12.2 broadcast_select_fusion
  1361.7 16.8 %collective-permute-done.69 = bf16[8,96,1024]{2,1,0:T(8,128)(2,1)S(1)} collective-permute-done((bf16[8,96,1024]{2,1,0:T(8,128)(2,1)S(1)}, bf16[8,96,1024]{2,1,0:T(8,128)(2,1)S(1)}, u32[]{:S(2)}, u32[]{:S(2)}) %collective-permute-start.69) | collective-permute-done | bytes 1572896 | tf_op jit(solution)/shard_map/ppermute | solution.py:53
  1409.8 14.4 collective-permute-done.100
  1477.8 10.8 multiply_subtract_fusion
  (1397 shorter events, 1106.3 us)
Async XLA Ops:
  50.4 58.9 %collective-permute-start.7 = (bf16[1,128,3,256]{3,1,2,0:T(8,128)(2,1)S(1)}, bf16[1,128,3,256]{3,1,2,0:T(8,128)(2,1)S(1)}, u32[]{:S(2)}, u32[]{:S(2)}) collective-permute-start(bf16[1,128,3,256]{3,1,2,0:T(8,128)(2,1)S(1)} %get-tuple-element.351), channel_id=1, source_target_pairs={{0,8},{1,9},{2,10},{3,11},{4,12},{5,13},{6,14},{7,15},{8,0},{9,1},... | collective-permute-start | bytes 589832 | tf_op jit(solution)/shard_map/ppermute | solution.py:53
  52.2 89.9 %collective-permute-start.29 = (bf16[1,128,3,256]{3,1,2,0:T(8,128)(2,1)S(1)}, bf16[1,128,3,256]{3,1,2,0:T(8,128)(2,1)}, u32[]{:S(2)}, u32[]{:S(2)}) collective-permute-start(bf16[1,128,3,256]{3,1,2,0:T(8,128)(2,1)S(1)} %get-tuple-element.350), channel_id=1, source_target_pairs={{0,8},{1,9},{2,10},{3,11},{4,12},{5,13},{6,14},{7,15},{8,0},{9,1},... | collective-permute-start | bytes 589832 | tf_op jit(solution)/shard_map/ppermute | solution.py:53
  86.3 57.4 %collective-permute-start.10 = (bf16[1,6,50]{2,1,0:T(8,128)(2,1)}, bf16[1,6,50]{2,1,0:T(8,128)(2,1)}, u32[]{:S(2)}, u32[]{:S(2)}) collective-permute-start(bf16[1,6,50]{2,1,0:T(8,128)(2,1)} %fusion.235), channel_id=1, source_target_pairs={{0,2},{1,3},{2,0},{3,1},{4,6},{5,7},{6,4},{7,5},{8,10},{9,11},{10,... | collective-permute-start | bytes 1808 | tf_op jit(solution)/shard_map/ppermute | solution.py:53
  278.3 54.8 %collective-permute-start.23 = (bf16[2,128,1024]{2,1,0:T(8,128)(2,1)S(1)}, bf16[2,128,1024]{2,1,0:T(8,128)(2,1)S(1)}, u32[]{:S(2)}, u32[]{:S(2)}) collective-permute-start(bf16[2,128,1024]{2,1,0:T(8,128)(2,1)S(1)} %pad_maximum_fusion.38), channel_id=1, source_target_pairs={{0,16},{1,17},{2,18},{3,19},{4,20},{5,21},{6,22},{7,23},{8,24},{9,... | collective-permute-start | bytes 1572872 | tf_op jit(solution)/shard_map/ppermute | solution.py:53
  284.0 60.3 %collective-permute-start.20 = (bf16[2,128,1024]{2,1,0:T(8,128)(2,1)S(1)}, bf16[2,128,1024]{2,1,0:T(8,128)(2,1)S(1)}, u32[]{:S(2)}, u32[]{:S(2)}) collective-permute-start(bf16[2,128,1024]{2,1,0:T(8,128)(2,1)S(1)} %pad_maximum_fusion.37), channel_id=1, source_target_pairs={{0,16},{1,17},{2,18},{3,19},{4,20},{5,21},{6,22},{7,23},{8,24},{9,... | collective-permute-start | bytes 1572872 | tf_op jit(solution)/shard_map/ppermute | solution.py:53
  289.3 66.2 %collective-permute-start.40 = (bf16[2,128,1024]{2,1,0:T(8,128)(2,1)S(1)}, bf16[2,128,1024]{2,1,0:T(8,128)(2,1)S(1)}, u32[]{:S(2)}, u32[]{:S(2)}) collective-permute-start(bf16[2,128,1024]{2,1,0:T(8,128)(2,1)S(1)} %pad_maximum_fusion.40), channel_id=1, source_target_pairs={{0,16},{1,17},{2,18},{3,19},{4,20},{5,21},{6,22},{7,23},{8,24},{9,... | collective-permute-start | bytes 1572872 | tf_op jit(solution)/shard_map/ppermute | solution.py:53
  294.7 63.5 %collective-permute-start.16 = (bf16[1,6,50,1024]{3,2,1,0:T(8,128)(2,1)S(1)}, bf16[1,6,50,1024]{3,2,1,0:T(8,128)(2,1)S(1)}, u32[]{:S(2)}, u32[]{:S(2)}) collective-permute-start(bf16[1,6,50,1024]{3,2,1,0:T(8,128)(2,1)S(1)} %copy.1026), channel_id=1, source_target_pairs={{0,2},{1,3},{2,0},{3,1},{4,6},{5,7},{6,4},{7,5},{8,10},{9,11},{10,... | collective-permute-start | bytes 1843208 | tf_op jit(solution)/shard_map/ppermute | solution.py:53
  297.4 71.0 %collective-permute-start.44 = (bf16[4,128,1024]{2,1,0:T(8,128)(2,1)}, bf16[4,128,1024]{2,1,0:T(8,128)(2,1)}, u32[]{:S(2)}, u32[]{:S(2)}) collective-permute-start(bf16[4,128,1024]{2,1,0:T(8,128)(2,1)} %pad_maximum_fusion.29), channel_id=1, source_target_pairs={{0,4},{1,5},{2,6},{3,7},{4,0},{5,1},{6,2},{7,3},{8,12},{9,13},{10,... | collective-permute-start | bytes 3145736 | tf_op jit(solution)/shard_map/ppermute | solution.py:53
  334.3 53.4 %collective-permute-start.24 = (bf16[4,128,1024]{2,1,0:T(8,128)(2,1)}, bf16[4,128,1024]{2,1,0:T(8,128)(2,1)}, u32[]{:S(2)}, u32[]{:S(2)}) collective-permute-start(bf16[4,128,1024]{2,1,0:T(8,128)(2,1)} %pad_maximum_fusion.27), channel_id=1, source_target_pairs={{0,4},{1,5},{2,6},{3,7},{4,0},{5,1},{6,2},{7,3},{8,12},{9,13},{10,... | collective-permute-start | bytes 3145736 | tf_op jit(solution)/shard_map/ppermute | solution.py:53
  345.5 48.6 %collective-permute-start.21 = (bf16[4,128,1024]{2,1,0:T(8,128)(2,1)}, bf16[4,128,1024]{2,1,0:T(8,128)(2,1)}, u32[]{:S(2)}, u32[]{:S(2)}) collective-permute-start(bf16[4,128,1024]{2,1,0:T(8,128)(2,1)} %pad_maximum_fusion.26), channel_id=1, source_target_pairs={{0,4},{1,5},{2,6},{3,7},{4,0},{5,1},{6,2},{7,3},{8,12},{9,13},{10,... | collective-permute-start | bytes 3145736 | tf_op jit(solution)/shard_map/ppermute | solution.py:53
  356.6 47.9 %collective-permute-start.41 = (bf16[4,128,1024]{2,1,0:T(8,128)(2,1)}, bf16[4,128,1024]{2,1,0:T(8,128)(2,1)}, u32[]{:S(2)}, u32[]{:S(2)}) collective-permute-start(bf16[4,128,1024]{2,1,0:T(8,128)(2,1)} %pad_maximum_fusion.28), channel_id=1, source_target_pairs={{0,4},{1,5},{2,6},{3,7},{4,0},{5,1},{6,2},{7,3},{8,12},{9,13},{10,... | collective-permute-start | bytes 3145736 | tf_op jit(solution)/shard_map/ppermute | solution.py:53
  748.8 82.8 %collective-permute-start.102 = (bf16[1,6,1024]{2,0,1:T(2,128)(2,1)}, bf16[1,6,1024]{2,0,1:T(2,128)(2,1)}, u32[]{:S(2)}, u32[]{:S(2)}) collective-permute-start(bf16[1,6,1024]{2,0,1:T(2,128)(2,1)} %fusion.228), channel_id=1, source_target_pairs={{0,8},{1,9},{2,10},{3,11},{4,12},{5,13},{6,14},{7,15},{8,0},{9,1},... | collective-permute-start | bytes 36872 | tf_op jit(solution)/shard_map/ppermute | solution.py:53
  749.7 84.4 %collective-permute-start.107 = (f32[1,6,1000]{2,1,0:T(8,128)}, f32[1,6,1000]{2,1,0:T(8,128)}, u32[]{:S(2)}, u32[]{:S(2)}) collective-permute-start(f32[1,6,1000]{2,1,0:T(8,128)} %fusion.258), channel_id=1, source_target_pairs={{0,8},{1,9},{2,10},{3,11},{4,12},{5,13},{6,14},{7,15},{8,0},{9,1},... | collective-permute-start | bytes 72008 | tf_op jit(solution)/shard_map/ppermute | solution.py:53
  809.4 48.1 %collective-permute-start.58 = (bf16[2,6,50,1024]{3,0,2,1:T(2,128)(2,1)}, bf16[2,6,50,1024]{3,0,2,1:T(2,128)(2,1)}, u32[]{:S(2)}, u32[]{:S(2)}) collective-permute-start(bf16[2,6,50,1024]{3,0,2,1:T(2,128)(2,1)} %copy.1109), channel_id=1, source_target_pairs={{0,1},{1,0},{2,3},{3,2},{4,5},{5,4},{6,7},{7,6},{8,9},{9,8},{10,11... | collective-permute-start | bytes 3686408 | tf_op jit(solution)/shard_map/ppermute | solution.py:53
  967.9 72.3 %collective-permute-start.62 = (bf16[2,6,50,1024]{3,0,2,1:T(2,128)(2,1)}, bf16[2,6,50,1024]{3,0,2,1:T(2,128)(2,1)}, u32[]{:S(2)}, u32[]{:S(2)}) collective-permute-start(bf16[2,6,50,1024]{3,0,2,1:T(2,128)(2,1)} %copy.1125), channel_id=1, source_target_pairs={{0,1},{1,0},{2,3},{3,2},{4,5},{5,4},{6,7},{7,6},{8,9},{9,8},{10,11... | collective-permute-start | bytes 3686408 | tf_op jit(solution)/shard_map/ppermute | solution.py:53
  1008.3 58.5 %collective-permute-start.91 = (bf16[4,128,1024]{2,1,0:T(8,128)(2,1)}, bf16[4,128,1024]{2,1,0:T(8,128)(2,1)S(1)}, u32[]{:S(2)}, u32[]{:S(2)}) collective-permute-start(bf16[4,128,1024]{2,1,0:T(8,128)(2,1)} %slice.992), channel_id=1, source_target_pairs={{0,4},{1,5},{2,6},{3,7},{4,0},{5,1},{6,2},{7,3},{8,12},{9,13},{10,... | collective-permute-start | bytes 3145736 | tf_op jit(solution)/shard_map/ppermute | solution.py:53
  1064.1 61.3 %collective-permute-start.88 = (bf16[4,128,1024]{2,1,0:T(8,128)(2,1)}, bf16[4,128,1024]{2,1,0:T(8,128)(2,1)}, u32[]{:S(2)}, u32[]{:S(2)}) collective-permute-start(bf16[4,128,1024]{2,1,0:T(8,128)(2,1)} %slice.993), channel_id=1, source_target_pairs={{0,4},{1,5},{2,6},{3,7},{4,0},{5,1},{6,2},{7,3},{8,12},{9,13},{10,... | collective-permute-start | bytes 3145736 | tf_op jit(solution)/shard_map/ppermute | solution.py:53
  1068.2 60.6 %collective-permute-start.92 = (bf16[2,128,1024]{2,1,0:T(8,128)(2,1)}, bf16[2,128,1024]{2,1,0:T(8,128)(2,1)}, u32[]{:S(2)}, u32[]{:S(2)}) collective-permute-start(bf16[2,128,1024]{2,1,0:T(8,128)(2,1)} %slice.1009), channel_id=1, source_target_pairs={{0,16},{1,17},{2,18},{3,19},{4,20},{5,21},{6,22},{7,23},{8,24},{9,... | collective-permute-start | bytes 1572872 | tf_op jit(solution)/shard_map/ppermute | solution.py:53
  1110.8 52.0 %collective-permute-start.65 = (bf16[2,6,50,1024]{3,0,2,1:T(2,128)(2,1)S(1)}, bf16[2,6,50,1024]{3,0,2,1:T(2,128)(2,1)S(1)}, u32[]{:S(2)}, u32[]{:S(2)}) collective-permute-start(bf16[2,6,50,1024]{3,0,2,1:T(2,128)(2,1)S(1)} %copy.1137), channel_id=1, source_target_pairs={{0,1},{1,0},{2,3},{3,2},{4,5},{5,4},{6,7},{7,6},{8,9},{9,8},{10,11... | collective-permute-start | bytes 3686408 | tf_op jit(solution)/shard_map/ppermute | solution.py:53
  1130.8 89.3 %collective-permute-start.93 = (bf16[1,128,1024]{2,1,0:T(8,128)(2,1)}, bf16[1,128,1024]{2,1,0:T(8,128)(2,1)}, u32[]{:S(2)}, u32[]{:S(2)}) collective-permute-start(bf16[1,128,1024]{2,1,0:T(8,128)(2,1)} %slice.1016), channel_id=1, source_target_pairs={{0,8},{1,9},{2,10},{3,11},{4,12},{5,13},{6,14},{7,15},{8,0},{9,1},... | collective-permute-start | bytes 786440 | tf_op jit(solution)/shard_map/ppermute | solution.py:53
  1132.6 88.7 %collective-permute-start.96 = (bf16[1,128,1024]{2,1,0:T(8,128)(2,1)}, bf16[1,128,1024]{2,1,0:T(8,128)(2,1)}, u32[]{:S(2)}, u32[]{:S(2)}) collective-permute-start(bf16[1,128,1024]{2,1,0:T(8,128)(2,1)} %slice.1015), channel_id=1, source_target_pairs={{0,8},{1,9},{2,10},{3,11},{4,12},{5,13},{6,14},{7,15},{8,0},{9,1},... | collective-permute-start | bytes 786440 | tf_op jit(solution)/shard_map/ppermute | solution.py:53
  1149.4 74.1 %collective-permute-start.87 = (bf16[1,128,1024]{2,1,0:T(8,128)(2,1)}, bf16[1,128,1024]{2,1,0:T(8,128)(2,1)}, u32[]{:S(2)}, u32[]{:S(2)}) collective-permute-start(bf16[1,128,1024]{2,1,0:T(8,128)(2,1)} %slice.1018), channel_id=1, source_target_pairs={{0,8},{1,9},{2,10},{3,11},{4,12},{5,13},{6,14},{7,15},{8,0},{9,1},... | collective-permute-start | bytes 786440 | tf_op jit(solution)/shard_map/ppermute | solution.py:53
  1160.6 64.1 %collective-permute-start.90 = (bf16[1,128,1024]{2,1,0:T(8,128)(2,1)}, bf16[1,128,1024]{2,1,0:T(8,128)(2,1)}, u32[]{:S(2)}, u32[]{:S(2)}) collective-permute-start(bf16[1,128,1024]{2,1,0:T(8,128)(2,1)} %slice.1017), channel_id=1, source_target_pairs={{0,8},{1,9},{2,10},{3,11},{4,12},{5,13},{6,14},{7,15},{8,0},{9,1},... | collective-permute-start | bytes 786440 | tf_op jit(solution)/shard_map/ppermute | solution.py:53
  1239.8 58.1 %collective-permute-start.112 = (f32[2,2,1024]{2,1,0:T(2,128)}, f32[2,2,1024]{2,1,0:T(2,128)}, u32[]{:S(2)}, u32[]{:S(2)}) collective-permute-start(f32[2,2,1024]{2,1,0:T(2,128)} %pad_maximum_fusion.58), channel_id=1, source_target_pairs={{0,1},{1,0},{2,3},{3,2},{4,5},{5,4},{6,7},{7,6},{8,9},{9,8},{10,11... | collective-permute-start | bytes 49160 | tf_op jit(solution)/shard_map/ppermute | solution.py:53
  (408 other events, 5589.6 us)

commit v2 on v0

v2 whole, which is shorter than its diff:
```python
import functools

import jax
import jax.numpy as jnp
from jax import lax
from jax.experimental import pallas as pl
from jax.experimental.pallas import tpu as pltpu
from jax.sharding import PartitionSpec as P

HEAD_DIM = 64
CLASSES = 1000
PATCHES = 49
LAYERS = 2
STEP = 10
SLOTS = 50
AXES = ("dp", "mp")

group_rates = (0.01, 0.2, 0.01, 0.01, 0.1, 0.03, 0.01, 0.1, 0.01)
beta_one = 0.9
beta_two = 0.95
adam_eps = 1e-08
decay_rate = 0.1
clip_limit = 0.02
norm_eps = 1e-06
highest = lax.Precision.HIGHEST
low_type = jnp.bfloat16
wide_type = jnp.float32


def swap(values, mask):
    count = lax.axis_size("dp") * lax.axis_size("mp")
    return lax.ppermute(values, AXES, [(n, n ^ mask) for n in range(count)])


def device_index():
    return lax.axis_index("dp") * lax.axis_size("mp") + lax.axis_index("mp")


def bit_masks():
    model, data = lax.axis_size("mp"), lax.axis_size("dp")
    wide = 1 << ((data.bit_length() - 1) // 2)
    z_masks = [m for m in (model * wide << b for b in range(16)) if m < model * data]
    y_masks = [m for m in (model << b for b in range(16)) if m < model * wide]
    x_masks = [m for m in (2 << b for b in range(16)) if m < model]
    return (z_masks, y_masks, x_masks, [1])


def offsets(masks):
    table = [0]
    for mask in masks:
        table = table + [entry ^ mask for entry in table]
    return table


def gather_halves(values, masks):
    blocks = values[None]
    for mask in masks[:-1]:
        blocks = jnp.concatenate([blocks, swap(blocks, mask)], 0)
    return blocks, swap(blocks, masks[-1])


def gather_ordered(values, masks):
    blocks = jnp.concatenate(gather_halves(values, masks), 0)
    inverse = [0] * len(offsets(masks))
    for place, entry in enumerate(offsets(masks)):
        inverse[entry] = place
    places = jnp.array(inverse, jnp.int32)
    order = places.at[jnp.arange(len(inverse)) ^ device_index()].get(mode="promise_in_bounds")
    return blocks.at[order].get(mode="promise_in_bounds")


def reduce_halves(kept, sent, masks):
    total = kept.astype(wide_type) + swap(sent, masks[-1]).astype(wide_type)
    for mask in reversed(masks[:-1]):
        half = total.shape[0] // 2
        total = total[:half] + swap(total[half:].astype(low_type), mask).astype(wide_type)
    return total[0]


def sum_all(values):
    for masks in reversed(bit_masks()):
        for mask in masks:
            values = jax.tree.map(lambda v: v + swap(v, mask), values)
    return values


def group_pieces(values, x_masks):
    pieces = [values]
    for mask in x_masks:
        pieces = pieces + [swap(piece, mask) for piece in pieces]
    return pieces + [swap(piece, 1) for piece in pieces]


def group_sum(partials, x_masks):
    sums = [kept + swap(sent, 1).astype(wide_type) for kept, sent in partials]
    for mask in reversed(x_masks):
        half = len(sums) // 2
        sums = [
            near + swap(far.astype(low_type), mask).astype(wide_type)
            for near, far in zip(sums[:half], sums[half:])
        ]
    return sums[0]


def dot_nn(left, right):
    return jnp.dot(left, right, preferred_element_type=wide_type)


def dot_nt(left, right):
    return lax.dot_general(left, right, (((1,), (1,)), ((), ())), preferred_element_type=wide_type)


def dot_tn(left, right):
    return lax.dot_general(left, right, (((0,), (0,)), ((), ())), preferred_element_type=wide_type)


def normalise(values):
    centre = values - jnp.mean(values, -1, keepdims=True)
    spread = jnp.mean(centre * centre, -1, keepdims=True)
    scale = lax.rsqrt(spread + norm_eps)
    return centre * scale, scale


def normalise_back(hat, scale, gain, grad):
    lifted = grad * gain
    return scale * (
        lifted
        - jnp.mean(lifted, -1, keepdims=True)
        - hat * jnp.mean(lifted * hat, -1, keepdims=True)
    )


def start_weights(tab_ref, halves, w_ref, sems):
    count, width, rows, columns = halves[0].shape
    for side, half in enumerate(halves):

        def step(r, carry):
            row = pl.multiple_of(tab_ref[0, side * count + r] * rows, rows)
            column = pl.multiple_of(tab_ref[1, side * count + r] * columns, columns)
            for k in range(width):
                pltpu.make_async_copy(
                    half.at[r, k],
                    w_ref.at[k, pl.ds(row, rows), pl.ds(column, columns)],
                    sems.at[k],
                ).start()
            return carry

        lax.fori_loop(0, count, step, 0)


def wait_weights(w_ref, sems, k):
    pltpu.make_async_copy(w_ref.at[k], w_ref.at[k], sems.at[k]).wait()


def store_grads(tab_ref, g_ref, halves, sem, k):
    count, width, rows, columns = halves[0].shape
    for side, half in enumerate(halves):

        def step(r, carry):
            row = pl.multiple_of(tab_ref[0, side * count + r] * rows, rows)
            column = pl.multiple_of(tab_ref[1, side * count + r] * columns, columns)
            pltpu.make_async_copy(
                g_ref.at[k, pl.ds(row, rows), pl.ds(column, columns)], half.at[r, k], sem.at[k]
            ).start()
            return carry

        lax.fori_loop(0, count, step, 0)


def lane_masks():
    lane = lax.broadcasted_iota(jnp.int32, (1, 2 * HEAD_DIM), 1)
    return (lane < HEAD_DIM, lane >= HEAD_DIM)


def softmax_rows(query, keys, bias):
    scores = dot_nt(query, keys) * 0.125 + bias
    powers = jnp.exp(scores - jnp.max(scores, -1, keepdims=True))
    return powers / jnp.sum(powers, -1, keepdims=True)


def attention_forward_kernel(
    tab_ref, stream_ref, vec_ref, shift_ref, bias_ref, half_a, half_b,
    middle_ref, second_ref, first_ref, qkv_ref, mixed_ref, w_ref, sems,
):
    start_weights(tab_ref, (half_a, half_b), w_ref, sems)
    width = stream_ref.shape[1]
    hat, scale = normalise(stream_ref[...])
    first_ref[...] = (hat * vec_ref[0:1, :] + vec_ref[1:2, :]).astype(low_type)
    for k in range(3):
        wait_weights(w_ref, sems, k)
        for c in range(0, width, 256):
            part = dot_nn(first_ref[...], w_ref[k, :, c : c + 256]) + shift_ref[k : k + 1, c : c + 256]
            qkv_ref[k, :, c : c + 256] = part.astype(low_type)

    def pair(h, carry):
        at = pl.ds(pl.multiple_of(h * 128, 128), 128)
        query, keys, values = qkv_ref[0, :, at], qkv_ref[1, :, at], qkv_ref[2, :, at]
        outs = []
        for lanes in lane_masks():
            own = jnp.where(lanes, query, jnp.zeros_like(query))
            probs = softmax_rows(own, keys, bias_ref[...]).astype(low_type)
            outs.append(dot_nn(probs, values))
        mixed_ref[:, at] = jnp.where(lane_masks()[0], outs[0], outs[1]).astype(low_type)
        return carry

    lax.fori_loop(0, width // 128, pair, 0)
    wait_weights(w_ref, sems, 3)
    for c in range(0, width, 256):
        middle_ref[:, c : c + 256] = (
            stream_ref[:, c : c + 256]
            + dot_nt(mixed_ref[...], w_ref[3, c : c + 256, :])
            + vec_ref[4:5, c : c + 256]
        )
    hat, scale = normalise(middle_ref[...])
    second_ref[...] = (hat * vec_ref[2:3, :] + vec_ref[3:4, :]).astype(low_type)


def attention_chain_kernel(
    tab_ref, upper_ref, pull_ref, middle_ref, stream_ref, vec_ref, bias_ref, qkv_ref, half_a, half_b,
    below_ref, below_low_ref, up_ref, joined_ref, rows_ref, w_ref, sems, mixed_grad_ref, mid_grad_ref, norm_grad_ref,
):
    start_weights(tab_ref, (half_a, half_b), w_ref, sems)
    width = stream_ref.shape[1]
    upper = upper_ref[...]
    rows_ref[5:6, :] = jnp.sum(upper, 0, keepdims=True)
    pull = pull_ref[...]
    hat, scale = normalise(middle_ref[...])
    rows_ref[2:3, :] = jnp.sum(pull * hat, 0, keepdims=True)
    rows_ref[3:4, :] = jnp.sum(pull, 0, keepdims=True)
    mid_grad = upper + normalise_back(hat, scale, vec_ref[2:3, :], pull)
    mid_grad_ref[...] = mid_grad
    rows_ref[4:5, :] = jnp.sum(mid_grad, 0, keepdims=True)
    up_ref[...] = mid_grad.astype(low_type)
    wait_weights(w_ref, sems, 3)
    for c in range(0, width, 256):
        mixed_grad_ref[:, c : c + 256] = dot_nn(up_ref[...], w_ref[3, :, c : c + 256]).astype(low_type)

    def pair(h, carry):
        at = pl.ds(pl.multiple_of(h * 128, 128), 128)
        query, keys, values = qkv_ref[0, :, at], qkv_ref[1, :, at], qkv_ref[2, :, at]
        grads = mixed_grad_ref[:, at]
        outs = []
        for lanes in lane_masks():
            own = jnp.where(lanes, query, jnp.zeros_like(query))
            own_grad = jnp.where(lanes, grads, jnp.zeros_like(grads))
            probs = softmax_rows(own, keys, bias_ref[...])
            value_grad = dot_tn(probs.astype(low_type), grads)
            prob_grad = dot_nt(own_grad, values)
            weighted = probs * prob_grad
            score_grad = (
                (weighted - probs * jnp.sum(weighted, -1, keepdims=True)) * 0.125
            ).astype(low_type)
            outs.append((dot_nn(score_grad, keys), dot_tn(score_grad, query), value_grad))
        for k in range(3):
            part = jnp.where(lane_masks()[0], outs[0][k], outs[1][k])
            joined_ref[k, :, at] = part.astype(low_type)
            if k != 1:
                rows_ref[6 + k // 2 : 7 + k // 2, at] = jnp.sum(part, 0, keepdims=True)
        return carry

    lax.fori_loop(0, width // 128, pair, 0)
    for k in range(3):
        wait_weights(w_ref, sems, k)
    for c in range(0, width, 256):
        norm_grad_ref[:, c : c + 256] = (
            dot_nt(joined_ref[0], w_ref[0, c : c + 256, :])
            + dot_nt(joined_ref[1], w_ref[1, c : c + 256, :])
            + dot_nt(joined_ref[2], w_ref[2, c : c + 256, :])
        )
    hat, scale = normalise(stream_ref[...])
    norm_grad = norm_grad_ref[...]
    rows_ref[0:1, :] = jnp.sum(norm_grad * hat, 0, keepdims=True)
    rows_ref[1:2, :] = jnp.sum(norm_grad, 0, keepdims=True)
    below = mid_grad_ref[...] + normalise_back(hat, scale, vec_ref[0:1, :], norm_grad)
    below_ref[...] = below
    below_low_ref[...] = below.astype(low_type)


def attention_weights_kernel(
    tab_ref, first_ref, joined_ref, up_ref, mixed_ref, half_a, half_b, g_ref, sems
):
    width = first_ref.shape[1]
    for k in range(4):
        for c in range(0, width, 256):
            if k < 3:
                part = dot_tn(first_ref[...], joined_ref[k, :, c : c + 256])
            else:
                part = dot_tn(up_ref[...], mixed_ref[:, c : c + 256])
            g_ref[k, :, c : c + 256] = part.astype(low_type)
        store_grads(tab_ref, g_ref, (half_a, half_b), sems, k)
    for k in range(4):
        wait_weights(g_ref, sems, k)


gelu_scale = 0.7978845608028654
gelu_cube = 0.044715


def hidden_forward_kernel(
    tab_ref, here_ref, there_ref, raise_ref, half_a, half_b, kept_ref, sent_ref, w_ref, active_ref, sems
):
    start_weights(tab_ref, (half_a, half_b), w_ref, sems)
    rows, width = here_ref.shape
    hidden_width = active_ref.shape[1]
    wait_weights(w_ref, sems, 0)
    for side, source in enumerate((here_ref, there_ref)):
        for c in range(0, hidden_width, 256):
            hidden = dot_nn(source[...], w_ref[0, :, c : c + 256]) + raise_ref[0:1, c : c + 256]
            bent = jnp.tanh(gelu_scale * (hidden + gelu_cube * (hidden * hidden * hidden)))
            active_ref[side * rows : (side + 1) * rows, c : c + 256] = (
                hidden * (0.5 * (1.0 + bent))
            ).astype(low_type)
    wait_weights(w_ref, sems, 1)
    for c in range(0, width, 256):
        kept_ref[:, c : c + 256] = dot_nt(active_ref[0:rows, :], w_ref[1, c : c + 256, :])
        sent_ref[:, c : c + 256] = dot_nt(active_ref[rows : 2 * rows, :], w_ref[1, c : c + 256, :]).astype(low_type)


def hidden_chain_kernel(
    tab_ref, here_ref, there_ref, down_here_ref, down_there_ref, raise_ref, half_a, half_b,
    kept_ref, sent_ref, active_ref, grad_ref, raise_grad_ref, w_ref, sems,
):
    start_weights(tab_ref, (half_a, half_b), w_ref, sems)
    rows, width = here_ref.shape
    hidden_width = active_ref.shape[1]
    wait_weights(w_ref, sems, 0)
    wait_weights(w_ref, sems, 1)
    pairs = ((here_ref, down_here_ref), (there_ref, down_there_ref))
    for c in range(0, hidden_width, 256):
        total = jnp.zeros((1, 256), wide_type)
        for side, (source, down) in enumerate(pairs):
            hidden = dot_nn(source[...], w_ref[0, :, c : c + 256]) + raise_ref[0:1, c : c + 256]
            pulled = dot_nn(down[...], w_ref[1, :, c : c + 256])
            square = hidden * hidden
            bent = jnp.tanh(gelu_scale * (hidden + gelu_cube * (square * hidden)))
            share = 0.5 * (1.0 + bent)
            active_ref[side * rows : (side + 1) * rows, c : c + 256] = (hidden * share).astype(low_type)
            slope = share + (0.5 * hidden) * (1.0 - bent * bent) * (
                gelu_scale + (3.0 * gelu_scale * gelu_cube) * square
            )
            grad = pulled * slope
            grad_ref[side * rows : (side + 1) * rows, c : c + 256] = grad.astype(low_type)
            total = total + jnp.sum(grad, 0, keepdims=True)
        raise_grad_ref[0:1, c : c + 256] = total
    for c in range(0, width, 256):
        kept_ref[:, c : c + 256] = dot_nt(grad_ref[0:rows, :], w_ref[0, c : c + 256, :])
        sent_ref[:, c : c + 256] = dot_nt(grad_ref[rows : 2 * rows, :], w_ref[0, c : c + 256, :]).astype(low_type)


def hidden_weights_kernel(count, tab_ref, *refs):
    groups = [refs[6 * g : 6 * g + 6] for g in range(count)]
    half_a, half_b, g_ref, inputs_ref, down_ref, active_ref, grad_ref, sems = refs[6 * count :]
    rows, width = groups[0][0].shape
    hidden_width = active_ref.shape[1]
    for g, (here, there, down_here, down_there, active, grad) in enumerate(groups):
        at = 2 * g * rows
        inputs_ref[at : at + rows, :] = here[...]
        inputs_ref[at + rows : at + 2 * rows, :] = there[...]
        down_ref[at : at + rows, :] = down_here[...]
        down_ref[at + rows : at + 2 * rows, :] = down_there[...]
        active_ref[at : at + 2 * rows, :] = active[...]
        grad_ref[at : at + 2 * rows, :] = grad[...]
    for k, (left, right) in enumerate(((inputs_ref, grad_ref), (down_ref, active_ref))):
        for c in range(0, hidden_width, 256):
            g_ref[k, :, c : c + 256] = dot_tn(left[...], right[:, c : c + 256]).astype(low_type)
        store_grads(tab_ref, g_ref, (half_a, half_b), sems, k)
    for k in range(2):
        wait_weights(g_ref, sems, k)


def head_kernel(final_ref, logit_ref, out_ref):
    width = final_ref.shape[1]
    logit = logit_ref[...]
    out_ref[0:width, :] = dot_tn(final_ref[...], logit.astype(low_type))
    out_ref[width : width + 1, :] = jnp.sum(logit, 0, keepdims=True)


smem = pl.BlockSpec(memory_space=pltpu.SMEM)
vmem = pl.BlockSpec(memory_space=pltpu.VMEM)
anywhere = pl.BlockSpec(memory_space=pl.ANY)


def call(kernel, in_specs, outs, scratch, flops, moved):
    return pl.pallas_call(
        kernel,
        out_shape=tuple(jax.ShapeDtypeStruct(shape, kind) for shape, kind, spec in outs),
        in_specs=in_specs,
        out_specs=tuple(spec for shape, kind, spec in outs),
        scratch_shapes=scratch,
        compiler_params=pltpu.CompilerParams(vmem_limit_bytes=48 * 1024 * 1024),
        cost_estimate=pl.CostEstimate(flops=flops, bytes_accessed=moved, transcendentals=0),
    )


def attention_forward(tab, stream, vec, shift, bias, halves):
    rows, width = stream.shape
    return call(
        attention_forward_kernel,
        [smem] + [vmem] * 4 + [anywhere] * 2,
        [
            ((rows, width), wide_type, vmem),
            ((rows, width), low_type, vmem),
            ((rows, width), low_type, vmem),
            ((3, rows, width), low_type, vmem),
            ((rows, width), low_type, vmem),
        ],
        [pltpu.VMEM((4, width, width), low_type), pltpu.SemaphoreType.DMA((4,))],
        20 * rows * width * width,
        20 * width * width,
    )(tab, stream, vec, shift, bias, *halves)


def attention_chain(tab, upper, pull, middle, stream, vec, bias, qkv, halves):
    rows, width = stream.shape
    return call(
        attention_chain_kernel,
        [smem] + [vmem] * 7 + [anywhere] * 2,
        [
            ((rows, width), wide_type, vmem),
            ((rows, width), low_type, vmem),
            ((rows, width), low_type, vmem),
            ((3, rows, width), low_type, vmem),
            ((8, width), wide_type, vmem),
        ],
        [
            pltpu.VMEM((4, width, width), low_type),
            pltpu.SemaphoreType.DMA((4,)),
            pltpu.VMEM((rows, width), low_type),
            pltpu.VMEM((rows, width), wide_type),
            pltpu.VMEM((rows, width), wide_type),
        ],
        30 * rows * width * width,
        30 * width * width,
    )(tab, upper, pull, middle, stream, vec, bias, qkv, *halves)


def attention_weights(tab, first, joined, up, mixed, half_shape):
    rows, width = first.shape
    return call(
        attention_weights_kernel,
        [smem] + [vmem] * 4,
        [(half_shape, low_type, anywhere)] * 2,
        [pltpu.VMEM((4, width, width), low_type), pltpu.SemaphoreType.DMA((4,))],
        16 * rows * width * width,
        16 * width * width,
    )(tab, first, joined, up, mixed)


def hidden_forward(tab, here, there, raise_row, halves):
    rows, width = here.shape
    hidden_width = raise_row.shape[1]
    return call(
        hidden_forward_kernel,
        [smem] + [vmem] * 3 + [anywhere] * 2,
        [((rows, width), wide_type, vmem), ((rows, width), low_type, vmem)],
        [
            pltpu.VMEM((2, width, hidden_width), low_type),
            pltpu.VMEM((2 * rows, hidden_width), low_type),
            pltpu.SemaphoreType.DMA((2,)),
        ],
        16 * rows * width * hidden_width,
        10 * width * hidden_width,
    )(tab, here, there, raise_row, *halves)


def hidden_chain(tab, here, there, down_here, down_there, raise_row, halves):
    rows, width = here.shape
    hidden_width = raise_row.shape[1]
    return call(
        hidden_chain_kernel,
        [smem] + [vmem] * 5 + [anywhere] * 2,
        [
            ((rows, width), wide_type, vmem),
            ((rows, width), low_type, vmem),
            ((2 * rows, hidden_width), low_type, vmem),
            ((2 * rows, hidden_width), low_type, vmem),
            ((1, hidden_width), wide_type, vmem),
        ],
        [pltpu.VMEM((2, width, hidden_width), low_type), pltpu.SemaphoreType.DMA((2,))],
        20 * rows * width * hidden_width,
        20 * width * hidden_width,
    )(tab, here, there, down_here, down_there, raise_row, *halves)


def hidden_weights(tab, groups, half_shape):
    rows, width = groups[0][0].shape
    hidden_width = groups[0][4].shape[1]
    count = len(groups)
    return call(
        functools.partial(hidden_weights_kernel, count),
        [smem] + [vmem] * (6 * count),
        [(half_shape, low_type, anywhere)] * 2,
        [
            pltpu.VMEM((2, width, hidden_width), low_type),
            pltpu.VMEM((2 * count * rows, width), low_type),
            pltpu.VMEM((2 * count * rows, width), low_type),
            pltpu.VMEM((2 * count * rows, hidden_width), low_type),
            pltpu.VMEM((2 * count * rows, hidden_width), low_type),
            pltpu.SemaphoreType.DMA((2,)),
        ],
        16 * count * rows * width * hidden_width,
        20 * width * hidden_width,
    )(tab, *[member for group in groups for member in group])


def head_gradient(final_every, logit_every):
    width = final_every.shape[1]
    return call(
        head_kernel,
        [vmem] * 2,
        [((width + 1, logit_every.shape[1]), wide_type, vmem)],
        [],
        1 << 28,
        1 << 23,
    )(final_every, logit_every)[0]


def layer_norm(values, gain_row, shift_row):
    centre = values - jnp.mean(values, -1, keepdims=True)
    spread = jnp.mean(centre * centre, -1, keepdims=True)
    return centre * lax.rsqrt(spread + norm_eps) * gain_row + shift_row


def product(form, left, right):
    return jnp.einsum(form, left, right, preferred_element_type=wide_type)


def adamw(weight, moment_one, moment_two, gradient, rate):
    first_new = beta_one * moment_one + (1.0 - beta_one) * gradient
    second_new = beta_two * moment_two + (1.0 - beta_two) * gradient * gradient
    corrected = first_new / (1.0 - beta_one**STEP)
    scaled = second_new / (1.0 - beta_two**STEP)
    weight_new = weight - rate * (corrected / (jnp.sqrt(scaled) + adam_eps) + decay_rate * weight)
    return (weight_new, first_new, second_new)


def on_device(
    patches,
    keep_list,
    keep_count,
    labels,
    patch_weight,
    vector_table,
    head_table,
    joint_weight,
    shift_table,
    output_weight,
    expand_weight,
    raise_table,
    shrink_weight,
    *moments,
):
    share_images = patches.shape[0]
    model_width = vector_table.shape[1]
    data, model = lax.axis_size("dp"), lax.axis_size("mp")
    devices = data * model
    total_images = share_images * devices
    real_rows = share_images * SLOTS
    rows = -(-real_rows // 16) * 16
    z_masks, y_masks, x_masks, c_masks = bit_masks()
    dp_masks = z_masks + y_masks
    all_masks = dp_masks + x_masks + c_masks
    me = device_index()
    model_index = lax.axis_index("mp")
    local_hidden = expand_weight.shape[2]

    every = jnp.array(offsets(all_masks), jnp.int32) ^ me
    every_tab = jnp.stack([every // model, every % model])
    column = jnp.array(offsets(dp_masks), jnp.int32) ^ me
    column_tab = jnp.stack([column // model, jnp.zeros_like(column)])

    patch_full = gather_ordered(patch_weight.astype(low_type), all_masks).reshape(-1, model_width)
    attention_halves, hidden_halves = [], []
    for layer in range(LAYERS):
        pack = jnp.concatenate(
            [joint_weight[layer].transpose(1, 0, 2), output_weight[layer].T[None]], 0
        ).astype(low_type)
        attention_halves.append(gather_halves(pack, all_masks))
        pack = jnp.stack([expand_weight[layer], shrink_weight[layer].T]).astype(low_type)
        hidden_halves.append(gather_halves(pack, dp_masks))

    patch_ids = jnp.arange(PATCHES, dtype=jnp.int32)
    kept_slot = patch_ids[None, :] < keep_count[:, None]
    selector = ((keep_list[:, :, None] == patch_ids[None, None, :]) & kept_slot[:, :, None]).astype(
        wide_type
    )
    selector = jnp.pad(selector, ((0, 0), (1, 0), (0, 0)))
    chosen = product("nsp,npc->nsc", selector.astype(low_type), patches).astype(low_type)
    chosen = jnp.pad(chosen.reshape(real_rows, -1), ((0, rows - real_rows), (0, 0)))
    slot_kept = jnp.pad(kept_slot, ((0, 0), (1, 0))).astype(wide_type)
    slot_first = jnp.zeros((share_images, SLOTS), wide_type).at[:, 0].set(1.0)
    spread = jnp.concatenate(
        [selector, slot_kept[:, :, None], slot_first[:, :, None]], 2
    ).reshape(real_rows, PATCHES + 2)
    spread = jnp.pad(spread, ((0, rows - real_rows), (0, 0)))
    sources = jnp.concatenate(
        [
            vector_table[1:SLOTS],
            vector_table[SLOTS + 1 : SLOTS + 2],
            vector_table[SLOTS : SLOTS + 1] + vector_table[0:1],
        ],
        0,
    )
    stream = product("sc,cd->sd", chosen, patch_full) + jnp.dot(spread, sources, precision=highest)

    row_ids = jnp.arange(rows, dtype=jnp.int32)
    image_ids, slot_ids = row_ids // SLOTS, row_ids % SLOTS
    row_count = jnp.pad(jnp.repeat(keep_count, SLOTS), (0, rows - real_rows), constant_values=SLOTS)
    live = (image_ids[:, None] == image_ids[None, :]) & (slot_ids <= row_count)[None, :]
    bias = jnp.where(live, 0.0, -1e30).astype(wide_type)

    saved = []
    for layer in range(LAYERS):
        base = SLOTS + 4 + 6 * layer
        vec = vector_table[base : base + 6]
        shift = jnp.stack(
            [shift_table[layer, 0], jnp.zeros((model_width,), wide_type), shift_table[layer, 1]]
        )
        raise_row = lax.dynamic_slice_in_dim(
            raise_table[layer], model_index * local_hidden, local_hidden, 0
        )[None]
        middle, second, first, qkv, mixed = attention_forward(
            every_tab, stream, vec, shift, bias, attention_halves[layer]
        )
        pieces = group_pieces(second, x_masks)
        steps = len(pieces) // 2
        partials = [
            hidden_forward(column_tab, pieces[k], pieces[steps + k], raise_row, hidden_halves[layer])
            for k in range(steps)
        ]
        saved.append((stream, middle, first, qkv, mixed, pieces, vec, raise_row))
        stream = middle + group_sum(partials, x_masks) + vec[5:6]

    lead_rows = stream[:real_rows].reshape(share_images, SLOTS, model_width)[:, 0]
    final_out, final_pull = jax.vjp(
        layer_norm, lead_rows, vector_table[SLOTS + 2], vector_table[SLOTS + 3]
    )
    final_low = final_out.astype(low_type)
    head_low = head_table[:model_width].astype(low_type)
    logits = product("nd,dc->nc", final_low, head_low) + head_table[model_width]
    target_hot = (labels[:, None] == jnp.arange(CLASSES, dtype=jnp.int32)[None, :]).astype(
        wide_type
    )
    loss_local = jnp.sum(jax.nn.logsumexp(logits, -1) - jnp.sum(logits * target_hot, -1))
    logit_grad = (jax.nn.softmax(logits, -1) - target_hot) / total_images
    logit_low = logit_grad.astype(low_type)
    final_every = gather_ordered(final_low, all_masks).reshape(-1, model_width)
    logit_every = gather_ordered(logit_grad, all_masks).reshape(-1, CLASSES)
    head_sum = head_gradient(final_every, logit_every)
    final_grad = product("nc,dc->nd", logit_low, head_low)
    lead_grad, gain_final, shift_final = final_pull(final_grad)
    upper = jnp.zeros((share_images, SLOTS, model_width), wide_type).at[:, 0].set(lead_grad)
    upper = jnp.pad(upper.reshape(real_rows, model_width), ((0, rows - real_rows), (0, 0)))
    upper_low = upper.astype(low_type)

    vector_rows, shift_rows, raise_rows = [None] * LAYERS, [None] * LAYERS, [None] * LAYERS
    attention_sums, hidden_sums = [None] * LAYERS, [None] * LAYERS
    for layer in reversed(range(LAYERS)):
        stream_in, middle, first, qkv, mixed, pieces, vec, raise_row = saved[layer]
        downs = group_pieces(upper_low, x_masks)
        steps = len(pieces) // 2
        partials, groups, raise_sum = [], [], 0.0
        for k in range(steps):
            kept, sent, active, grad, raise_part = hidden_chain(
                column_tab,
                pieces[k],
                pieces[steps + k],
                downs[k],
                downs[steps + k],
                raise_row,
                hidden_halves[layer],
            )
            partials.append((kept, sent))
            groups.append((pieces[k], pieces[steps + k], downs[k], downs[steps + k], active, grad))
            raise_sum = raise_sum + raise_part
        hidden_grads = hidden_weights(column_tab, groups, hidden_halves[layer][0].shape)
        hidden_sums[layer] = reduce_halves(*hidden_grads, dp_masks)
        pull = group_sum(partials, x_masks)
        upper, upper_low, up, joined, tail = attention_chain(
            every_tab, upper, pull, middle, stream_in, vec, bias, qkv, attention_halves[layer]
        )
        attention_grads = attention_weights(
            every_tab, first, joined, up, mixed, attention_halves[layer][0].shape
        )
        attention_sums[layer] = reduce_halves(*attention_grads, all_masks)
        vector_rows[layer], shift_rows[layer] = tail[:6], tail[6:]
        raise_rows[layer] = lax.dynamic_update_slice_in_dim(
            jnp.zeros((model, local_hidden), wide_type), raise_sum, model_index, 0
        ).reshape(-1, model_width)

    place = lax.dot_general(
        spread, upper, (((0,), (0,)), ((), ())), precision=highest, preferred_element_type=wide_type
    )
    patch_grad = lax.dot_general(
        chosen, upper_low, (((0,), (0,)), ((), ())), preferred_element_type=wide_type
    ).astype(low_type)
    patch_blocks = patch_grad.reshape(devices, -1, model_width)
    patch_blocks = patch_blocks.at[every].get(mode="promise_in_bounds")
    half = devices // 2
    patch_sum = reduce_halves(patch_blocks[:half], patch_blocks[half:], all_masks)

    small = jnp.concatenate(
        [
            place[PATCHES + 1 :],
            place[:PATCHES],
            place[PATCHES + 1 :],
            place[PATCHES : PATCHES + 1],
            gain_final[None],
            shift_final[None],
        ]
        + vector_rows
        + shift_rows
        + raise_rows
        + [jnp.zeros((1, model_width), wide_type).at[0, 0].set(loss_local)],
        0,
    )
    small = sum_all(small)
    vector_count = vector_table.shape[0]
    vector_sum = small[:vector_count]
    shift_sum = small[vector_count : vector_count + 2 * LAYERS].reshape(shift_table.shape)
    raise_sum = small[vector_count + 2 * LAYERS : -1].reshape(raise_table.shape)
    loss_total = small[-1, 0]
    joint_sum = jnp.stack([total[:3].transpose(1, 0, 2) for total in attention_sums])
    output_sum = jnp.stack([total[3].T for total in attention_sums])
    expand_sum = jnp.stack([total[0] for total in hidden_sums])
    shrink_sum = jnp.stack([total[1].T for total in hidden_sums])

    sharded_sq = jnp.zeros((), wide_type)
    for member in [patch_sum] + attention_sums + hidden_sums:
        sharded_sq = sharded_sq + jnp.sum(member * member)
    shared_sq = jnp.sum(head_sum * head_sum) + jnp.sum(small[:-1] * small[:-1])
    total_sq = sum_all(sharded_sq) + shared_sq
    gradient_norm = jnp.sqrt(total_sq)
    factor = jnp.minimum(1.0, clip_limit / (gradient_norm + norm_eps))
    weights_in = (
        patch_weight,
        vector_table,
        head_table,
        joint_weight,
        shift_table,
        output_weight,
        expand_weight,
        raise_table,
        shrink_weight,
    )
    reduced = (
        patch_sum,
        vector_sum,
        head_sum,
        joint_sum,
        shift_sum,
        output_sum,
        expand_sum,
        raise_sum,
        shrink_sum,
    )
    outputs = [loss_total, gradient_norm]
    for weight, moment_one, moment_two, gradient, rate in zip(
        weights_in, moments[:9], moments[9:], reduced, group_rates
    ):
        outputs.extend(adamw(weight, moment_one, moment_two, gradient * factor, rate))
    return tuple(outputs)


def solution(mesh):
    params = (
        P(("dp", "mp"), None),
        P(),
        P(),
        P(None, "dp", None, "mp"),
        P(),
        P(None, "mp", "dp"),
        P(None, "dp", "mp"),
        P(),
        P(None, "mp", "dp"),
    )
    in_specs = (
        P(("dp", "mp"), None, None),
        P(("dp", "mp"), None),
        P(("dp", "mp")),
        P(("dp", "mp")),
    ) + 3 * params
    out_specs = (P(), P()) + tuple(spec for spec in params for _ in range(3))
    return jax.shard_map(
        on_device, mesh=mesh, in_specs=in_specs, out_specs=out_specs, check_vma=False
    )
```

time: 2230 us -> 1000 us (0.45)
  waiting for transfers between devices: 1540 us -> 454 us
  matrix products: 209 us -> 22.7 us
  Pallas kernels: 0 us -> 181 us
  blocking collectives: 148 us -> 0 us
  starting transfers between devices: 3.19 us -> 83.4 us
  other arithmetic: 145 us -> 105 us
    reduce_scatter x13 -> x0, waiting for transfers between devices: 910 us -> none  [the longest x1 159 us: on_device(): lax.psum_scatter(patch_grad, ('dp', 'mp'), scatter_dimension=0, tiled=True)]
    all_gather x15 -> x0, waiting for transfers between devices: 475 us -> none  [the longest x2 91.9 us: fetch_layers(): lax.all_gather(shrink_part.astype(jnp.bfloat16), 'dp', axis=2, tiled=True)]
    ppermute x0 -> x86, waiting for transfers between devices: none -> 454 us  [swap(): return lax.ppermute(values, AXES, [(n, n ^ mask) for n in range(count)])]
    dot_general x44 -> x7, matrix products: 209 us -> 22.7 us  [the longest x4 13 us: product(): return jnp.einsum(form, left, right, preferred_element_type=wide_type)]
    pallas_call x0 -> x17, Pallas kernels: none -> 181 us  [the longest x2 48.1 us: attention_chain(): call(attention_chain_kernel, [smem] + [vmem] * 7 + [anywhere] * 2, [((row...]
    psum x1 -> x0, waiting for transfers between devices: 149 us -> none  [on_device(): lax.psum((vector_grad, head_grad, stacked[4], stacked[5], loss_local), ('...]
    ppermute x0 -> x86, starting transfers between devices: none -> 83.4 us  [swap(): return lax.ppermute(values, AXES, [(n, n ^ mask) for n in range(count)])]
    psum x2 -> x0, blocking collectives: 80.1 us -> none  [on_device(): lax.psum((vector_grad, head_grad, stacked[4], stacked[5], loss_local), ('...]
  transfers between devices with their start and end apart: 29 -> 86, of which waited for: 29 -> 36; matrix products, arithmetic and copies ran while one was open for 8% -> 18% of each run, Pallas kernels for 0% -> 18%
where the time goes in v2:
time: 1000 us; the launch traced here: 992 us
  waiting for transfers between devices  454 us (45%)
  Pallas kernels  181 us (18%)
  local copies, waits for them, and re-layouts  133 us (13%)
  other arithmetic  105 us (10%)
  starting transfers between devices  83.4 us (8%)
  matrix products  22.7 us (2%)
  between operations  14 us (1%)
    ppermute x86, waiting for transfers between devices, swap(): return lax.ppermute(values, AXES, [(n, n ^ mask) for n in range(count)])  454 us
    ppermute x86, starting transfers between devices, swap(): return lax.ppermute(values, AXES, [(n, n ^ mask) for n in range(count)])  83.4 us
    unnamed x340, local copies, waits for them, and re-layouts  63.5 us
    pallas_call x2, Pallas kernels, attention_chain(): call(attention_chain_kernel, [smem] + [vmem] * 7 + [anywhere] * 2, [((row...  48.1 us
    pallas_call x4, Pallas kernels, hidden_chain(): call(hidden_chain_kernel, [smem] + [vmem] * 5 + [anywhere] * 2, [((rows,...  36.4 us
    pallas_call x2, Pallas kernels, attention_forward(): call(attention_forward_kernel, [smem] + [vmem] * 4 + [anywhere] * 2, [((r...  34.1 us
    sub x9, other arithmetic, adamw(): weight - rate * (corrected / (jnp.sqrt(scaled) + adam_eps) + decay_rate *...  25.1 us
    pallas_call x4, Pallas kernels, hidden_forward(): call(hidden_forward_kernel, [smem] + [vmem] * 3 + [anywhere] * 2, [((rows...  24.3 us
  transfers between devices with their start and end apart: 86, of which 36 were waited for; matrix products, arithmetic and copies ran while one was open for 18% of the time, Pallas kernels for 18%

profile of v2, /device:TPU:0, one launch (start us, length us, event | category | flops | bytes accessed | tf_op | source)
XLA Modules:
  0.0 992.4 jit_solution(17878627908448406260)
XLA Ops:
  24.7 15.7 %collective-permute-done.6 = bf16[2,4,128,256]{3,2,1,0:T(8,128)(2,1)} collective-permute-done((bf16[2,4,128,256]{3,2,1,0:T(8,128)(2,1)}, bf16[2,4,128,256]{3,2,1,0:T(8,128)(2,1)}, u32[]{:S(2)}, u32[]{:S(2)}) %collective-permute-start.6) | collective-permute-done | bytes 524320 | tf_op jit(solution)/shard_map/ppermute | solution.py:32
  50.8 19.9 %collective-permute-done.1 = bf16[2,96,1024]{2,1,0:T(8,128)(2,1)S(1)} collective-permute-done((bf16[2,96,1024]{2,1,0:T(8,128)(2,1)S(1)}, bf16[2,96,1024]{2,1,0:T(8,128)(2,1)S(1)}, u32[]{:S(2)}, u32[]{:S(2)}) %collective-permute-start.1) | collective-permute-done | bytes 393248 | tf_op jit(solution)/shard_map/ppermute | solution.py:32
  106.5 18.5 %collective-permute-done.8 = bf16[8,4,128,256]{3,2,1,0:T(8,128)(2,1)} collective-permute-done((bf16[8,4,128,256]{3,2,1,0:T(8,128)(2,1)}, bf16[8,4,128,256]{3,2,1,0:T(8,128)(2,1)}, u32[]{:S(2)}, u32[]{:S(2)}) %collective-permute-start.8) | collective-permute-done | bytes 2097184 | tf_op jit(solution)/shard_map/ppermute | solution.py:32
  128.1 28.0 %collective-permute-done.3 = bf16[8,96,1024]{2,1,0:T(8,128)(2,1)S(1)} collective-permute-done((bf16[8,96,1024]{2,1,0:T(8,128)(2,1)S(1)}, bf16[8,96,1024]{2,1,0:T(8,128)(2,1)S(1)}, u32[]{:S(2)}, u32[]{:S(2)}) %collective-permute-start.3) | collective-permute-done | bytes 1572896 | tf_op jit(solution)/shard_map/ppermute | solution.py:32
  174.4 14.0 %collective-permute-done.20 = bf16[2,4,128,256]{3,2,1,0:T(8,128)(2,1)S(1)} collective-permute-done((bf16[2,4,128,256]{3,2,1,0:T(8,128)(2,1)}, bf16[2,4,128,256]{3,2,1,0:T(8,128)(2,1)S(1)}, u32[]{:S(2)}, u32[]{:S(2)}) %collective-permute-start.20) | collective-permute-done | bytes 524320 | tf_op jit(solution)/shard_map/ppermute | solution.py:32
  192.5 21.0 %collective-permute-done.21 = bf16[4,4,128,256]{3,2,1,0:T(8,128)(2,1)S(1)} collective-permute-done((bf16[4,4,128,256]{3,2,1,0:T(8,128)(2,1)S(1)}, bf16[4,4,128,256]{3,2,1,0:T(8,128)(2,1)S(1)}, u32[]{:S(2)}, u32[]{:S(2)}) %collective-permute-start.21) | collective-permute-done | bytes 1048608 | tf_op jit(solution)/shard_map/ppermute | solution.py:32
  218.2 22.2 %collective-permute-done.12 = bf16[2,2,128,1024]{3,2,1,0:T(8,128)(2,1)S(1)} collective-permute-done((bf16[2,2,128,1024]{3,2,1,0:T(8,128)(2,1)S(1)}, bf16[2,2,128,1024]{3,2,1,0:T(8,128)(2,1)S(1)}, u32[]{:S(2)}, u32[]{:S(2)}) %collective-permute-start.12) | collective-permute-done | bytes 1048608 | tf_op jit(solution)/shard_map/ppermute | solution.py:32
  260.1 17.3 %shard_map.563 = (f32[304,1024]{1,0:T(8,128)S(1)}, bf16[304,1024]{1,0:T(8,128)(2,1)S(1)}, bf16[304,1024]{1,0:T(8,128)(2,1)S(1)}, bf16[3,304,1024]{2,1,0:T(8,128)(2,1)}, bf16[304,1024]{1,0:T(8,128)(2,1)S(1)}) custom-call(s32[2,32]{1,0:T(2,128)S(1)} %pad_add_fusion.tab_ref, f32[304,1024]{1,0:T(8,128)S(1)} %fusion.4.stream_ref, ...), custom_call_target="tpu_custom_call" | custom-call | flops 6375342080 | bytes 20971520 | tf_op jit(solution)/shard_map/pallas_call | solution.py:397
  311.9 39.8 %collective-permute-done.26 = bf16[2,2,128,1024]{3,2,1,0:T(8,128)(2,1)S(1)} collective-permute-done((bf16[2,2,128,1024]{3,2,1,0:T(8,128)(2,1)S(1)}, bf16[2,2,128,1024]{3,2,1,0:T(8,128)(2,1)S(1)}, u32[]{:S(2)}, u32[]{:S(2)}) %collective-permute-start.26) | collective-permute-done | bytes 1048608 | tf_op jit(solution)/shard_map/ppermute | solution.py:32
  355.0 16.9 %shard_map.566 = (f32[304,1024]{1,0:T(8,128)S(1)}, bf16[304,1024]{1,0:T(8,128)(2,1)S(1)}, bf16[304,1024]{1,0:T(8,128)(2,1)S(1)}, bf16[3,304,1024]{2,1,0:T(8,128)(2,1)}, bf16[304,1024]{1,0:T(8,128)(2,1)S(1)}) custom-call(s32[2,32]{1,0:T(2,128)S(1)} %pad_add_fusion.tab_ref, f32[304,1024]{1,0:T(8,128)S(1)} %add_add_fusion.stream_ref, ...), custom_call_target="tpu_custom_call" | custom-call | flops 6375342080 | bytes 20971520 | tf_op jit(solution)/shard_map/pallas_call | solution.py:397
  374.3 14.2 %collective-permute-done.29.here_ref.refs_6_ = bf16[304,1024]{1,0:T(8,128)(2,1)S(1)} collective-permute-done((bf16[304,1024]{1,0:T(8,128)(2,1)S(1)}, bf16[304,1024]{1,0:T(8,128)(2,1)S(1)}, u32[]{:S(2)}, u32[]{:S(2)}) %collective-permute-start.29) | collective-permute-done | bytes 622624 | tf_op jit(solution)/shard_map/ppermute | solution.py:32
  389.0 11.6 %collective-permute-done.27.half_b = bf16[4,2,128,1024]{3,2,1,0:T(8,128)(2,1)S(1)} collective-permute-done((bf16[4,2,128,1024]{3,2,1,0:T(8,128)(2,1)S(1)}, bf16[4,2,128,1024]{3,2,1,0:T(8,128)(2,1)S(1)}, u32[]{:S(2)}, u32[]{:S(2)}) %collective-permute-start.27) | collective-permute-done | bytes 2097184 | tf_op jit(solution)/shard_map/ppermute | solution.py:32
  415.8 14.5 %collective-permute-done.32 = bf16[304,1024]{1,0:T(8,128)(2,1)S(1)} collective-permute-done((bf16[304,1024]{1,0:T(8,128)(2,1)S(1)}, bf16[304,1024]{1,0:T(8,128)(2,1)S(1)}, u32[]{:S(2)}, u32[]{:S(2)}) %collective-permute-start.32) | collective-permute-done | bytes 622624 | tf_op jit(solution)/shard_map/ppermute | solution.py:32
  447.4 13.6 %collective-permute-done.35.down_here_ref.refs_8_ = bf16[304,1024]{1,0:T(8,128)(2,1)S(1)} collective-permute-done((bf16[304,1024]{1,0:T(8,128)(2,1)S(1)}, bf16[304,1024]{1,0:T(8,128)(2,1)S(1)}, u32[]{:S(2)}, u32[]{:S(2)}) %collective-permute-start.35) | collective-permute-done | bytes 622624 | tf_op jit(solution)/shard_map/ppermute | solution.py:32
  501.5 10.8 %collective-permute-done.38 = bf16[304,1024]{1,0:T(8,128)(2,1)} collective-permute-done((bf16[304,1024]{1,0:T(8,128)(2,1)}, bf16[304,1024]{1,0:T(8,128)(2,1)}, u32[]{:S(2)}, u32[]{:S(2)}) %collective-permute-start.38) | collective-permute-done | bytes 622624 | tf_op jit(solution)/shard_map/ppermute | solution.py:32
  514.6 24.4 %shard_map.571 = (f32[304,1024]{1,0:T(8,128)S(1)}, bf16[304,1024]{1,0:T(8,128)(2,1)}, bf16[304,1024]{1,0:T(8,128)(2,1)S(1)}, bf16[3,304,1024]{2,1,0:T(8,128)(2,1)}, f32[8,1024]{1,0:T(8,128)S(1)}) custom-call(s32[2,32]{1,0:T(2,128)S(1)} %pad_add_fusion.tab_ref, f32[304,1024]{1,0:T(8,128)S(1)} %pad.46.upper_ref, f32[304,1024]{1,0:T(8,128)S(1)} %convert_add_fusion.6.pull_ref, ...), custom_call_target="tpu_custom_call" | custom-call | flops 9563013120 | bytes 31457280 | tf_op jit(solution)/shard_map/pallas_call | solution.py:415
  625.1 23.7 %shard_map.574 = (f32[304,1024]{1,0:T(8,128)S(1)}, bf16[304,1024]{1,0:T(8,128)(2,1)S(1)}, bf16[304,1024]{1,0:T(8,128)(2,1)S(1)}, bf16[3,304,1024]{2,1,0:T(8,128)(2,1)}, f32[8,1024]{1,0:T(8,128)S(1)}) custom-call(s32[2,32]{1,0:T(2,128)S(1)} %pad_add_fusion.tab_ref, f32[304,1024]{1,0:T(8,128)S(1)} %copy-done.64, f32[304,1024]{1,0:T(8,128)S(1)} %convert_add_fusion.5.pull_ref, ...), custom_call_target="tpu_custom_call" | custom-call | flops 9563013120 | bytes 31457280 | tf_op jit(solution)/shard_map/pallas_call | solution.py:415
  707.6 34.5 %collective-permute-done.69 = bf16[2,2,128,1024]{3,2,1,0:T(8,128)(2,1)} collective-permute-done((bf16[2,2,128,1024]{3,2,1,0:T(8,128)(2,1)}, bf16[2,2,128,1024]{3,2,1,0:T(8,128)(2,1)}, u32[]{:S(2)}, u32[]{:S(2)}) %collective-permute-start.69) | collective-permute-done | bytes 1048608 | tf_op jit(solution)/shard_map/ppermute | solution.py:32
  773.6 12.0 %collective-permute-done.48 = f32[79,1024]{1,0:T(8,128)S(1)} collective-permute-done((f32[79,1024]{1,0:T(8,128)S(1)}, f32[79,1024]{1,0:T(8,128)S(1)}, u32[]{:S(2)}, u32[]{:S(2)}) %collective-permute-start.48) | collective-permute-done | bytes 323616 | tf_op jit(solution)/shard_map/ppermute | solution.py:32
  797.0 18.8 %collective-permute-done.49 = f32[79,1024]{1,0:T(8,128)S(1)} collective-permute-done((f32[79,1024]{1,0:T(8,128)S(1)}, f32[79,1024]{1,0:T(8,128)S(1)}, u32[]{:S(2)}, u32[]{:S(2)}) %collective-permute-start.49) | collective-permute-done | bytes 323616 | tf_op jit(solution)/shard_map/ppermute | solution.py:32
  831.4 37.3 %collective-permute-done.56 = bf16[8,4,128,256]{3,2,1,0:T(8,128)(2,1)} collective-permute-done((bf16[8,4,128,256]{3,2,1,0:T(8,128)(2,1)}, bf16[8,4,128,256]{3,2,1,0:T(8,128)(2,1)}, u32[]{:S(2)}, u32[]{:S(2)}) %collective-permute-start.56) | collective-permute-done | bytes 2097184 | tf_op jit(solution)/shard_map/ppermute | solution.py:32
  877.8 17.8 %collective-permute-done.57 = bf16[4,4,128,256]{3,2,1,0:T(8,128)(2,1)S(1)} collective-permute-done((bf16[4,4,128,256]{3,2,1,0:T(8,128)(2,1)S(1)}, bf16[4,4,128,256]{3,2,1,0:T(8,128)(2,1)S(1)}, u32[]{:S(2)}, u32[]{:S(2)}) %collective-permute-start.57) | collective-permute-done | bytes 1048608 | tf_op jit(solution)/shard_map/ppermute | solution.py:32
  899.4 20.1 %collective-permute-done.58 = bf16[2,4,128,256]{3,2,1,0:T(8,128)(2,1)S(1)} collective-permute-done((bf16[2,4,128,256]{3,2,1,0:T(8,128)(2,1)S(1)}, bf16[2,4,128,256]{3,2,1,0:T(8,128)(2,1)S(1)}, u32[]{:S(2)}, u32[]{:S(2)}) %collective-permute-start.58) | collective-permute-done | bytes 524320 | tf_op jit(solution)/shard_map/ppermute | solution.py:32
  971.6 11.4 %multiply_subtract_fusion = (f32[1025,1000]{1,0:T(8,128)}, f32[1025,1000]{1,0:T(8,128)}, f32[1025,1000]{1,0:T(8,128)}) fusion(f32[1025,1000]{1,0:T(8,128)} %param.48, f32[1025,1000]{1,0:T(8,128)} %copy-done.2, f32[]{:T(128)S(6)} %min.3, f32[1025,1000]{1,0:T(8,128)} %param.57, f32[1025,1000]{1,0:T(8,128)} %param.66), kind=kLoop, calls=%fused_computation.11 | loop fusion | flops 16400000 | bytes 28700004 | tf_op jit(solution)/shard_map/sub | solution.py:533
  (701 shorter events, 500.5 us)
Async XLA Ops:
  44.7 146.4 %collective-permute-start.11 = (bf16[1,2,128,1024]{3,2,1,0:T(8,128)(2,1)}, bf16[1,2,128,1024]{3,2,1,0:T(8,128)(2,1)}, u32[]{:S(2)}, u32[]{:S(2)}) collective-permute-start(bf16[1,2,128,1024]{3,2,1,0:T(8,128)(2,1)} %pad_maximum_fusion.11), channel_id=1, source_target_pairs={{0,8},{1,9},{2,10},{3,11},{4,12},{5,13},{6,14},{7,15},{8,0},{9,1},... | collective-permute-start | bytes 1572872 | tf_op jit(solution)/shard_map/ppermute | solution.py:32
  46.2 113.9 %collective-permute-start.19 = (bf16[1,4,128,256]{3,2,1,0:T(8,128)(2,1)}, bf16[1,4,128,256]{3,2,1,0:T(8,128)(2,1)S(1)}, u32[]{:S(2)}, u32[]{:S(2)}) collective-permute-start(bf16[1,4,128,256]{3,2,1,0:T(8,128)(2,1)} %get-tuple-element.312), channel_id=1, source_target_pairs={{0,8},{1,9},{2,10},{3,11},{4,12},{5,13},{6,14},{7,15},{8,0},{9,1},... | collective-permute-start | bytes 786440 | tf_op jit(solution)/shard_map/ppermute | solution.py:32
  76.1 48.9 %collective-permute-start.8 = (bf16[8,4,128,256]{3,2,1,0:T(8,128)(2,1)}, bf16[8,4,128,256]{3,2,1,0:T(8,128)(2,1)}, u32[]{:S(2)}, u32[]{:S(2)}) collective-permute-start(bf16[8,4,128,256]{3,2,1,0:T(8,128)(2,1)} %pad_maximum_fusion), channel_id=1, source_target_pairs={{0,2},{1,3},{2,0},{3,1},{4,6},{5,7},{6,4},{7,5},{8,10},{9,11},{10,... | collective-permute-start | bytes 6291464 | tf_op jit(solution)/shard_map/ppermute | solution.py:32
  92.7 63.4 %collective-permute-start.3 = (bf16[8,96,1024]{2,1,0:T(8,128)(2,1)S(1)}, bf16[8,96,1024]{2,1,0:T(8,128)(2,1)S(1)}, u32[]{:S(2)}, u32[]{:S(2)}) collective-permute-start(bf16[8,96,1024]{2,1,0:T(8,128)(2,1)S(1)} %pad_maximum_fusion.4), channel_id=1, source_target_pairs={{0,2},{1,3},{2,0},{3,1},{4,6},{5,7},{6,4},{7,5},{8,10},{9,11},{10,... | collective-permute-start | bytes 4718600 | tf_op jit(solution)/shard_map/ppermute | solution.py:32
  128.1 132.0 %collective-permute-start.9 = (bf16[16,4,128,256]{3,2,1,0:T(8,128)(2,1)}, bf16[16,4,128,256]{3,2,1,0:T(8,128)(2,1)}, u32[]{:S(2)}, u32[]{:S(2)}) collective-permute-start(bf16[16,4,128,256]{3,2,1,0:T(8,128)(2,1)} %constant_dynamic-update-slice_fusion.11.half_a), channel_id=1, source_target_pairs={{0,1},{1,0},{2,3},{3,2},{4,5},{5,4},{6,7},{7,6},{8,9},{9,8},{10,11... | collective-permute-start | bytes 12582920 | tf_op jit(solution)/shard_map/ppermute | solution.py:32
  158.3 86.2 %collective-permute-start.4 = (bf16[16,96,1024]{2,1,0:T(8,128)(2,1)}, bf16[16,96,1024]{2,1,0:T(8,128)(2,1)}, u32[]{:S(2)}, u32[]{:S(2)}) collective-permute-start(bf16[16,96,1024]{2,1,0:T(8,128)(2,1)} %get-tuple-element.284), channel_id=1, source_target_pairs={{0,1},{1,0},{2,3},{3,2},{4,5},{5,4},{6,7},{7,6},{8,9},{9,8},{10,11... | collective-permute-start | bytes 9437192 | tf_op jit(solution)/shard_map/ppermute | solution.py:32
  192.2 48.1 %collective-permute-start.12 = (bf16[2,2,128,1024]{3,2,1,0:T(8,128)(2,1)S(1)}, bf16[2,2,128,1024]{3,2,1,0:T(8,128)(2,1)S(1)}, u32[]{:S(2)}, u32[]{:S(2)}) collective-permute-start(bf16[2,2,128,1024]{3,2,1,0:T(8,128)(2,1)S(1)} %pad_maximum_fusion.6), channel_id=1, source_target_pairs={{0,16},{1,17},{2,18},{3,19},{4,20},{5,21},{6,22},{7,23},{8,24},{9,... | collective-permute-start | bytes 3145736 | tf_op jit(solution)/shard_map/ppermute | solution.py:32
  215.1 64.7 %collective-permute-start.22 = (bf16[8,4,128,256]{3,2,1,0:T(8,128)(2,1)}, bf16[8,4,128,256]{3,2,1,0:T(8,128)(2,1)}, u32[]{:S(2)}, u32[]{:S(2)}) collective-permute-start(bf16[8,4,128,256]{3,2,1,0:T(8,128)(2,1)} %pad_maximum_fusion.2), channel_id=1, source_target_pairs={{0,2},{1,3},{2,0},{3,1},{4,6},{5,7},{6,4},{7,5},{8,10},{9,11},{10,... | collective-permute-start | bytes 6291464 | tf_op jit(solution)/shard_map/ppermute | solution.py:32
  242.9 51.0 %collective-permute-start.13 = (bf16[4,2,128,1024]{3,2,1,0:T(8,128)(2,1)}, bf16[4,2,128,1024]{3,2,1,0:T(8,128)(2,1)}, u32[]{:S(2)}, u32[]{:S(2)}) collective-permute-start(bf16[4,2,128,1024]{3,2,1,0:T(8,128)(2,1)} %pad_maximum_fusion.1.half_a), channel_id=1, source_target_pairs={{0,4},{1,5},{2,6},{3,7},{4,0},{5,1},{6,2},{7,3},{8,12},{9,13},{10,... | collective-permute-start | bytes 6291464 | tf_op jit(solution)/shard_map/ppermute | solution.py:32
  283.0 72.0 %collective-permute-start.23 = (bf16[16,4,128,256]{3,2,1,0:T(8,128)(2,1)}, bf16[16,4,128,256]{3,2,1,0:T(8,128)(2,1)}, u32[]{:S(2)}, u32[]{:S(2)}) collective-permute-start(bf16[16,4,128,256]{3,2,1,0:T(8,128)(2,1)} %constant_dynamic-update-slice_fusion.16.half_a), channel_id=1, source_target_pairs={{0,1},{1,0},{2,3},{3,2},{4,5},{5,4},{6,7},{7,6},{8,9},{9,8},{10,11... | collective-permute-start | bytes 12582920 | tf_op jit(solution)/shard_map/ppermute | solution.py:32
  303.4 48.3 %collective-permute-start.26 = (bf16[2,2,128,1024]{3,2,1,0:T(8,128)(2,1)S(1)}, bf16[2,2,128,1024]{3,2,1,0:T(8,128)(2,1)S(1)}, u32[]{:S(2)}, u32[]{:S(2)}) collective-permute-start(bf16[2,2,128,1024]{3,2,1,0:T(8,128)(2,1)S(1)} %pad_maximum_fusion.8), channel_id=1, source_target_pairs={{0,16},{1,17},{2,18},{3,19},{4,20},{5,21},{6,22},{7,23},{8,24},{9,... | collective-permute-start | bytes 3145736 | tf_op jit(solution)/shard_map/ppermute | solution.py:32
  483.4 58.2 %collective-permute-start.81 = (f32[1,6,1000]{2,1,0:T(8,128)S(1)}, f32[1,6,1000]{2,1,0:T(8,128)S(1)}, u32[]{:S(2)}, u32[]{:S(2)}) collective-permute-start(f32[1,6,1000]{2,1,0:T(8,128)S(1)} %fusion.70), channel_id=1, source_target_pairs={{0,8},{1,9},{2,10},{3,11},{4,12},{5,13},{6,14},{7,15},{8,0},{9,1},... | collective-permute-start | bytes 72008 | tf_op jit(solution)/shard_map/ppermute | solution.py:32
  568.3 116.2 %collective-permute-start.85 = (f32[16,6,1000]{2,1,0:T(8,128)}, f32[16,6,1000]{2,1,0:T(8,128)}, u32[]{:S(2)}, u32[]{:S(2)}) collective-permute-start(f32[16,6,1000]{2,1,0:T(8,128)} %get-tuple-element.310), channel_id=1, source_target_pairs={{0,1},{1,0},{2,3},{3,2},{4,5},{5,4},{6,7},{7,6},{8,9},{9,8},{10,11... | collective-permute-start | bytes 1152008 | tf_op jit(solution)/shard_map/ppermute | solution.py:32
  610.4 76.7 %collective-permute-start.68 = (bf16[4,2,128,1024]{3,2,1,0:T(8,128)(2,1)}, bf16[4,2,128,1024]{3,2,1,0:T(8,128)(2,1)}, u32[]{:S(2)}, u32[]{:S(2)}) collective-permute-start(bf16[4,2,128,1024]{3,2,1,0:T(8,128)(2,1)} %get-tuple-element.176), channel_id=1, source_target_pairs={{0,4},{1,5},{2,6},{3,7},{4,0},{5,1},{6,2},{7,3},{8,12},{9,13},{10,... | collective-permute-start | bytes 6291464 | tf_op jit(solution)/shard_map/ppermute | solution.py:32
  623.3 77.4 %collective-permute-start.60 = (bf16[16,4,128,256]{3,2,1,0:T(8,128)(2,1)}, bf16[16,4,128,256]{3,2,1,0:T(8,128)(2,1)}, u32[]{:S(2)}, u32[]{:S(2)}) collective-permute-start(bf16[16,4,128,256]{3,2,1,0:T(8,128)(2,1)} %get-tuple-element.164), channel_id=1, source_target_pairs={{0,1},{1,0},{2,3},{3,2},{4,5},{5,4},{6,7},{7,6},{8,9},{9,8},{10,11... | collective-permute-start | bytes 12582920 | tf_op jit(solution)/shard_map/ppermute | solution.py:32
  665.0 91.2 %collective-permute-start.50 = (bf16[16,96,1024]{2,1,0:T(8,128)(2,1)}, bf16[16,96,1024]{2,1,0:T(8,128)(2,1)}, u32[]{:S(2)}, u32[]{:S(2)}) collective-permute-start(bf16[16,96,1024]{2,1,0:T(8,128)(2,1)} %slice.455), channel_id=1, source_target_pairs={{0,1},{1,0},{2,3},{3,2},{4,5},{5,4},{6,7},{7,6},{8,9},{9,8},{10,11... | collective-permute-start | bytes 9437192 | tf_op jit(solution)/shard_map/ppermute | solution.py:32
  673.5 88.1 %collective-permute-start.55 = (bf16[16,4,128,256]{3,2,1,0:T(8,128)(2,1)}, bf16[16,4,128,256]{3,2,1,0:T(8,128)(2,1)}, u32[]{:S(2)}, u32[]{:S(2)}) collective-permute-start(bf16[16,4,128,256]{3,2,1,0:T(8,128)(2,1)} %get-tuple-element.158), channel_id=1, source_target_pairs={{0,1},{1,0},{2,3},{3,2},{4,5},{5,4},{6,7},{7,6},{8,9},{9,8},{10,11... | collective-permute-start | bytes 12582920 | tf_op jit(solution)/shard_map/ppermute | solution.py:32
  684.5 60.2 %collective-permute-start.65 = (bf16[4,2,128,1024]{3,2,1,0:T(8,128)(2,1)}, bf16[4,2,128,1024]{3,2,1,0:T(8,128)(2,1)}, u32[]{:S(2)}, u32[]{:S(2)}) collective-permute-start(bf16[4,2,128,1024]{3,2,1,0:T(8,128)(2,1)} %get-tuple-element.170), channel_id=1, source_target_pairs={{0,4},{1,5},{2,6},{3,7},{4,0},{5,1},{6,2},{7,3},{8,12},{9,13},{10,... | collective-permute-start | bytes 6291464 | tf_op jit(solution)/shard_map/ppermute | solution.py:32
  693.5 48.7 %collective-permute-start.69 = (bf16[2,2,128,1024]{3,2,1,0:T(8,128)(2,1)}, bf16[2,2,128,1024]{3,2,1,0:T(8,128)(2,1)}, u32[]{:S(2)}, u32[]{:S(2)}) collective-permute-start(bf16[2,2,128,1024]{3,2,1,0:T(8,128)(2,1)} %slice.588), channel_id=1, source_target_pairs={{0,16},{1,17},{2,18},{3,19},{4,20},{5,21},{6,22},{7,23},{8,24},{9,... | collective-permute-start | bytes 3145736 | tf_op jit(solution)/shard_map/ppermute | solution.py:32
  742.2 48.8 %collective-permute-start.61 = (bf16[8,4,128,256]{3,2,1,0:T(8,128)(2,1)}, bf16[8,4,128,256]{3,2,1,0:T(8,128)(2,1)}, u32[]{:S(2)}, u32[]{:S(2)}) collective-permute-start(bf16[8,4,128,256]{3,2,1,0:T(8,128)(2,1)} %slice.585), channel_id=1, source_target_pairs={{0,2},{1,3},{2,0},{3,1},{4,6},{5,7},{6,4},{7,5},{8,10},{9,11},{10,... | collective-permute-start | bytes 6291464 | tf_op jit(solution)/shard_map/ppermute | solution.py:32
  754.1 64.2 %collective-permute-start.66 = (bf16[2,2,128,1024]{3,2,1,0:T(8,128)(2,1)}, bf16[2,2,128,1024]{3,2,1,0:T(8,128)(2,1)S(1)}, u32[]{:S(2)}, u32[]{:S(2)}) collective-permute-start(bf16[2,2,128,1024]{3,2,1,0:T(8,128)(2,1)} %slice.589), channel_id=1, source_target_pairs={{0,16},{1,17},{2,18},{3,19},{4,20},{5,21},{6,22},{7,23},{8,24},{9,... | collective-permute-start | bytes 3145736 | tf_op jit(solution)/shard_map/ppermute | solution.py:32
  761.6 63.1 %collective-permute-start.51 = (bf16[8,96,1024]{2,1,0:T(8,128)(2,1)}, bf16[8,96,1024]{2,1,0:T(8,128)(2,1)}, u32[]{:S(2)}, u32[]{:S(2)}) collective-permute-start(bf16[8,96,1024]{2,1,0:T(8,128)(2,1)} %slice.587), channel_id=1, source_target_pairs={{0,2},{1,3},{2,0},{3,1},{4,6},{5,7},{6,4},{7,5},{8,10},{9,11},{10,... | collective-permute-start | bytes 4718600 | tf_op jit(solution)/shard_map/ppermute | solution.py:32
  770.0 98.7 %collective-permute-start.56 = (bf16[8,4,128,256]{3,2,1,0:T(8,128)(2,1)}, bf16[8,4,128,256]{3,2,1,0:T(8,128)(2,1)}, u32[]{:S(2)}, u32[]{:S(2)}) collective-permute-start(bf16[8,4,128,256]{3,2,1,0:T(8,128)(2,1)} %slice.586), channel_id=1, source_target_pairs={{0,2},{1,3},{2,0},{3,1},{4,6},{5,7},{6,4},{7,5},{8,10},{9,11},{10,... | collective-permute-start | bytes 6291464 | tf_op jit(solution)/shard_map/ppermute | solution.py:32
  820.3 52.5 %collective-permute-start.67 = (bf16[1,2,128,1024]{3,2,1,0:T(8,128)(2,1)S(1)}, bf16[1,2,128,1024]{3,2,1,0:T(8,128)(2,1)S(1)}, u32[]{:S(2)}, u32[]{:S(2)}) collective-permute-start(bf16[1,2,128,1024]{3,2,1,0:T(8,128)(2,1)S(1)} %slice.594), channel_id=1, source_target_pairs={{0,8},{1,9},{2,10},{3,11},{4,12},{5,13},{6,14},{7,15},{8,0},{9,1},... | collective-permute-start | bytes 1572872 | tf_op jit(solution)/shard_map/ppermute | solution.py:32
  (218 other events, 3399.4 us)

commit v3 on v2

--- a/solution.py
+++ b/solution.py
@@ -27,21 +27,34 @@
 wide_type = jnp.float32
 
 
+def move(values, pairs):
+    return lax.ppermute(values, AXES, pairs)
+
+
+def across(mask):
+    return [(n, n ^ mask) for n in range(lax.axis_size("dp") * lax.axis_size("mp"))]
+
+
 def swap(values, mask):
-    count = lax.axis_size("dp") * lax.axis_size("mp")
-    return lax.ppermute(values, AXES, [(n, n ^ mask) for n in range(count)])
+    return move(values, across(mask))
 
 
 def device_index():
     return lax.axis_index("dp") * lax.axis_size("mp") + lax.axis_index("mp")
 
 
-def bit_masks():
+def sizes():
     model, data = lax.axis_size("mp"), lax.axis_size("dp")
     wide = 1 << ((data.bit_length() - 1) // 2)
-    z_masks = [m for m in (model * wide << b for b in range(16)) if m < model * data]
-    y_masks = [m for m in (model << b for b in range(16)) if m < model * wide]
-    x_masks = [m for m in (2 << b for b in range(16)) if m < model]
+    return data // wide, wide, model // 2, wide * model
+
+
+def bit_masks():
+    deep, wide, across_x, stride = sizes()
+    model = lax.axis_size("mp")
+    z_masks = [stride << b for b in range(deep.bit_length() - 1)]
+    y_masks = [model << b for b in range(wide.bit_length() - 1)]
+    x_masks = [2 << b for b in range(across_x.bit_length() - 1)]
     return (z_masks, y_masks, x_masks, [1])
 
 
@@ -52,29 +65,147 @@
     return table
 
 
-def gather_halves(values, masks):
+def origins(masks):
+    deep, wide, across_x, stride = sizes()
+    me = device_index()
+    places = [(flip, t) for flip in offsets(masks) for t in range(deep)]
+    flips = jnp.array([flip for flip, t in places], jnp.int32)
+    turns = jnp.array([t for flip, t in places], jnp.int32)
+    return (me // stride + turns) % deep * stride + ((me % stride) ^ flips)
+
+
+def along_z(shift, first, last):
+    deep, wide, across_x, stride = sizes()
+    return [
+        (z * stride + n, (z + shift) * stride + n) for z in range(first, last + 1) for n in range(stride)
+    ]
+
+
+def gather_z(values):
+    deep, wide, across_x, stride = sizes()
+    z = device_index() // stride
+    up, down, ups, downs = values, values, [], []
+    for k in range(1, deep):
+        up, down = yield [
+            (up, along_z(1, k - 1, deep - 2)),
+            (down, along_z(-1, 1, deep - k)),
+        ]
+        ups.append(up)
+        downs.append(down)
+    return jnp.stack(
+        [values] + [jnp.where(z + t < deep, downs[t - 1], ups[deep - t - 1]) for t in range(1, deep)]
+    )
+
+
+def gather_flips(blocks, masks):
+    for mask in masks[:-1]:
+        (arrived,) = yield [(blocks, across(mask))]
+        blocks = jnp.concatenate([blocks, arrived], 0)
+    (arrived,) = yield [(blocks, across(masks[-1]))]
+    return blocks, arrived
+
+
+def gather_quarters(blocks, masks):
+    for mask in masks[:-2]:
+        (arrived,) = yield [(blocks, across(mask))]
+        blocks = jnp.concatenate([blocks, arrived], 0)
+    arrived, beside = yield [(blocks, across(masks[-2])), (blocks, across(masks[-1]))]
+    (last,) = yield [(arrived, across(masks[-1]))]
+    return blocks, arrived, beside, last
+
+
+def gather_all(values, masks):
+    blocks = yield from gather_z(values)
+    return (yield from gather_flips(blocks, masks))
+
+
+def reduce_quarters(parts, masks):
+    kept, sent, kept_beside, sent_beside = parts
+    beside, last = yield [(kept_beside, across(masks[-1])), (sent_beside, across(masks[-1]))]
+    sent = (sent.astype(wide_type) + last.astype(wide_type)).astype(low_type)
+    (arrived,) = yield [(sent, across(masks[-2]))]
+    terms = [kept, beside, arrived]
+    for mask in reversed(masks[:-2]):
+        half = terms[0].shape[0] // 2
+        sent = sum(term[half:].astype(wide_type) for term in terms).astype(low_type)
+        kept = sum(term[:half].astype(wide_type) for term in terms)
+        (arrived,) = yield [(sent, across(mask))]
+        terms = [kept, arrived]
+    return sum(term.astype(wide_type) for term in terms)
+
+
+def reduce_z(blocks):
+    deep = blocks.shape[0]
+    up = down = None
+    for k in range(deep - 1, 0, -1):
+        rising, falling = blocks[k], blocks[deep - k]
+        if up is not None:
+            rising, falling = rising + up.astype(wide_type), falling + down.astype(wide_type)
+        up, down = yield [
+            (rising.astype(low_type), along_z(1, 0, deep - 1 - k)),
+            (falling.astype(low_type), along_z(-1, k, deep - 1)),
+        ]
+    return blocks[0] + up.astype(wide_type) + down.astype(wide_type)
+
+
+def reduce_all(parts, masks):
+    blocks = yield from reduce_quarters(parts, masks)
+    return (yield from reduce_z(blocks))
+
+
+class Transfer:
+    def __init__(self, steps):
+        self.steps = steps
+        self.wanted = next(steps)
+        self.result = None
+
+    def send(self):
+        return [move(*item) for item in self.wanted]
+
+    def receive(self, arrived):
+        try:
+            self.wanted = self.steps.send(arrived)
+        except StopIteration as end:
+            self.wanted, self.result = None, end.value
+
+    def finish(self):
+        while self.wanted is not None:
+            self.receive(self.send())
+        return self.result
+
+
+def advance(transfers, others=()):
+    moving = [t for t in transfers if t.wanted is not None]
+    arrived, others = lax.optimization_barrier(([t.send() for t in moving], others))
+    for transfer, values in zip(moving, arrived):
+        transfer.receive(values)
+    return others
+
+
+def gather_ordered(values):
+    z_masks, y_masks, x_masks, c_masks = bit_masks()
+    masks = z_masks + y_masks + x_masks + c_masks
     blocks = values[None]
-    for mask in masks[:-1]:
+    for mask in masks:
         blocks = jnp.concatenate([blocks, swap(blocks, mask)], 0)
-    return blocks, swap(blocks, masks[-1])
-
-
-def gather_ordered(values, masks):
-    blocks = jnp.concatenate(gather_halves(values, masks), 0)
-    inverse = [0] * len(offsets(masks))
+    inverse = [0] * blocks.shape[0]
     for place, entry in enumerate(offsets(masks)):
         inverse[entry] = place
     places = jnp.array(inverse, jnp.int32)
     order = places.at[jnp.arange(len(inverse)) ^ device_index()].get(mode="promise_in_bounds")
-    return blocks.at[order].get(mode="promise_in_bounds")
-
-
-def reduce_halves(kept, sent, masks):
-    total = kept.astype(wide_type) + swap(sent, masks[-1]).astype(wide_type)
-    for mask in reversed(masks[:-1]):
-        half = total.shape[0] // 2
-        total = total[:half] + swap(total[half:].astype(low_type), mask).astype(wide_type)
-    return total[0]
+    return blocks.at[order].get(mode="promise_in_bounds").reshape((-1,) + values.shape[1:])
+
+
+def together(*values):
+    return lax.optimization_barrier(values)
+
+
+def sum_steps(values):
+    for masks in bit_masks():
+        for mask in masks:
+            (arrived,) = yield [(values, across(mask))]
+            values = values + arrived
+    return values
 
 
 def sum_all(values):
@@ -84,11 +215,11 @@
     return values
 
 
-def group_pieces(values, x_masks):
+def near_far(values, x_masks):
     pieces = [values]
     for mask in x_masks:
         pieces = pieces + [swap(piece, mask) for piece in pieces]
-    return pieces + [swap(piece, 1) for piece in pieces]
+    return pieces
 
 
 def group_sum(partials, x_masks):
@@ -131,7 +262,9 @@
 
 
 def start_weights(tab_ref, halves, w_ref, sems):
-    count, width, rows, columns = halves[0].shape
+    count, rows, columns = halves[0].shape
+    width = w_ref.shape[0]
+    columns = columns // width
     for side, half in enumerate(halves):
 
         def step(r, carry):
@@ -139,7 +272,7 @@
             column = pl.multiple_of(tab_ref[1, side * count + r] * columns, columns)
             for k in range(width):
                 pltpu.make_async_copy(
-                    half.at[r, k],
+                    half.at[r, :, pl.ds(k * columns, columns)],
                     w_ref.at[k, pl.ds(row, rows), pl.ds(column, columns)],
                     sems.at[k],
                 ).start()
@@ -153,14 +286,17 @@
 
 
 def store_grads(tab_ref, g_ref, halves, sem, k):
-    count, width, rows, columns = halves[0].shape
+    count, rows, columns = halves[0].shape
+    columns = columns // g_ref.shape[0]
     for side, half in enumerate(halves):
 
         def step(r, carry):
             row = pl.multiple_of(tab_ref[0, side * count + r] * rows, rows)
             column = pl.multiple_of(tab_ref[1, side * count + r] * columns, columns)
             pltpu.make_async_copy(
-                g_ref.at[k, pl.ds(row, rows), pl.ds(column, columns)], half.at[r, k], sem.at[k]
+                g_ref.at[k, pl.ds(row, rows), pl.ds(column, columns)],
+                half.at[r, :, pl.ds(k * columns, columns)],
+                sem.at[k],
             ).start()
             return carry
 
@@ -178,11 +314,9 @@
     return powers / jnp.sum(powers, -1, keepdims=True)
 
 
-def attention_forward_kernel(
-    tab_ref, stream_ref, vec_ref, shift_ref, bias_ref, half_a, half_b,
-    middle_ref, second_ref, first_ref, qkv_ref, mixed_ref, w_ref, sems,
-):
-    start_weights(tab_ref, (half_a, half_b), w_ref, sems)
+def attention_forward_kernel(count, tab_ref, stream_ref, vec_ref, shift_ref, bias_ref, *refs):
+    middle_ref, second_ref, first_ref, qkv_ref, mixed_ref, w_ref, sems = refs[count:]
+    start_weights(tab_ref, refs[:count], w_ref, sems)
     width = stream_ref.shape[1]
     hat, scale = normalise(stream_ref[...])
     first_ref[...] = (hat * vec_ref[0:1, :] + vec_ref[1:2, :]).astype(low_type)
@@ -216,10 +350,11 @@
 
 
 def attention_chain_kernel(
-    tab_ref, upper_ref, pull_ref, middle_ref, stream_ref, vec_ref, bias_ref, qkv_ref, half_a, half_b,
-    below_ref, below_low_ref, up_ref, joined_ref, rows_ref, w_ref, sems, mixed_grad_ref, mid_grad_ref, norm_grad_ref,
+    count, tab_ref, upper_ref, pull_ref, middle_ref, stream_ref, vec_ref, bias_ref, qkv_ref, *refs
 ):
-    start_weights(tab_ref, (half_a, half_b), w_ref, sems)
+    below_ref, below_low_ref, up_ref, joined_ref, rows_ref, w_ref, sems = refs[count : count + 7]
+    mixed_grad_ref, mid_grad_ref, norm_grad_ref = refs[count + 7 :]
+    start_weights(tab_ref, refs[:count], w_ref, sems)
     width = stream_ref.shape[1]
     upper = upper_ref[...]
     rows_ref[5:6, :] = jnp.sum(upper, 0, keepdims=True)
@@ -276,9 +411,8 @@
     below_low_ref[...] = below.astype(low_type)
 
 
-def attention_weights_kernel(
-    tab_ref, first_ref, joined_ref, up_ref, mixed_ref, half_a, half_b, g_ref, sems
-):
+def attention_weights_kernel(tab_ref, first_ref, joined_ref, up_ref, mixed_ref, *refs):
+    g_ref, sems = refs[-2:]
     width = first_ref.shape[1]
     for k in range(4):
         for c in range(0, width, 256):
@@ -287,19 +421,74 @@
             else:
                 part = dot_tn(up_ref[...], mixed_ref[:, c : c + 256])
             g_ref[k, :, c : c + 256] = part.astype(low_type)
-        store_grads(tab_ref, g_ref, (half_a, half_b), sems, k)
+        store_grads(tab_ref, g_ref, refs[:-2], sems, k)
     for k in range(4):
         wait_weights(g_ref, sems, k)
 
 
+def pack_kernel(joint_ref, output_ref, expand_ref, shrink_ref, attention_ref, hidden_ref):
+    cut, local_hidden = joint_ref.shape[3], expand_ref.shape[2]
+    for layer in range(LAYERS):
+        for k in range(3):
+            attention_ref[layer, :, k * cut : (k + 1) * cut] = joint_ref[layer, k].astype(low_type)
+        attention_ref[layer, :, 3 * cut :] = output_ref[layer].T.astype(low_type)
+        hidden_ref[layer, :, :local_hidden] = expand_ref[layer].astype(low_type)
+        hidden_ref[layer, :, local_hidden:] = shrink_ref[layer].T.astype(low_type)
+
+
+def unpack_kernel(attention_ref, hidden_ref, joint_ref, output_ref, expand_ref, shrink_ref, square_ref):
+    cut, local_hidden = joint_ref.shape[3], expand_ref.shape[2]
+    total = jnp.zeros((1, 1), wide_type)
+    for layer in range(LAYERS):
+        for k in range(3):
+            joint_ref[layer, k] = attention_ref[layer, :, k * cut : (k + 1) * cut]
+        output_ref[layer] = attention_ref[layer, :, 3 * cut :].T
+        expand_ref[layer] = hidden_ref[layer, :, :local_hidden]
+        shrink_ref[layer] = hidden_ref[layer, :, local_hidden:].T
+        for source in (attention_ref, hidden_ref):
+            total = total + jnp.sum(source[layer] * source[layer], keepdims=True)
+    square_ref[...] = total
+
+
+def embed_kernel(tab_ref, chosen_ref, base_ref, *refs):
+    out_ref, w_ref, sem = refs[-3:]
+    count, rows, width = refs[0].shape
+    for side, half in enumerate(refs[:-3]):
+
+        def step(r, carry):
+            row = pl.multiple_of(tab_ref[side * count + r] * rows, rows)
+            pltpu.make_async_copy(half.at[r], w_ref.at[pl.ds(row, rows)], sem).start()
+            return carry
+
+        lax.fori_loop(0, count, step, 0)
+    pltpu.make_async_copy(w_ref, w_ref, sem).wait()
+    for c in range(0, width, 256):
+        out_ref[:, c : c + 256] = base_ref[:, c : c + 256] + dot_nn(chosen_ref[...], w_ref[:, c : c + 256])
+
+
+def embed_weights_kernel(tab_ref, chosen_ref, upper_ref, *refs):
+    g_ref, sem = refs[-2:]
+    count, rows, width = refs[0].shape
+    for c in range(0, width, 256):
+        g_ref[:, c : c + 256] = dot_tn(chosen_ref[...], upper_ref[:, c : c + 256]).astype(low_type)
+    for side, half in enumerate(refs[:-2]):
+
+        def step(r, carry):
+            row = pl.multiple_of(tab_ref[side * count + r] * rows, rows)
+            pltpu.make_async_copy(g_ref.at[pl.ds(row, rows)], half.at[r], sem).start()
+            return carry
+
+        lax.fori_loop(0, count, step, 0)
+    pltpu.make_async_copy(g_ref, g_ref, sem).wait()
+
+
 gelu_scale = 0.7978845608028654
 gelu_cube = 0.044715
 
 
-def hidden_forward_kernel(
-    tab_ref, here_ref, there_ref, raise_ref, half_a, half_b, kept_ref, sent_ref, w_ref, active_ref, sems
-):
-    start_weights(tab_ref, (half_a, half_b), w_ref, sems)
+def hidden_forward_kernel(count, tab_ref, here_ref, there_ref, raise_ref, *refs):
+    kept_ref, sent_ref, w_ref, active_ref, sems = refs[count:]
+    start_weights(tab_ref, refs[:count], w_ref, sems)
     rows, width = here_ref.shape
     hidden_width = active_ref.shape[1]
     wait_weights(w_ref, sems, 0)
@@ -317,10 +506,10 @@
 
 
 def hidden_chain_kernel(
-    tab_ref, here_ref, there_ref, down_here_ref, down_there_ref, raise_ref, half_a, half_b,
-    kept_ref, sent_ref, active_ref, grad_ref, raise_grad_ref, w_ref, sems,
+    count, tab_ref, here_ref, there_ref, down_here_ref, down_there_ref, raise_ref, *refs
 ):
-    start_weights(tab_ref, (half_a, half_b), w_ref, sems)
+    kept_ref, sent_ref, active_ref, grad_ref, raise_grad_ref, w_ref, sems = refs[count:]
+    start_weights(tab_ref, refs[:count], w_ref, sems)
     rows, width = here_ref.shape
     hidden_width = active_ref.shape[1]
     wait_weights(w_ref, sems, 0)
@@ -349,7 +538,7 @@
 
 def hidden_weights_kernel(count, tab_ref, *refs):
     groups = [refs[6 * g : 6 * g + 6] for g in range(count)]
-    half_a, half_b, g_ref, inputs_ref, down_ref, active_ref, grad_ref, sems = refs[6 * count :]
+    out_ref, g_ref, inputs_ref, down_ref, active_ref, grad_ref, sems = refs[6 * count :]
     rows, width = groups[0][0].shape
     hidden_width = active_ref.shape[1]
     for g, (here, there, down_here, down_there, active, grad) in enumerate(groups):
@@ -363,7 +552,7 @@
     for k, (left, right) in enumerate(((inputs_ref, grad_ref), (down_ref, active_ref))):
         for c in range(0, hidden_width, 256):
             g_ref[k, :, c : c + 256] = dot_tn(left[...], right[:, c : c + 256]).astype(low_type)
-        store_grads(tab_ref, g_ref, (half_a, half_b), sems, k)
+        store_grads(tab_ref, g_ref, (out_ref,), sems, k)
     for k in range(2):
         wait_weights(g_ref, sems, k)
 
@@ -392,11 +581,48 @@
     )
 
 
-def attention_forward(tab, stream, vec, shift, bias, halves):
+def embed(places, chosen, base, halves):
+    count, rows, width = halves[0].shape
+    depth = chosen.shape[1]
+    if rows % 16:
+        order = jnp.zeros_like(places).at[places].set(jnp.arange(places.shape[0], dtype=jnp.int32))
+        full = jnp.concatenate(halves, 0)[order].reshape(depth, width)
+        return base + jnp.dot(chosen, full, preferred_element_type=wide_type)
+    return call(
+        embed_kernel,
+        [smem] + [vmem] * 2 + [anywhere] * len(halves),
+        [(base.shape, wide_type, vmem)],
+        [pltpu.VMEM((depth, width), low_type), pltpu.SemaphoreType.DMA],
+        2 * chosen.shape[0] * depth * width,
+        4 * depth * width,
+    )(places, chosen, base, *halves)[0]
+
+
+def embed_weights(places, chosen, upper, half_shape):
+    count, rows, width = half_shape
+    depth = chosen.shape[1]
+    if rows % 16:
+        full = lax.dot_general(
+            chosen, upper, (((0,), (0,)), ((), ())), preferred_element_type=wide_type
+        )
+        blocks = full.astype(low_type).reshape(-1, rows, width)[places]
+        return tuple(blocks[k * count : (k + 1) * count] for k in range(4))
+    return call(
+        embed_weights_kernel,
+        [smem] + [vmem] * 2,
+        [(half_shape, low_type, anywhere)] * 4,
+        [pltpu.VMEM((depth, width), low_type), pltpu.SemaphoreType.DMA],
+        2 * chosen.shape[0] * depth * width,
+        4 * depth * width,
+    )(places, chosen, upper)
+
+
+def attention_forward(stream, vec, shift, bias, gathered):
+    tab, *halves = gathered
     rows, width = stream.shape
     return call(
-        attention_forward_kernel,
-        [smem] + [vmem] * 4 + [anywhere] * 2,
+        functools.partial(attention_forward_kernel, len(halves)),
+        [smem] + [vmem] * 4 + [anywhere] * len(halves),
         [
             ((rows, width), wide_type, vmem),
             ((rows, width), low_type, vmem),
@@ -410,11 +636,12 @@
     )(tab, stream, vec, shift, bias, *halves)
 
 
-def attention_chain(tab, upper, pull, middle, stream, vec, bias, qkv, halves):
+def attention_chain(upper, pull, middle, stream, vec, bias, qkv, gathered):
+    tab, *halves = gathered
     rows, width = stream.shape
     return call(
-        attention_chain_kernel,
-        [smem] + [vmem] * 7 + [anywhere] * 2,
+        functools.partial(attention_chain_kernel, len(halves)),
+        [smem] + [vmem] * 7 + [anywhere] * len(halves),
         [
             ((rows, width), wide_type, vmem),
             ((rows, width), low_type, vmem),
@@ -439,19 +666,20 @@
     return call(
         attention_weights_kernel,
         [smem] + [vmem] * 4,
-        [(half_shape, low_type, anywhere)] * 2,
+        [(half_shape, low_type, anywhere)] * 4,
         [pltpu.VMEM((4, width, width), low_type), pltpu.SemaphoreType.DMA((4,))],
         16 * rows * width * width,
         16 * width * width,
     )(tab, first, joined, up, mixed)
 
 
-def hidden_forward(tab, here, there, raise_row, halves):
+def hidden_forward(here, there, raise_row, gathered):
+    tab, *halves = gathered
     rows, width = here.shape
     hidden_width = raise_row.shape[1]
     return call(
-        hidden_forward_kernel,
-        [smem] + [vmem] * 3 + [anywhere] * 2,
+        functools.partial(hidden_forward_kernel, len(halves)),
+        [smem] + [vmem] * 3 + [anywhere] * len(halves),
         [((rows, width), wide_type, vmem), ((rows, width), low_type, vmem)],
         [
             pltpu.VMEM((2, width, hidden_width), low_type),
@@ -463,12 +691,13 @@
     )(tab, here, there, raise_row, *halves)
 
 
-def hidden_chain(tab, here, there, down_here, down_there, raise_row, halves):
+def hidden_chain(here, there, down_here, down_there, raise_row, gathered):
+    tab, *halves = gathered
     rows, width = here.shape
     hidden_width = raise_row.shape[1]
     return call(
-        hidden_chain_kernel,
-        [smem] + [vmem] * 5 + [anywhere] * 2,
+        functools.partial(hidden_chain_kernel, len(halves)),
+        [smem] + [vmem] * 5 + [anywhere] * len(halves),
         [
             ((rows, width), wide_type, vmem),
             ((rows, width), low_type, vmem),
@@ -482,14 +711,14 @@
     )(tab, here, there, down_here, down_there, raise_row, *halves)
 
 
-def hidden_weights(tab, groups, half_shape):
+def hidden_weights(tab, groups, out_shape):
     rows, width = groups[0][0].shape
     hidden_width = groups[0][4].shape[1]
     count = len(groups)
     return call(
         functools.partial(hidden_weights_kernel, count),
         [smem] + [vmem] * (6 * count),
-        [(half_shape, low_type, anywhere)] * 2,
+        [(out_shape, low_type, anywhere)],
         [
             pltpu.VMEM((2, width, hidden_width), low_type),
             pltpu.VMEM((2 * count * rows, width), low_type),
@@ -500,7 +729,39 @@
         ],
         16 * count * rows * width * hidden_width,
         20 * width * hidden_width,
-    )(tab, *[member for group in groups for member in group])
+    )(tab, *[member for group in groups for member in group])[0]
+
+
+def pack_weights(joint, output, expand, shrink):
+    rows, cut, local_hidden = joint.shape[2], joint.shape[3], expand.shape[2]
+    return call(
+        pack_kernel,
+        [vmem] * 4,
+        [
+            ((LAYERS, rows, 4 * cut), low_type, vmem),
+            ((LAYERS, rows, 2 * local_hidden), low_type, vmem),
+        ],
+        [],
+        1 << 20,
+        1 << 22,
+    )(joint, output, expand, shrink)
+
+
+def unpack_grads(attention, hidden, rows, cut, local_hidden):
+    return call(
+        unpack_kernel,
+        [vmem] * 2,
+        [
+            ((LAYERS, 3, rows, cut), wide_type, vmem),
+            ((LAYERS, cut, rows), wide_type, vmem),
+            ((LAYERS, rows, local_hidden), wide_type, vmem),
+            ((LAYERS, local_hidden, rows), wide_type, vmem),
+            ((1, 1), wide_type, vmem),
+        ],
+        [],
+        1 << 20,
+        1 << 22,
+    )(attention, hidden)
 
 
 def head_gradient(final_every, logit_every):
@@ -558,26 +819,51 @@
     real_rows = share_images * SLOTS
     rows = -(-real_rows // 16) * 16
     z_masks, y_masks, x_masks, c_masks = bit_masks()
-    dp_masks = z_masks + y_masks
-    all_masks = dp_masks + x_masks + c_masks
     me = device_index()
     model_index = lax.axis_index("mp")
     local_hidden = expand_weight.shape[2]
 
-    every = jnp.array(offsets(all_masks), jnp.int32) ^ me
-    every_tab = jnp.stack([every // model, every % model])
-    column = jnp.array(offsets(dp_masks), jnp.int32) ^ me
-    column_tab = jnp.stack([column // model, jnp.zeros_like(column)])
-
-    patch_full = gather_ordered(patch_weight.astype(low_type), all_masks).reshape(-1, model_width)
-    attention_halves, hidden_halves = [], []
-    for layer in range(LAYERS):
-        pack = jnp.concatenate(
-            [joint_weight[layer].transpose(1, 0, 2), output_weight[layer].T[None]], 0
-        ).astype(low_type)
-        attention_halves.append(gather_halves(pack, all_masks))
-        pack = jnp.stack([expand_weight[layer], shrink_weight[layer].T]).astype(low_type)
-        hidden_halves.append(gather_halves(pack, dp_masks))
+    def column_of(devices_at):
+        return devices_at // model
+
+    def table(devices_at):
+        return jnp.stack([devices_at // model, devices_at % model])
+
+    flip_masks = y_masks + x_masks + c_masks
+    turned_masks = x_masks + y_masks + c_masks
+    every, turned = origins(flip_masks), origins(turned_masks)
+    every_tab, turned_tab, direct_tab = table(every), table(turned), table(jnp.arange(devices, dtype=jnp.int32))
+    column = jnp.arange(data, dtype=jnp.int32)
+    column_tab = jnp.stack([column, jnp.zeros_like(column)])
+
+    attention_packs, hidden_packs = pack_weights(
+        joint_weight.transpose(0, 2, 1, 3), output_weight, expand_weight, shrink_weight
+    )
+    pack_rows, pack_width = attention_packs.shape[1:]
+    first_pack = jnp.concatenate(
+        [attention_packs[0], patch_weight.astype(low_type).reshape(-1, pack_width)], 0
+    )
+    first_move = Transfer(gather_z(first_pack))
+    while first_move.wanted is not None:
+        hidden_packs, attention_packs = advance([first_move], (hidden_packs, attention_packs))
+    hidden_halves = [(column_tab, lax.all_gather(hidden_packs[0], "dp"))]
+    attention_later = [
+        (direct_tab, lax.all_gather(attention_packs[layer], AXES)) for layer in range(1, LAYERS)
+    ]
+    attention_blocks = first_move.result[:, :pack_rows]
+    patch_blocks = first_move.result[:, pack_rows:].reshape(-1, *patch_weight.shape)
+    attention_blocks, patch_blocks, later_packs = together(
+        attention_blocks, patch_blocks, hidden_packs
+    )
+    attention_move = Transfer(gather_quarters(attention_blocks, flip_masks))
+    patch_move = Transfer(gather_quarters(patch_blocks, turned_masks))
+    later_moves = [Transfer(gather_all(later_packs[layer], y_masks)) for layer in range(1, LAYERS)]
+    for step in range(len(flip_masks) - 2):
+        advance([patch_move, attention_move])
+    advance([patch_move, attention_move] + later_moves)
+    patch_halves, attention_first = patch_move.finish(), attention_move.finish()
+    attention_halves = [(every_tab,) + attention_first] + attention_later
+    halves_tab = jnp.stack([column_of(origins(y_masks)), jnp.zeros_like(column)])
 
     patch_ids = jnp.arange(PATCHES, dtype=jnp.int32)
     kept_slot = patch_ids[None, :] < keep_count[:, None]
@@ -601,7 +887,8 @@
         ],
         0,
     )
-    stream = product("sc,cd->sd", chosen, patch_full) + jnp.dot(spread, sources, precision=highest)
+    base = jnp.dot(spread, sources, precision=highest)
+    stream = embed(turned, chosen, base, patch_halves)
 
     row_ids = jnp.arange(rows, dtype=jnp.int32)
     image_ids, slot_ids = row_ids // SLOTS, row_ids % SLOTS
@@ -620,16 +907,22 @@
             raise_table[layer], model_index * local_hidden, local_hidden, 0
         )[None]
         middle, second, first, qkv, mixed = attention_forward(
-            every_tab, stream, vec, shift, bias, attention_halves[layer]
+            stream, vec, shift, bias, attention_halves[layer]
         )
-        pieces = group_pieces(second, x_masks)
-        steps = len(pieces) // 2
-        partials = [
-            hidden_forward(column_tab, pieces[k], pieces[steps + k], raise_row, hidden_halves[layer])
-            for k in range(steps)
-        ]
+        second = advance(later_moves, second)
+        if layer > 0:
+            hidden_halves.append((halves_tab,) + later_moves[layer - 1].finish())
+        outer = near_far(second, x_masks)
+        inner = [swap(outer[0], 1)]
+        partials = [hidden_forward(outer[0], inner[0], raise_row, hidden_halves[layer])]
+        partials, outer = advance(later_moves, (partials, outer))
+        for k in range(1, len(outer)):
+            inner.append(swap(outer[k], 1))
+            partials.append(hidden_forward(outer[k], inner[k], raise_row, hidden_halves[layer]))
+        pieces = (outer, inner)
         saved.append((stream, middle, first, qkv, mixed, pieces, vec, raise_row))
-        stream = middle + group_sum(partials, x_masks) + vec[5:6]
+        mlp_out = group_sum(partials, x_masks)
+        stream = middle + mlp_out + vec[5:6]
 
     lead_rows = stream[:real_rows].reshape(share_images, SLOTS, model_width)[:, 0]
     final_out, final_pull = jax.vjp(
@@ -644,9 +937,7 @@
     loss_local = jnp.sum(jax.nn.logsumexp(logits, -1) - jnp.sum(logits * target_hot, -1))
     logit_grad = (jax.nn.softmax(logits, -1) - target_hot) / total_images
     logit_low = logit_grad.astype(low_type)
-    final_every = gather_ordered(final_low, all_masks).reshape(-1, model_width)
-    logit_every = gather_ordered(logit_grad, all_masks).reshape(-1, CLASSES)
-    head_sum = head_gradient(final_every, logit_every)
+    head_every = gather_ordered(jnp.concatenate([final_low.astype(wide_type), logit_grad], 1))
     final_grad = product("nc,dc->nd", logit_low, head_low)
     lead_grad, gain_final, shift_final = final_pull(final_grad)
     upper = jnp.zeros((share_images, SLOTS, model_width), wide_type).at[:, 0].set(lead_grad)
@@ -654,35 +945,41 @@
     upper_low = upper.astype(low_type)
 
     vector_rows, shift_rows, raise_rows = [None] * LAYERS, [None] * LAYERS, [None] * LAYERS
-    attention_sums, hidden_sums = [None] * LAYERS, [None] * LAYERS
+    attention_moves, hidden_sums = [None] * LAYERS, [None] * LAYERS
+    waiting = None
     for layer in reversed(range(LAYERS)):
         stream_in, middle, first, qkv, mixed, pieces, vec, raise_row = saved[layer]
-        downs = group_pieces(upper_low, x_masks)
-        steps = len(pieces) // 2
+        outer, inner = pieces
+        outer_down = near_far(upper_low, x_masks)
+        inner_down = [swap(outer_down[0], 1)]
         partials, groups, raise_sum = [], [], 0.0
-        for k in range(steps):
+        if waiting is not None:
+            waiting, inner_down = together(waiting, inner_down)
+            attention_moves[layer + 1] = Transfer(reduce_all(waiting, turned_masks))
+        for k in range(len(outer)):
+            if k == 1:
+                partials, outer_down = advance(attention_moves[layer + 1 :], (partials, outer_down))
+            if k > 0:
+                inner_down.append(swap(outer_down[k], 1))
             kept, sent, active, grad, raise_part = hidden_chain(
-                column_tab,
-                pieces[k],
-                pieces[steps + k],
-                downs[k],
-                downs[steps + k],
-                raise_row,
-                hidden_halves[layer],
+                outer[k], inner[k], outer_down[k], inner_down[k], raise_row, hidden_halves[layer]
             )
             partials.append((kept, sent))
-            groups.append((pieces[k], pieces[steps + k], downs[k], downs[steps + k], active, grad))
+            groups.append((outer[k], inner[k], outer_down[k], inner_down[k], active, grad))
             raise_sum = raise_sum + raise_part
-        hidden_grads = hidden_weights(column_tab, groups, hidden_halves[layer][0].shape)
-        hidden_sums[layer] = reduce_halves(*hidden_grads, dp_masks)
+        hidden_grads = hidden_weights(column_tab, groups, (data,) + hidden_packs[0].shape)
         pull = group_sum(partials, x_masks)
+        pull, hidden_grads, head_every = together(pull, hidden_grads, head_every)
+        hidden_sums[layer] = lax.psum_scatter(hidden_grads, "dp", scatter_dimension=0).astype(wide_type)
         upper, upper_low, up, joined, tail = attention_chain(
-            every_tab, upper, pull, middle, stream_in, vec, bias, qkv, attention_halves[layer]
+            upper, pull, middle, stream_in, vec, bias, qkv, attention_halves[layer]
         )
-        attention_grads = attention_weights(
-            every_tab, first, joined, up, mixed, attention_halves[layer][0].shape
+        upper, upper_low, up, joined = advance(
+            attention_moves[layer + 1 :], (upper, upper_low, up, joined)
         )
-        attention_sums[layer] = reduce_halves(*attention_grads, all_masks)
+        waiting = attention_weights(
+            turned_tab if layer > 0 else every_tab, first, joined, up, mixed, (devices // 4, pack_rows, pack_width)
+        )
         vector_rows[layer], shift_rows[layer] = tail[:6], tail[6:]
         raise_rows[layer] = lax.dynamic_update_slice_in_dim(
             jnp.zeros((model, local_hidden), wide_type), raise_sum, model_index, 0
@@ -691,14 +988,6 @@
     place = lax.dot_general(
         spread, upper, (((0,), (0,)), ((), ())), precision=highest, preferred_element_type=wide_type
     )
-    patch_grad = lax.dot_general(
-        chosen, upper_low, (((0,), (0,)), ((), ())), preferred_element_type=wide_type
-    ).astype(low_type)
-    patch_blocks = patch_grad.reshape(devices, -1, model_width)
-    patch_blocks = patch_blocks.at[every].get(mode="promise_in_bounds")
-    half = devices // 2
-    patch_sum = reduce_halves(patch_blocks[:half], patch_blocks[half:], all_masks)
-
     small = jnp.concatenate(
         [
             place[PATCHES + 1 :],
@@ -714,20 +1003,33 @@
         + [jnp.zeros((1, model_width), wide_type).at[0, 0].set(loss_local)],
         0,
     )
-    small = sum_all(small)
+    patch_grads = embed_weights(turned, chosen, upper_low, patch_halves[0].shape)
+    patch_move = Transfer(reduce_quarters(patch_grads, turned_masks))
+    attention_move = Transfer(reduce_quarters(waiting, flip_masks))
+    small_move = Transfer(sum_steps(small))
+    while attention_move.wanted is not None:
+        advance([patch_move, attention_move, small_move] + attention_moves[1:])
+    head_sum = head_gradient(head_every[:, :model_width].astype(low_type), head_every[:, model_width:])
+    last_blocks = jnp.concatenate(
+        [attention_move.result, patch_move.result.reshape(data // sizes()[1], -1, pack_width)], 1
+    )
+    last_move = Transfer(reduce_z(last_blocks))
+    while last_move.wanted is not None:
+        advance([last_move, small_move] + attention_moves[1:])
+    last_sum, small = last_move.result, small_move.finish()
+    patch_sum = last_sum[pack_rows:].reshape(patch_weight.shape)
+    attention_sums = [last_sum[:pack_rows]] + [m.finish() for m in attention_moves[1:]]
+    joint_sum, output_sum, expand_sum, shrink_sum, shard_sq = unpack_grads(
+        jnp.stack(attention_sums), jnp.stack(hidden_sums), pack_rows, pack_width // 4, local_hidden
+    )
+    joint_sum = joint_sum.transpose(0, 2, 1, 3)
+
     vector_count = vector_table.shape[0]
     vector_sum = small[:vector_count]
     shift_sum = small[vector_count : vector_count + 2 * LAYERS].reshape(shift_table.shape)
     raise_sum = small[vector_count + 2 * LAYERS : -1].reshape(raise_table.shape)
     loss_total = small[-1, 0]
-    joint_sum = jnp.stack([total[:3].transpose(1, 0, 2) for total in attention_sums])
-    output_sum = jnp.stack([total[3].T for total in attention_sums])
-    expand_sum = jnp.stack([total[0] for total in hidden_sums])
-    shrink_sum = jnp.stack([total[1].T for total in hidden_sums])
-
-    sharded_sq = jnp.zeros((), wide_type)
-    for member in [patch_sum] + attention_sums + hidden_sums:
-        sharded_sq = sharded_sq + jnp.sum(member * member)
+    sharded_sq = shard_sq[0, 0] + jnp.sum(patch_sum * patch_sum)
     shared_sq = jnp.sum(head_sum * head_sum) + jnp.sum(small[:-1] * small[:-1])
     total_sq = sum_all(sharded_sq) + shared_sq
     gradient_norm = jnp.sqrt(total_sq)

time: 1000 us -> 812 us (0.81)
  waiting for transfers between devices: 454 us -> 328 us
  local copies, waits for them, and re-layouts: 133 us -> 58.4 us
  other arithmetic: 105 us -> 82.3 us
  Pallas kernels: 181 us -> 202 us
  starting transfers between devices: 83.4 us -> 98.7 us
  matrix products: 22.7 us -> 9.83 us
  between operations: 14 us -> 25 us
    ppermute x86 -> x84, waiting for transfers between devices: 454 us -> 321 us  [move(): return lax.ppermute(values, AXES, pairs)]
    unnamed x340 -> x276, local copies, waits for them, and re-layouts: 63.5 us -> 34 us
    add x23 -> x11, other arithmetic: 34.1 us -> 11.4 us  [the longest x3 6.72 us: reduce_quarters(): return sum((term.astype(wide_type) for term in terms))]
    pallas_call x12 -> x16, Pallas kernels: 143 us -> 164 us  [the longest x2 48.4 us: attention_chain(): call(functools.partial(attention_chain_kernel, len(halves)), [smem] + [vm...]
    convert_element_type x0 -> x12, other arithmetic: none -> 20.3 us  [the longest x3 10.5 us: reduce_quarters(): sent = (sent.astype(wide_type) + last.astype(wide_type)).astype(low_type)]
    concatenate x21 -> x3, other arithmetic: 20.7 us -> 0.89 us  [gather_ordered(): blocks = jnp.concatenate([blocks, swap(blocks, mask)], 0)]
    ppermute x86 -> x84, starting transfers between devices: 83.4 us -> 98.6 us  [move(): return lax.ppermute(values, AXES, pairs)]
    gather x4 -> x1, local copies, waits for them, and re-layouts: 17.5 us -> 3.59 us  [gather_ordered(): blocks.at[order].get(mode='promise_in_bounds')]
  transfers between devices with their start and end apart: 86 -> 88, of which waited for: 36 -> 46; matrix products, arithmetic and copies ran while one was open for 18% -> 9% of each run, Pallas kernels for 18% -> 21%
where the time goes in v3:
time: 812 us; the launch traced here: 805 us
  waiting for transfers between devices  328 us (40%)
  Pallas kernels  202 us (25%)
  starting transfers between devices  98.7 us (12%)
  other arithmetic  82.3 us (10%)
  local copies, waits for them, and re-layouts  58.4 us (7%)
  between operations  25 us (3%)
  matrix products  9.83 us (1%)
    ppermute x84, waiting for transfers between devices, move(): return lax.ppermute(values, AXES, pairs)  321 us
    ppermute x84, starting transfers between devices, move(): return lax.ppermute(values, AXES, pairs)  98.6 us
    pallas_call x2, Pallas kernels, attention_chain(): call(functools.partial(attention_chain_kernel, len(halves)), [smem] + [vm...  48.4 us
    pallas_call x2, Pallas kernels, attention_forward(): call(functools.partial(attention_forward_kernel, len(halves)), [smem] + [...  35.2 us
    pallas_call x4, Pallas kernels, hidden_chain(): call(functools.partial(hidden_chain_kernel, len(halves)), [smem] + [vmem]...  34.1 us
    unnamed x276, local copies, waits for them, and re-layouts  34 us
    pallas_call x4, Pallas kernels, hidden_forward(): call(functools.partial(hidden_forward_kernel, len(halves)), [smem] + [vme...  26.2 us
    sub x9, other arithmetic, adamw(): weight - rate * (corrected / (jnp.sqrt(scaled) + adam_eps) + decay_rate *...  25.1 us
  transfers between devices with their start and end apart: 88, of which 46 were waited for; matrix products, arithmetic and copies ran while one was open for 9% of the time, Pallas kernels for 21%

profile of v3, /device:TPU:0, one launch (start us, length us, event | category | flops | bytes accessed | tf_op | source)
XLA Modules:
  0.0 804.7 jit_solution(11324624671061157194)
XLA Ops:
  35.8 14.0 %collective-permute-done.3 = bf16[224,1024]{1,0:T(8,128)(2,1)S(1)} collective-permute-done((bf16[224,1024]{1,0:T(8,128)(2,1)S(1)}, bf16[224,1024]{1,0:T(8,128)(2,1)S(1)}, u32[]{:S(2)}, u32[]{:S(2)}) %collective-permute-start.3) | collective-permute-done | bytes 458784 | tf_op jit(solution)/shard_map/ppermute | solution.py:31
  52.5 10.8 %collective-permute-done.5 = bf16[224,1024]{1,0:T(8,128)(2,1)} collective-permute-done((bf16[224,1024]{1,0:T(8,128)(2,1)S(1)}, bf16[224,1024]{1,0:T(8,128)(2,1)}, u32[]{:S(2)}, u32[]{:S(2)}) %collective-permute-start.5) | collective-permute-done | bytes 458784 | tf_op jit(solution)/shard_map/ppermute | solution.py:31
  73.0 13.4 %collective-permute-done.6 = bf16[4,96,1024]{2,1,0:T(8,128)(2,1)S(1)} collective-permute-done((bf16[4,96,1024]{2,1,0:T(8,128)(2,1)S(1)}, bf16[4,96,1024]{2,1,0:T(8,128)(2,1)S(1)}, u32[]{:S(2)}, u32[]{:S(2)}) %collective-permute-start.6) | collective-permute-done | bytes 786464 | tf_op jit(solution)/shard_map/ppermute | solution.py:31
  86.4 10.0 %collective-permute-done.7 = bf16[4,128,1024]{2,1,0:T(8,128)(2,1)S(1)} collective-permute-done((bf16[4,128,1024]{2,1,0:T(8,128)(2,1)S(1)}, bf16[4,128,1024]{2,1,0:T(8,128)(2,1)S(1)}, u32[]{:S(2)}, u32[]{:S(2)}) %collective-permute-start.7) | collective-permute-done | bytes 1048608 | tf_op jit(solution)/shard_map/ppermute | solution.py:31
  112.1 18.1 %collective-permute-done.12 = bf16[128,2048]{1,0:T(8,128)(2,1)S(1)} collective-permute-done((bf16[128,2048]{1,0:T(8,128)(2,1)}, bf16[128,2048]{1,0:T(8,128)(2,1)S(1)}, u32[]{:S(2)}, u32[]{:S(2)}) %collective-permute-start.12) | collective-permute-done | bytes 524320 | tf_op jit(solution)/shard_map/ppermute | solution.py:31
  131.7 21.5 %collective-permute-done.13 = bf16[128,2048]{1,0:T(8,128)(2,1)} collective-permute-done((bf16[128,2048]{1,0:T(8,128)(2,1)}, bf16[128,2048]{1,0:T(8,128)(2,1)}, u32[]{:S(2)}, u32[]{:S(2)}) %collective-permute-start.13) | collective-permute-done | bytes 524320 | tf_op jit(solution)/shard_map/ppermute | solution.py:31
  172.2 18.1 %shard_map.583 = (f32[304,1024]{1,0:T(8,128)S(1)}, bf16[304,1024]{1,0:T(8,128)(2,1)S(1)}, bf16[304,1024]{1,0:T(8,128)(2,1)S(1)}, bf16[3,304,1024]{2,1,0:T(8,128)(2,1)}, bf16[304,1024]{1,0:T(8,128)(2,1)S(1)}) custom-call(s32[2,32]{1,0:T(2,128)S(1)} %pad_add_fusion.2.tab_ref, f32[304,1024]{1,0:T(8,128)S(1)} %shard_map.582.stream_ref, ...), custom_call_target="tpu_custom_call" | custom-call | flops 6375342080 | bytes 20971520 | tf_op jit(solution)/shard_map/pallas_call | solution.py:623
  204.0 14.4 %collective-permute-done.19 = bf16[128,2048]{1,0:T(8,128)(2,1)} collective-permute-done((bf16[128,2048]{1,0:T(8,128)(2,1)}, bf16[128,2048]{1,0:T(8,128)(2,1)}, u32[]{:S(2)}, u32[]{:S(2)}) %collective-permute-start.19) | collective-permute-done | bytes 524320 | tf_op jit(solution)/shard_map/ppermute | solution.py:31
  233.9 17.5 %collective-permute-done.25 = bf16[304,1024]{1,0:T(8,128)(2,1)S(1)} collective-permute-done((bf16[304,1024]{1,0:T(8,128)(2,1)S(1)}, bf16[304,1024]{1,0:T(8,128)(2,1)S(1)}, u32[]{:S(2)}, u32[]{:S(2)}) %collective-permute-start.25) | collective-permute-done | bytes 622624 | tf_op jit(solution)/shard_map/ppermute | solution.py:31
  259.9 17.0 %shard_map.586 = (f32[304,1024]{1,0:T(8,128)S(1)}, bf16[304,1024]{1,0:T(8,128)(2,1)S(1)}, bf16[304,1024]{1,0:T(8,128)(2,1)S(1)}, bf16[3,304,1024]{2,1,0:T(8,128)(2,1)}, bf16[304,1024]{1,0:T(8,128)(2,1)S(1)}) custom-call(s32[2,32]{1,0:T(2,128)S(1)} %pad_add_fusion.1.tab_ref, f32[304,1024]{1,0:T(8,128)S(1)} %add_add_fusion.stream_ref, ...), custom_call_target="tpu_custom_call" | custom-call | flops 6375342080 | bytes 20971520 | tf_op jit(solution)/shard_map/pallas_call | solution.py:623
  312.5 14.0 %collective-permute-done.32 = bf16[304,1024]{1,0:T(8,128)(2,1)} collective-permute-done((bf16[304,1024]{1,0:T(8,128)(2,1)S(1)}, bf16[304,1024]{1,0:T(8,128)(2,1)}, u32[]{:S(2)}, u32[]{:S(2)}) %collective-permute-start.32) | collective-permute-done | bytes 622624 | tf_op jit(solution)/shard_map/ppermute | solution.py:31
  381.9 10.0 %shard_map.591 = bf16[8,128,2048]{2,1,0:T(8,128)(2,1)} custom-call(s32[2,8]{1,0:T(2,128)S(1)} %copy-done.61, bf16[304,1024]{1,0:T(8,128)(2,1)S(1)} %copy-done.45, bf16[304,1024]{1,0:T(8,128)(2,1)S(1)} %copy-done.47, bf16[304,1024]{1,0:T(8,128)(2,1)S(1)} %pad.245.down_here_ref.refs_2_, bf16[304,1024]{1,0:T(8,128)(2,1)S(1)} %collective-permute-done.33.down_there_ref.refs_3_, ...), custom_call_target="tpu_custom_call" | custom-call | flops 10200547328 | bytes 20971520 | tf_op jit(solution)/shard_map/pallas_call | solution.py:718
  401.3 24.5 %shard_map.592 = (f32[304,1024]{1,0:T(8,128)S(1)}, bf16[304,1024]{1,0:T(8,128)(2,1)S(1)}, bf16[304,1024]{1,0:T(8,128)(2,1)S(1)}, bf16[3,304,1024]{2,1,0:T(8,128)(2,1)}, f32[8,1024]{1,0:T(8,128)S(1)}) custom-call(s32[2,32]{1,0:T(2,128)S(1)} %pad_add_fusion.1.tab_ref, f32[304,1024]{1,0:T(8,128)S(1)} %copy-done.20, f32[304,1024]{1,0:T(8,128)S(1)} %convert_add_fusion.4.pull_ref, ...), custom_call_target="tpu_custom_call" | custom-call | flops 9563013120 | bytes 31457280 | tf_op jit(solution)/shard_map/pallas_call | solution.py:642
  441.6 9.0 %shard_map.594 = (f32[304,1024]{1,0:T(8,128)S(1)}, bf16[304,1024]{1,0:T(8,128)(2,1)}, bf16[608,1024]{1,0:T(8,128)(2,1)S(1)}, bf16[608,1024]{1,0:T(8,128)(2,1)}, f32[1,1024]{1,0:T(1,128)S(1)}) custom-call(s32[2,8]{1,0:T(2,128)S(1)} %copy-done.61, bf16[304,1024]{1,0:T(8,128)(2,1)S(1)} %copy-done.33, bf16[304,1024]{1,0:T(8,128)(2,1)S(1)} %copy-done.36, ...), custom_call_target="tpu_custom_call" | custom-call | flops 6375342080 | bytes 20971520 | tf_op jit(solution)/shard_map/pallas_call | solution.py:698
  458.3 8.9 %shard_map.595 = (f32[304,1024]{1,0:T(8,128)S(1)}, bf16[304,1024]{1,0:T(8,128)(2,1)}, bf16[608,1024]{1,0:T(8,128)(2,1)S(1)}, bf16[608,1024]{1,0:T(8,128)(2,1)}, f32[1,1024]{1,0:T(1,128)S(1)}) custom-call(s32[2,8]{1,0:T(2,128)S(1)} %copy-done.61, bf16[304,1024]{1,0:T(8,128)(2,1)S(1)} %copy-done.39, bf16[304,1024]{1,0:T(8,128)(2,1)S(1)} %copy-done.42, ...), custom_call_target="tpu_custom_call" | custom-call | flops 6375342080 | bytes 20971520 | tf_op jit(solution)/shard_map/pallas_call | solution.py:698
  476.8 10.5 %shard_map.596 = bf16[8,128,2048]{2,1,0:T(8,128)(2,1)} custom-call(s32[2,8]{1,0:T(2,128)S(1)} %copy-done.61, bf16[304,1024]{1,0:T(8,128)(2,1)S(1)} %copy-done.34, bf16[304,1024]{1,0:T(8,128)(2,1)S(1)} %copy-done.37, bf16[304,1024]{1,0:T(8,128)(2,1)S(1)} %copy-done.53, bf16[304,1024]{1,0:T(8,128)(2,1)S(1)} %copy-done.56, bf16[608,1024]{1,0:T(8,128)(2,1)} %copy-done.67, ...), custom_call_target="tpu_custom_call" | custom-call | flops 10200547328 | bytes 20971520 | tf_op jit(solution)/shard_map/pallas_call | solution.py:718
  496.4 23.9 %shard_map.597 = (f32[304,1024]{1,0:T(8,128)S(1)}, bf16[304,1024]{1,0:T(8,128)(2,1)S(1)}, bf16[304,1024]{1,0:T(8,128)(2,1)S(1)}, bf16[3,304,1024]{2,1,0:T(8,128)(2,1)}, f32[8,1024]{1,0:T(8,128)S(1)}) custom-call(s32[2,32]{1,0:T(2,128)S(1)} %pad_add_fusion.2.tab_ref, f32[304,1024]{1,0:T(8,128)S(1)} %copy-done.79, f32[304,1024]{1,0:T(8,128)S(1)} %convert_add_fusion.3.pull_ref, ...), custom_call_target="tpu_custom_call" | custom-call | flops 9563013120 | bytes 31457280 | tf_op jit(solution)/shard_map/pallas_call | solution.py:642
  521.1 17.3 %collective-permute-done.48 = bf16[8,128,1024]{2,1,0:T(8,128)(2,1)} collective-permute-done((bf16[8,128,1024]{2,1,0:T(8,128)(2,1)}, bf16[8,128,1024]{2,1,0:T(8,128)(2,1)}, u32[]{:S(2)}, u32[]{:S(2)}) %collective-permute-start.48) | collective-permute-done | bytes 2097184 | tf_op jit(solution)/shard_map/ppermute | solution.py:31
  553.6 10.9 %shard_map.598 = (bf16[8,96,1024]{2,1,0:T(8,128)(2,1)S(1)}, bf16[8,96,1024]{2,1,0:T(8,128)(2,1)S(1)}, bf16[8,96,1024]{2,1,0:T(8,128)(2,1)}, bf16[8,96,1024]{2,1,0:T(8,128)(2,1)}) custom-call(s32[32]{0:T(128)S(1)} %get-tuple-element.422.tab_ref, bf16[304,3072]{1,0:T(8,128)(2,1)} %pad.45.chosen_ref, bf16[304,1024]{1,0:T(8,128)(2,1)S(1)} %copy-done.63), custom_call_target="tpu_custom_call" | custom-call | flops 1912602624 | bytes 12582912 | tf_op jit(solution)/shard_map/pallas_call | solution.py:610
  578.2 23.8 %collective-permute-done.58 = bf16[4,128,1024]{2,1,0:T(8,128)(2,1)S(1)} collective-permute-done((bf16[4,128,1024]{2,1,0:T(8,128)(2,1)}, bf16[4,128,1024]{2,1,0:T(8,128)(2,1)S(1)}, u32[]{:S(2)}, u32[]{:S(2)}) %collective-permute-start.58) | collective-permute-done | bytes 1048608 | tf_op jit(solution)/shard_map/ppermute | solution.py:31
  618.3 13.3 %collective-permute-done.62 = bf16[128,1024]{1,0:T(8,128)(2,1)S(1)} collective-permute-done((bf16[128,1024]{1,0:T(8,128)(2,1)S(1)}, bf16[128,1024]{1,0:T(8,128)(2,1)S(1)}, u32[]{:S(2)}, u32[]{:S(2)}) %collective-permute-start.62) | collective-permute-done | bytes 262176 | tf_op jit(solution)/shard_map/ppermute | solution.py:31
  636.1 16.2 %collective-permute-done.59 = bf16[8,96,1024]{2,1,0:T(8,128)(2,1)S(1)} collective-permute-done((bf16[8,96,1024]{2,1,0:T(8,128)(2,1)S(1)}, bf16[8,96,1024]{2,1,0:T(8,128)(2,1)S(1)}, u32[]{:S(2)}, u32[]{:S(2)}) %collective-permute-start.59) | collective-permute-done | bytes 1572896 | tf_op jit(solution)/shard_map/ppermute | solution.py:31
  675.2 14.4 %collective-permute-done.66 = f32[79,1024]{1,0:T(8,128)S(1)} collective-permute-done((f32[79,1024]{1,0:T(8,128)S(1)}, f32[79,1024]{1,0:T(8,128)S(1)}, u32[]{:S(2)}, u32[]{:S(2)}) %collective-permute-start.66) | collective-permute-done | bytes 323616 | tf_op jit(solution)/shard_map/ppermute | solution.py:31
  775.1 11.4 %multiply_subtract_fusion = (f32[1025,1000]{1,0:T(8,128)}, f32[1025,1000]{1,0:T(8,128)}, f32[1025,1000]{1,0:T(8,128)}) fusion(f32[1025,1000]{1,0:T(8,128)} %param.50, f32[1025,1000]{1,0:T(8,128)} %copy-done.2, f32[]{:T(128)S(6)} %min.3, f32[1025,1000]{1,0:T(8,128)} %param.59, f32[1025,1000]{1,0:T(8,128)} %param.68), kind=kLoop, calls=%fused_computation.10 | loop fusion | flops 16400000 | bytes 28700004 | tf_op jit(solution)/shard_map/sub | solution.py:794
  (609 shorter events, 416.7 us)
Async XLA Ops:
  7.2 190.4 %all-gather.3.cloned.1.call-start = ((), (), s32[]{:S(2)}) async-start(), calls=%async_computation.2 | async-start | bytes 4718592 | tf_op jit(solution)/shard_map/all_gather | solution.py:849
  64.2 194.7 %all-gather.5.cloned.1.call-start = ((), (), s32[]{:S(2)}) async-start(), calls=%async_computation.3 | async-start | bytes 8650752 | tf_op jit(solution)/shard_map/all_gather | solution.py:851
  66.0 675.9 %reduce-scatter.5.cloned.1.call-start = ((), (), s32[]{:S(2)}) async-start(), calls=%async_computation.5 | async-start | bytes 4718592 | tf_op jit(solution)/shard_map/reduce_scatter | solution.py:973
  68.9 27.5 %collective-permute-start.7 = (bf16[4,128,1024]{2,1,0:T(8,128)(2,1)S(1)}, bf16[4,128,1024]{2,1,0:T(8,128)(2,1)S(1)}, u32[]{:S(2)}, u32[]{:S(2)}) collective-permute-start(bf16[4,128,1024]{2,1,0:T(8,128)(2,1)S(1)} %slice.337), channel_id=1, source_target_pairs={{0,4},{1,5},{2,6},{3,7},{4,0},{5,1},{6,2},{7,3},{8,12},{9,13},{10,... | collective-permute-start | bytes 3145736 | tf_op jit(solution)/shard_map/ppermute | solution.py:31
  97.5 60.3 %collective-permute-start.10 = (bf16[8,128,1024]{2,1,0:T(8,128)(2,1)}, bf16[8,128,1024]{2,1,0:T(8,128)(2,1)}, u32[]{:S(2)}, u32[]{:S(2)}) collective-permute-start(bf16[8,128,1024]{2,1,0:T(8,128)(2,1)} %constant_dynamic-update-slice_fusion.2.refs_0_), channel_id=1, source_target_pairs={{0,2},{1,3},{2,0},{3,1},{4,6},{5,7},{6,4},{7,5},{8,10},{9,11},{10,... | collective-permute-start | bytes 6291464 | tf_op jit(solution)/shard_map/ppermute | solution.py:31
  99.0 58.8 %collective-permute-start.11 = (bf16[8,128,1024]{2,1,0:T(8,128)(2,1)}, bf16[8,128,1024]{2,1,0:T(8,128)(2,1)}, u32[]{:S(2)}, u32[]{:S(2)}) collective-permute-start(bf16[8,128,1024]{2,1,0:T(8,128)(2,1)} %constant_dynamic-update-slice_fusion.2.refs_0_), channel_id=1, source_target_pairs={{0,1},{1,0},{2,3},{3,2},{4,5},{5,4},{6,7},{7,6},{8,9},{9,8},{10,11... | collective-permute-start | bytes 6291464 | tf_op jit(solution)/shard_map/ppermute | solution.py:31
  102.3 55.4 %collective-permute-start.8 = (bf16[8,96,1024]{2,1,0:T(8,128)(2,1)}, bf16[8,96,1024]{2,1,0:T(8,128)(2,1)}, u32[]{:S(2)}, u32[]{:S(2)}) collective-permute-start(bf16[8,96,1024]{2,1,0:T(8,128)(2,1)} %constant_dynamic-update-slice_fusion.refs_0_), channel_id=1, source_target_pairs={{0,4},{1,5},{2,6},{3,7},{4,0},{5,1},{6,2},{7,3},{8,12},{9,13},{10,... | collective-permute-start | bytes 4718600 | tf_op jit(solution)/shard_map/ppermute | solution.py:31
  103.9 53.8 %collective-permute-start.9 = (bf16[8,96,1024]{2,1,0:T(8,128)(2,1)}, bf16[8,96,1024]{2,1,0:T(8,128)(2,1)}, u32[]{:S(2)}, u32[]{:S(2)}) collective-permute-start(bf16[8,96,1024]{2,1,0:T(8,128)(2,1)} %constant_dynamic-update-slice_fusion.refs_0_), channel_id=1, source_target_pairs={{0,1},{1,0},{2,3},{3,2},{4,5},{5,4},{6,7},{7,6},{8,9},{9,8},{10,11... | collective-permute-start | bytes 4718600 | tf_op jit(solution)/shard_map/ppermute | solution.py:31
  161.9 30.1 %collective-permute-start.16 = (bf16[128,2048]{1,0:T(8,128)(2,1)S(1)}, bf16[128,2048]{1,0:T(8,128)(2,1)S(1)}, u32[]{:S(2)}, u32[]{:S(2)}) collective-permute-start(bf16[128,2048]{1,0:T(8,128)(2,1)S(1)} %collective-permute-done.12), channel_id=1, source_target_pairs={{8,16},{9,17},{10,18},{11,19},{12,20},{13,21},{14,22},{15,23},{16,... | collective-permute-start | bytes 1572872 | tf_op jit(solution)/shard_map/ppermute | solution.py:31
  162.6 29.5 %collective-permute-start.17 = (bf16[128,2048]{1,0:T(8,128)(2,1)}, bf16[128,2048]{1,0:T(8,128)(2,1)S(1)}, u32[]{:S(2)}, u32[]{:S(2)}) collective-permute-start(bf16[128,2048]{1,0:T(8,128)(2,1)} %collective-permute-done.13), channel_id=1, source_target_pairs={{8,0},{9,1},{10,2},{11,3},{12,4},{13,5},{14,6},{15,7},{16,8},{17,9... | collective-permute-start | bytes 1572872 | tf_op jit(solution)/shard_map/ppermute | solution.py:31
  230.3 52.9 %collective-permute-start.26 = (bf16[4,128,2048]{2,1,0:T(8,128)(2,1)}, bf16[4,128,2048]{2,1,0:T(8,128)(2,1)}, u32[]{:S(2)}, u32[]{:S(2)}) collective-permute-start(bf16[4,128,2048]{2,1,0:T(8,128)(2,1)} %pad_maximum_fusion.refs_0_), channel_id=1, source_target_pairs={{0,4},{1,5},{2,6},{3,7},{4,0},{5,1},{6,2},{7,3},{8,12},{9,13},{10,... | collective-permute-start | bytes 6291464 | tf_op jit(solution)/shard_map/ppermute | solution.py:31
  373.6 25.9 %collective-permute-start.35 = (bf16[304,1024]{1,0:T(8,128)(2,1)S(1)}, bf16[304,1024]{1,0:T(8,128)(2,1)}, u32[]{:S(2)}, u32[]{:S(2)}) collective-permute-start(bf16[304,1024]{1,0:T(8,128)(2,1)S(1)} %get-tuple-element.279), channel_id=1, source_target_pairs={{0,1},{1,0},{2,3},{3,2},{4,5},{5,4},{6,7},{7,6},{8,9},{9,8},{10,11... | collective-permute-start | bytes 1867784 | tf_op jit(solution)/shard_map/ppermute | solution.py:31
  439.8 302.1 %reduce-scatter.3.cloned.1.call-start = ((), (), s32[]{:S(2)}) async-start(), calls=%async_computation.4 | async-start | bytes 4718592 | tf_op jit(solution)/shard_map/reduce_scatter | solution.py:973
  473.2 65.2 %collective-permute-start.48 = (bf16[8,128,1024]{2,1,0:T(8,128)(2,1)}, bf16[8,128,1024]{2,1,0:T(8,128)(2,1)}, u32[]{:S(2)}, u32[]{:S(2)}) collective-permute-start(bf16[8,128,1024]{2,1,0:T(8,128)(2,1)} %add_convert_fusion.1), channel_id=1, source_target_pairs={{0,4},{1,5},{2,6},{3,7},{4,0},{5,1},{6,2},{7,3},{8,12},{9,13},{10,... | collective-permute-start | bytes 6291464 | tf_op jit(solution)/shard_map/ppermute | solution.py:31
  549.9 52.1 %collective-permute-start.55 = (bf16[8,128,1024]{2,1,0:T(8,128)(2,1)}, bf16[8,128,1024]{2,1,0:T(8,128)(2,1)}, u32[]{:S(2)}, u32[]{:S(2)}) collective-permute-start(bf16[8,128,1024]{2,1,0:T(8,128)(2,1)} %get-tuple-element.340), channel_id=1, source_target_pairs={{0,1},{1,0},{2,3},{3,2},{4,5},{5,4},{6,7},{7,6},{8,9},{9,8},{10,11... | collective-permute-start | bytes 6291464 | tf_op jit(solution)/shard_map/ppermute | solution.py:31
  549.9 52.1 %collective-permute-start.56 = (bf16[8,128,1024]{2,1,0:T(8,128)(2,1)}, bf16[8,128,1024]{2,1,0:T(8,128)(2,1)}, u32[]{:S(2)}, u32[]{:S(2)}) collective-permute-start(bf16[8,128,1024]{2,1,0:T(8,128)(2,1)} %get-tuple-element.341), channel_id=1, source_target_pairs={{0,1},{1,0},{2,3},{3,2},{4,5},{5,4},{6,7},{7,6},{8,9},{9,8},{10,11... | collective-permute-start | bytes 6291464 | tf_op jit(solution)/shard_map/ppermute | solution.py:31
  565.8 36.2 %collective-permute-start.53 = (bf16[8,96,1024]{2,1,0:T(8,128)(2,1)}, bf16[8,96,1024]{2,1,0:T(8,128)(2,1)}, u32[]{:S(2)}, u32[]{:S(2)}) collective-permute-start(bf16[8,96,1024]{2,1,0:T(8,128)(2,1)} %get-tuple-element.334), channel_id=1, source_target_pairs={{0,1},{1,0},{2,3},{3,2},{4,5},{5,4},{6,7},{7,6},{8,9},{9,8},{10,11... | collective-permute-start | bytes 4718600 | tf_op jit(solution)/shard_map/ppermute | solution.py:31
  565.8 36.2 %collective-permute-start.54 = (bf16[8,96,1024]{2,1,0:T(8,128)(2,1)}, bf16[8,96,1024]{2,1,0:T(8,128)(2,1)}, u32[]{:S(2)}, u32[]{:S(2)}) collective-permute-start(bf16[8,96,1024]{2,1,0:T(8,128)(2,1)} %get-tuple-element.335), channel_id=1, source_target_pairs={{0,1},{1,0},{2,3},{3,2},{4,5},{5,4},{6,7},{7,6},{8,9},{9,8},{10,11... | collective-permute-start | bytes 4718600 | tf_op jit(solution)/shard_map/ppermute | solution.py:31
  605.5 46.8 %collective-permute-start.60 = (bf16[8,128,1024]{2,1,0:T(8,128)(2,1)S(1)}, bf16[8,128,1024]{2,1,0:T(8,128)(2,1)S(1)}, u32[]{:S(2)}, u32[]{:S(2)}) collective-permute-start(bf16[8,128,1024]{2,1,0:T(8,128)(2,1)S(1)} %add_convert_fusion), channel_id=1, source_target_pairs={{0,2},{1,3},{2,0},{3,1},{4,6},{5,7},{6,4},{7,5},{8,10},{9,11},{10,... | collective-permute-start | bytes 6291464 | tf_op jit(solution)/shard_map/ppermute | solution.py:31
  608.5 43.8 %collective-permute-start.59 = (bf16[8,96,1024]{2,1,0:T(8,128)(2,1)S(1)}, bf16[8,96,1024]{2,1,0:T(8,128)(2,1)S(1)}, u32[]{:S(2)}, u32[]{:S(2)}) collective-permute-start(bf16[8,96,1024]{2,1,0:T(8,128)(2,1)S(1)} %add_convert_fusion.2), channel_id=1, source_target_pairs={{0,4},{1,5},{2,6},{3,7},{4,0},{5,1},{6,2},{7,3},{8,12},{9,13},{10,... | collective-permute-start | bytes 4718600 | tf_op jit(solution)/shard_map/ppermute | solution.py:31
  609.1 27.0 %collective-permute-start.61 = (f32[79,1024]{1,0:T(8,128)S(1)}, f32[79,1024]{1,0:T(8,128)S(1)}, u32[]{:S(2)}, u32[]{:S(2)}) collective-permute-start(f32[79,1024]{1,0:T(8,128)S(1)} %add.596), channel_id=1, source_target_pairs={{0,16},{1,17},{2,18},{3,19},{4,20},{5,21},{6,22},{7,23},{8,24},{9,... | collective-permute-start | bytes 970760 | tf_op jit(solution)/shard_map/ppermute | solution.py:31
  654.2 35.4 %collective-permute-start.65 = (bf16[4,128,1024]{2,1,0:T(8,128)(2,1)S(1)}, bf16[4,128,1024]{2,1,0:T(8,128)(2,1)S(1)}, u32[]{:S(2)}, u32[]{:S(2)}) collective-permute-start(bf16[4,128,1024]{2,1,0:T(8,128)(2,1)S(1)} %add_convert_fusion.3), channel_id=1, source_target_pairs={{0,4},{1,5},{2,6},{3,7},{4,0},{5,1},{6,2},{7,3},{8,12},{9,13},{10,... | collective-permute-start | bytes 3145736 | tf_op jit(solution)/shard_map/ppermute | solution.py:31
  655.8 33.7 %collective-permute-start.64 = (bf16[4,96,1024]{2,1,0:T(8,128)(2,1)S(1)}, bf16[4,96,1024]{2,1,0:T(8,128)(2,1)S(1)}, u32[]{:S(2)}, u32[]{:S(2)}) collective-permute-start(bf16[4,96,1024]{2,1,0:T(8,128)(2,1)S(1)} %add_convert_fusion.5), channel_id=1, source_target_pairs={{0,2},{1,3},{2,0},{3,1},{4,6},{5,7},{6,4},{7,5},{8,10},{9,11},{10,... | collective-permute-start | bytes 2359304 | tf_op jit(solution)/shard_map/ppermute | solution.py:31
  657.1 32.5 %collective-permute-start.66 = (f32[79,1024]{1,0:T(8,128)S(1)}, f32[79,1024]{1,0:T(8,128)S(1)}, u32[]{:S(2)}, u32[]{:S(2)}) collective-permute-start(f32[79,1024]{1,0:T(8,128)S(1)} %add.602), channel_id=1, source_target_pairs={{0,4},{1,5},{2,6},{3,7},{4,0},{5,1},{6,2},{7,3},{8,12},{9,13},{10,... | collective-permute-start | bytes 970760 | tf_op jit(solution)/shard_map/ppermute | solution.py:31
  (200 other events, 2178.2 us)
Sparse Core Ops, SparseCore 0:
  64.3 98.3 all-gather.2
  166.1 92.7 all-gather.4
  439.9 103.7 reduce-scatter.4
  578.3 111.8 reduce-scatter.2

commit v4 on v3

--- a/solution.py
+++ b/solution.py
@@ -65,10 +65,12 @@
     return table
 
 
-def origins(masks):
+def origins(masks, early=()):
     deep, wide, across_x, stride = sizes()
     me = device_index()
-    places = [(flip, t) for flip in offsets(masks) for t in range(deep)]
+    places = [
+        (flip ^ first, t) for flip in offsets(masks) for t in range(deep) for first in offsets(early)
+    ]
     flips = jnp.array([flip for flip, t in places], jnp.int32)
     turns = jnp.array([t for flip, t in places], jnp.int32)
     return (me // stride + turns) % deep * stride + ((me % stride) ^ flips)
@@ -119,13 +121,11 @@
     return (yield from gather_flips(blocks, masks))
 
 
-def reduce_quarters(parts, masks):
-    kept, sent, kept_beside, sent_beside = parts
-    beside, last = yield [(kept_beside, across(masks[-1])), (sent_beside, across(masks[-1]))]
-    sent = (sent.astype(wide_type) + last.astype(wide_type)).astype(low_type)
-    (arrived,) = yield [(sent, across(masks[-2]))]
-    terms = [kept, beside, arrived]
-    for mask in reversed(masks[:-2]):
+def reduce_halves(parts, masks):
+    kept, sent = parts
+    (arrived,) = yield [(sent, across(masks[-1]))]
+    terms = [kept, arrived]
+    for mask in reversed(masks[:-1]):
         half = terms[0].shape[0] // 2
         sent = sum(term[half:].astype(wide_type) for term in terms).astype(low_type)
         kept = sum(term[:half].astype(wide_type) for term in terms)
@@ -140,17 +140,40 @@
     for k in range(deep - 1, 0, -1):
         rising, falling = blocks[k], blocks[deep - k]
         if up is not None:
-            rising, falling = rising + up.astype(wide_type), falling + down.astype(wide_type)
+            rising = rising.astype(wide_type) + up.astype(wide_type)
+            falling = falling.astype(wide_type) + down.astype(wide_type)
         up, down = yield [
             (rising.astype(low_type), along_z(1, 0, deep - 1 - k)),
             (falling.astype(low_type), along_z(-1, k, deep - 1)),
         ]
-    return blocks[0] + up.astype(wide_type) + down.astype(wide_type)
+    return blocks[0].astype(wide_type) + up.astype(wide_type) + down.astype(wide_type)
+
+
+def reduce_deep(blocks, early):
+    blocks = blocks.reshape((sizes()[0], -1) + blocks.shape[1:])
+    blocks = yield from reduce_z(blocks)
+    for mask in reversed(early):
+        half = blocks.shape[0] // 2
+        (arrived,) = yield [(blocks[half:].astype(low_type), across(mask))]
+        blocks = blocks[:half] + arrived.astype(wide_type)
+    return blocks[0]
 
 
 def reduce_all(parts, masks):
-    blocks = yield from reduce_quarters(parts, masks)
-    return (yield from reduce_z(blocks))
+    kept, sent = parts
+    half = sent.shape[0] // 2
+    (later,) = yield [(sent[half:], across(masks[-1]))]
+    (sooner,) = yield [(sent[:half], across(masks[-1]))]
+    onward = (kept[half:].astype(wide_type) + later.astype(wide_type)).astype(low_type)
+    (arrived,) = yield [(onward, across(masks[-2]))]
+    terms = [kept[:half], sooner, arrived]
+    for mask in reversed(masks[:-2]):
+        half = terms[0].shape[0] // 2
+        onward = sum(term[half:].astype(wide_type) for term in terms).astype(low_type)
+        kept = sum(term[:half].astype(wide_type) for term in terms)
+        (arrived,) = yield [(onward, across(mask))]
+        terms = [kept, arrived]
+    return (yield from reduce_z(sum(term.astype(wide_type) for term in terms)))
 
 
 class Transfer:
@@ -182,18 +205,24 @@
     return others
 
 
-def gather_ordered(values):
+def gather_rows(values):
     z_masks, y_masks, x_masks, c_masks = bit_masks()
     masks = z_masks + y_masks + x_masks + c_masks
     blocks = values[None]
     for mask in masks:
         blocks = jnp.concatenate([blocks, swap(blocks, mask)], 0)
+    return blocks
+
+
+def in_order(blocks):
+    z_masks, y_masks, x_masks, c_masks = bit_masks()
+    masks = z_masks + y_masks + x_masks + c_masks
     inverse = [0] * blocks.shape[0]
     for place, entry in enumerate(offsets(masks)):
         inverse[entry] = place
     places = jnp.array(inverse, jnp.int32)
     order = places.at[jnp.arange(len(inverse)) ^ device_index()].get(mode="promise_in_bounds")
-    return blocks.at[order].get(mode="promise_in_bounds").reshape((-1,) + values.shape[1:])
+    return blocks.at[order].get(mode="promise_in_bounds").reshape((-1,) + blocks.shape[2:])
 
 
 def together(*values):
@@ -203,8 +232,9 @@
 def sum_steps(values):
     for masks in bit_masks():
         for mask in masks:
-            (arrived,) = yield [(values, across(mask))]
-            values = values + arrived
+            rounded = values.astype(low_type)
+            (arrived,) = yield [(rounded, across(mask))]
+            values = rounded.astype(wide_type) + arrived.astype(wide_type)
     return values
 
 
@@ -308,10 +338,10 @@
     return (lane < HEAD_DIM, lane >= HEAD_DIM)
 
 
-def softmax_rows(query, keys, bias):
-    scores = dot_nt(query, keys) * 0.125 + bias
-    powers = jnp.exp(scores - jnp.max(scores, -1, keepdims=True))
-    return powers / jnp.sum(powers, -1, keepdims=True)
+def softmax_columns(keys, query, bias):
+    scores = dot_nt(keys, query) + bias
+    powers = jnp.exp(scores - jnp.max(scores, 0, keepdims=True))
+    return powers * (1.0 / jnp.sum(powers, 0, keepdims=True))
 
 
 def attention_forward_kernel(count, tab_ref, stream_ref, vec_ref, shift_ref, bias_ref, *refs):
@@ -329,15 +359,18 @@
     def pair(h, carry):
         at = pl.ds(pl.multiple_of(h * 128, 128), 128)
         query, keys, values = qkv_ref[0, :, at], qkv_ref[1, :, at], qkv_ref[2, :, at]
+        query = query * 0.125
         outs = []
         for lanes in lane_masks():
             own = jnp.where(lanes, query, jnp.zeros_like(query))
-            probs = softmax_rows(own, keys, bias_ref[...]).astype(low_type)
-            outs.append(dot_nn(probs, values))
+            scores = dot_nt(own, keys) + bias_ref[...]
+            powers = jnp.exp(scores - jnp.max(scores, -1, keepdims=True))
+            probs = powers * (1.0 / jnp.sum(powers, -1, keepdims=True))
+            outs.append(dot_nn(probs.astype(low_type), values))
         mixed_ref[:, at] = jnp.where(lane_masks()[0], outs[0], outs[1]).astype(low_type)
         return carry
 
-    lax.fori_loop(0, width // 128, pair, 0)
+    lax.fori_loop(0, width // 128, pair, 0, unroll=8)
     wait_weights(w_ref, sems, 3)
     for c in range(0, width, 256):
         middle_ref[:, c : c + 256] = (
@@ -374,26 +407,33 @@
         at = pl.ds(pl.multiple_of(h * 128, 128), 128)
         query, keys, values = qkv_ref[0, :, at], qkv_ref[1, :, at], qkv_ref[2, :, at]
         grads = mixed_grad_ref[:, at]
+        query = query * 0.125
+        turned = keys.T
         outs = []
-        for lanes in lane_masks():
+        for h, lanes in enumerate(lane_masks()):
             own = jnp.where(lanes, query, jnp.zeros_like(query))
             own_grad = jnp.where(lanes, grads, jnp.zeros_like(grads))
-            probs = softmax_rows(own, keys, bias_ref[...])
-            value_grad = dot_tn(probs.astype(low_type), grads)
-            prob_grad = dot_nt(own_grad, values)
-            weighted = probs * prob_grad
-            score_grad = (
-                (weighted - probs * jnp.sum(weighted, -1, keepdims=True)) * 0.125
-            ).astype(low_type)
-            outs.append((dot_nn(score_grad, keys), dot_tn(score_grad, query), value_grad))
+            probs = softmax_columns(keys, own, bias_ref[...])
+            value_grad = dot_nn(probs.astype(low_type), grads)
+            prob_grad = dot_nt(values, own_grad)
+            drift = jnp.sum(probs * prob_grad, 0, keepdims=True)
+            score_grad = (probs * (prob_grad - drift)).astype(low_type)
+            query_grad = dot_nn(turned[h * HEAD_DIM : (h + 1) * HEAD_DIM], score_grad)
+            outs.append((query_grad, dot_nn(score_grad, query), value_grad))
+        first_head = lane_masks()[0]
+        parts = (
+            jnp.concatenate([outs[0][0], outs[1][0]], 0).T * 0.125,
+            jnp.where(first_head, outs[0][1], outs[1][1]),
+            jnp.where(first_head, outs[0][2], outs[1][2]),
+        )
         for k in range(3):
-            part = jnp.where(lane_masks()[0], outs[0][k], outs[1][k])
+            part = parts[k]
             joined_ref[k, :, at] = part.astype(low_type)
             if k != 1:
                 rows_ref[6 + k // 2 : 7 + k // 2, at] = jnp.sum(part, 0, keepdims=True)
         return carry
 
-    lax.fori_loop(0, width // 128, pair, 0)
+    lax.fori_loop(0, width // 128, pair, 0, unroll=4)
     for k in range(3):
         wait_weights(w_ref, sems, k)
     for c in range(0, width, 256):
@@ -411,42 +451,62 @@
     below_low_ref[...] = below.astype(low_type)
 
 
-def attention_weights_kernel(tab_ref, first_ref, joined_ref, up_ref, mixed_ref, *refs):
-    g_ref, sems = refs[-2:]
-    width = first_ref.shape[1]
+def attention_weights_kernel(tab_ref, *refs):
+    half_a, half_b, g_ref, first_all, joined_all, up_all, mixed_all, sems = refs[8:]
+    rows, width = refs[0].shape
+    for side in range(2):
+        first_ref, joined_ref, up_ref, mixed_ref = refs[4 * side : 4 * side + 4]
+        at = slice(side * rows, (side + 1) * rows)
+        first_all[at, :] = first_ref[...]
+        up_all[at, :] = up_ref[...]
+        mixed_all[at, :] = mixed_ref[...]
+        for k in range(3):
+            joined_all[k, at, :] = joined_ref[k]
     for k in range(4):
         for c in range(0, width, 256):
             if k < 3:
-                part = dot_tn(first_ref[...], joined_ref[k, :, c : c + 256])
+                part = dot_tn(first_all[...], joined_all[k, :, c : c + 256])
             else:
-                part = dot_tn(up_ref[...], mixed_ref[:, c : c + 256])
+                part = dot_tn(up_all[...], mixed_all[:, c : c + 256])
             g_ref[k, :, c : c + 256] = part.astype(low_type)
-        store_grads(tab_ref, g_ref, refs[:-2], sems, k)
+        store_grads(tab_ref, g_ref, (half_a, half_b), sems, k)
+    done = g_ref.at[0, :, pl.ds(0, width // 2)]
     for k in range(4):
-        wait_weights(g_ref, sems, k)
-
-
-def pack_kernel(joint_ref, output_ref, expand_ref, shrink_ref, attention_ref, hidden_ref):
-    cut, local_hidden = joint_ref.shape[3], expand_ref.shape[2]
-    for layer in range(LAYERS):
+        pltpu.make_async_copy(done, done, sems.at[k]).wait()
+
+
+def pack_attention_kernel(joint_ref, output_ref, attention_ref):
+    cut = joint_ref.shape[3]
+    for layer in range(joint_ref.shape[0]):
         for k in range(3):
             attention_ref[layer, :, k * cut : (k + 1) * cut] = joint_ref[layer, k].astype(low_type)
         attention_ref[layer, :, 3 * cut :] = output_ref[layer].T.astype(low_type)
+
+
+def pack_hidden_kernel(expand_ref, shrink_ref, hidden_ref):
+    local_hidden = expand_ref.shape[2]
+    for layer in range(LAYERS):
         hidden_ref[layer, :, :local_hidden] = expand_ref[layer].astype(low_type)
         hidden_ref[layer, :, local_hidden:] = shrink_ref[layer].T.astype(low_type)
 
 
-def unpack_kernel(attention_ref, hidden_ref, joint_ref, output_ref, expand_ref, shrink_ref, square_ref):
-    cut, local_hidden = joint_ref.shape[3], expand_ref.shape[2]
+def unpack_attention_kernel(pack_ref, joint_ref, output_ref, square_ref):
+    cut = joint_ref.shape[2]
+    for k in range(3):
+        joint_ref[k] = pack_ref[:, k * cut : (k + 1) * cut]
+    output_ref[...] = pack_ref[:, 3 * cut :].T
+    square_ref[...] = jnp.sum(pack_ref[...] * pack_ref[...], keepdims=True)
+
+
+def unpack_hidden_kernel(*refs):
+    expand_ref, shrink_ref, square_ref = refs[LAYERS:]
+    local_hidden = expand_ref.shape[2]
     total = jnp.zeros((1, 1), wide_type)
-    for layer in range(LAYERS):
-        for k in range(3):
-            joint_ref[layer, k] = attention_ref[layer, :, k * cut : (k + 1) * cut]
-        output_ref[layer] = attention_ref[layer, :, 3 * cut :].T
-        expand_ref[layer] = hidden_ref[layer, :, :local_hidden]
-        shrink_ref[layer] = hidden_ref[layer, :, local_hidden:].T
-        for source in (attention_ref, hidden_ref):
-            total = total + jnp.sum(source[layer] * source[layer], keepdims=True)
+    for layer, pack_ref in enumerate(refs[:LAYERS]):
+        pack = pack_ref[...].astype(wide_type)
+        expand_ref[layer] = pack[:, :local_hidden]
+        shrink_ref[layer] = pack[:, local_hidden:].T
+        total = total + jnp.sum(pack * pack, keepdims=True)
     square_ref[...] = total
 
 
@@ -466,12 +526,18 @@
         out_ref[:, c : c + 256] = base_ref[:, c : c + 256] + dot_nn(chosen_ref[...], w_ref[:, c : c + 256])
 
 
-def embed_weights_kernel(tab_ref, chosen_ref, upper_ref, *refs):
-    g_ref, sem = refs[-2:]
-    count, rows, width = refs[0].shape
+def embed_weights_kernel(
+    tab_ref, chosen_ref, upper_ref, chosen_other, upper_other, half_a, half_b, g_ref, chosen_all, upper_all, sem
+):
+    count, rows, width = half_a.shape
+    depth = chosen_ref.shape[0]
+    chosen_all[0:depth, :] = chosen_ref[...]
+    chosen_all[depth : 2 * depth, :] = chosen_other[...]
+    upper_all[0:depth, :] = upper_ref[...]
+    upper_all[depth : 2 * depth, :] = upper_other[...]
     for c in range(0, width, 256):
-        g_ref[:, c : c + 256] = dot_tn(chosen_ref[...], upper_ref[:, c : c + 256]).astype(low_type)
-    for side, half in enumerate(refs[:-2]):
+        g_ref[:, c : c + 256] = dot_tn(chosen_all[...], upper_all[:, c : c + 256]).astype(low_type)
+    for side, half in enumerate((half_a, half_b)):
 
         def step(r, carry):
             row = pl.multiple_of(tab_ref[side * count + r] * rows, rows)
@@ -479,7 +545,8 @@
             return carry
 
         lax.fori_loop(0, count, step, 0)
-    pltpu.make_async_copy(g_ref, g_ref, sem).wait()
+    done = g_ref.at[pl.ds(0, 2 * count * rows)]
+    pltpu.make_async_copy(done, done, sem).wait()
 
 
 gelu_scale = 0.7978845608028654
@@ -598,23 +665,31 @@
     )(places, chosen, base, *halves)[0]
 
 
-def embed_weights(places, chosen, upper, half_shape):
+def embed_weights(places, chosen, upper, chosen_other, upper_other, half_shape):
     count, rows, width = half_shape
-    depth = chosen.shape[1]
+    depth, pixels = chosen.shape
     if rows % 16:
         full = lax.dot_general(
-            chosen, upper, (((0,), (0,)), ((), ())), preferred_element_type=wide_type
+            jnp.concatenate([chosen, chosen_other], 0),
+            jnp.concatenate([upper, upper_other], 0),
+            (((0,), (0,)), ((), ())),
+            preferred_element_type=wide_type,
         )
         blocks = full.astype(low_type).reshape(-1, rows, width)[places]
-        return tuple(blocks[k * count : (k + 1) * count] for k in range(4))
+        return blocks[:count], blocks[count:]
     return call(
         embed_weights_kernel,
-        [smem] + [vmem] * 2,
-        [(half_shape, low_type, anywhere)] * 4,
-        [pltpu.VMEM((depth, width), low_type), pltpu.SemaphoreType.DMA],
-        2 * chosen.shape[0] * depth * width,
-        4 * depth * width,
-    )(places, chosen, upper)
+        [smem] + [vmem] * 4,
+        [(half_shape, low_type, anywhere)] * 2,
+        [
+            pltpu.VMEM((pixels, width), low_type),
+            pltpu.VMEM((2 * depth, pixels), low_type),
+            pltpu.VMEM((2 * depth, width), low_type),
+            pltpu.SemaphoreType.DMA,
+        ],
+        4 * depth * pixels * width,
+        4 * pixels * width,
+    )(places, chosen, upper, chosen_other, upper_other)
 
 
 def attention_forward(stream, vec, shift, bias, gathered):
@@ -661,16 +736,23 @@
     )(tab, upper, pull, middle, stream, vec, bias, qkv, *halves)
 
 
-def attention_weights(tab, first, joined, up, mixed, half_shape):
-    rows, width = first.shape
+def attention_weights(tab, own, other, half_shape):
+    rows, width = own[0].shape
     return call(
         attention_weights_kernel,
-        [smem] + [vmem] * 4,
-        [(half_shape, low_type, anywhere)] * 4,
-        [pltpu.VMEM((4, width, width), low_type), pltpu.SemaphoreType.DMA((4,))],
+        [smem] + [vmem] * 8,
+        [(half_shape, low_type, anywhere)] * 2,
+        [
+            pltpu.VMEM((4, width, width), low_type),
+            pltpu.VMEM((2 * rows, width), low_type),
+            pltpu.VMEM((3, 2 * rows, width), low_type),
+            pltpu.VMEM((2 * rows, width), low_type),
+            pltpu.VMEM((2 * rows, width), low_type),
+            pltpu.SemaphoreType.DMA((4,)),
+        ],
         16 * rows * width * width,
         16 * width * width,
-    )(tab, first, joined, up, mixed)
+    )(tab, *own, *other)
 
 
 def hidden_forward(here, there, raise_row, gathered):
@@ -732,28 +814,50 @@
     )(tab, *[member for group in groups for member in group])[0]
 
 
-def pack_weights(joint, output, expand, shrink):
-    rows, cut, local_hidden = joint.shape[2], joint.shape[3], expand.shape[2]
+def pack_attention(joint, output):
+    layers, rows, cut = joint.shape[0], joint.shape[2], joint.shape[3]
     return call(
-        pack_kernel,
-        [vmem] * 4,
-        [
-            ((LAYERS, rows, 4 * cut), low_type, vmem),
-            ((LAYERS, rows, 2 * local_hidden), low_type, vmem),
-        ],
+        pack_attention_kernel,
+        [vmem] * 2,
+        [((layers, rows, 4 * cut), low_type, vmem)],
+        [],
+        1 << 20,
+        1 << 21,
+    )(joint, output)[0]
+
+
+def pack_hidden(expand, shrink):
+    layers, rows, local_hidden = expand.shape
+    return call(
+        pack_hidden_kernel,
+        [vmem] * 2,
+        [((layers, rows, 2 * local_hidden), low_type, vmem)],
         [],
         1 << 20,
         1 << 22,
-    )(joint, output, expand, shrink)
-
-
-def unpack_grads(attention, hidden, rows, cut, local_hidden):
+    )(expand, shrink)[0]
+
+
+def unpack_attention(pack):
+    rows, width = pack.shape
+    cut = width // 4
     return call(
-        unpack_kernel,
-        [vmem] * 2,
+        unpack_attention_kernel,
+        [vmem],
+        [((3, rows, cut), wide_type, vmem), ((cut, rows), wide_type, vmem), ((1, 1), wide_type, vmem)],
+        [],
+        1 << 20,
+        1 << 20,
+    )(pack)
+
+
+def unpack_hidden(packs):
+    rows, width = packs[0].shape
+    local_hidden = width // 2
+    return call(
+        unpack_hidden_kernel,
+        [vmem] * LAYERS,
         [
-            ((LAYERS, 3, rows, cut), wide_type, vmem),
-            ((LAYERS, cut, rows), wide_type, vmem),
             ((LAYERS, rows, local_hidden), wide_type, vmem),
             ((LAYERS, local_hidden, rows), wide_type, vmem),
             ((1, 1), wide_type, vmem),
@@ -761,7 +865,7 @@
         [],
         1 << 20,
         1 << 22,
-    )(attention, hidden)
+    )(*packs)
 
 
 def head_gradient(final_every, logit_every):
@@ -836,19 +940,20 @@
     column = jnp.arange(data, dtype=jnp.int32)
     column_tab = jnp.stack([column, jnp.zeros_like(column)])
 
-    attention_packs, hidden_packs = pack_weights(
-        joint_weight.transpose(0, 2, 1, 3), output_weight, expand_weight, shrink_weight
-    )
+    joint_rows = joint_weight.transpose(0, 2, 1, 3)
+    first_attention = pack_attention(joint_rows[:1], output_weight[:1])
+    attention_packs = pack_attention(joint_rows[1:], output_weight[1:])
+    hidden_packs = pack_hidden(expand_weight, shrink_weight)
     pack_rows, pack_width = attention_packs.shape[1:]
     first_pack = jnp.concatenate(
-        [attention_packs[0], patch_weight.astype(low_type).reshape(-1, pack_width)], 0
+        [first_attention[0], patch_weight.astype(low_type).reshape(-1, pack_width)], 0
     )
     first_move = Transfer(gather_z(first_pack))
     while first_move.wanted is not None:
         hidden_packs, attention_packs = advance([first_move], (hidden_packs, attention_packs))
     hidden_halves = [(column_tab, lax.all_gather(hidden_packs[0], "dp"))]
     attention_later = [
-        (direct_tab, lax.all_gather(attention_packs[layer], AXES)) for layer in range(1, LAYERS)
+        (direct_tab, lax.all_gather(attention_packs[layer - 1], AXES)) for layer in range(1, LAYERS)
     ]
     attention_blocks = first_move.result[:, :pack_rows]
     patch_blocks = first_move.result[:, pack_rows:].reshape(-1, *patch_weight.shape)
@@ -859,10 +964,11 @@
     patch_move = Transfer(gather_quarters(patch_blocks, turned_masks))
     later_moves = [Transfer(gather_all(later_packs[layer], y_masks)) for layer in range(1, LAYERS)]
     for step in range(len(flip_masks) - 2):
-        advance([patch_move, attention_move])
-    advance([patch_move, attention_move] + later_moves)
+        advance([patch_move, attention_move] + (later_moves if step == 0 else []))
+    advance([patch_move, attention_move])
     patch_halves, attention_first = patch_move.finish(), attention_move.finish()
     attention_halves = [(every_tab,) + attention_first] + attention_later
+    first_tab = jnp.stack([column_of(origins((), y_masks)), jnp.zeros_like(column)])
     halves_tab = jnp.stack([column_of(origins(y_masks)), jnp.zeros_like(column)])
 
     patch_ids = jnp.arange(PATCHES, dtype=jnp.int32)
@@ -888,13 +994,16 @@
         0,
     )
     base = jnp.dot(spread, sources, precision=highest)
+    chosen_other = swap(chosen, 1)
     stream = embed(turned, chosen, base, patch_halves)
 
     row_ids = jnp.arange(rows, dtype=jnp.int32)
     image_ids, slot_ids = row_ids // SLOTS, row_ids % SLOTS
     row_count = jnp.pad(jnp.repeat(keep_count, SLOTS), (0, rows - real_rows), constant_values=SLOTS)
-    live = (image_ids[:, None] == image_ids[None, :]) & (slot_ids <= row_count)[None, :]
-    bias = jnp.where(live, 0.0, -1e30).astype(wide_type)
+    same_image = image_ids[:, None] == image_ids[None, :]
+    live = slot_ids <= row_count
+    bias = jnp.where(same_image & live[None, :], 0.0, -1e30).astype(wide_type)
+    turned_bias = jnp.where(same_image & live[:, None], 0.0, -1e30).astype(wide_type)
 
     saved = []
     for layer in range(LAYERS):
@@ -920,7 +1029,8 @@
             inner.append(swap(outer[k], 1))
             partials.append(hidden_forward(outer[k], inner[k], raise_row, hidden_halves[layer]))
         pieces = (outer, inner)
-        saved.append((stream, middle, first, qkv, mixed, pieces, vec, raise_row))
+        beside = (swap(first, 1), swap(mixed, 1))
+        saved.append((stream, middle, first, qkv, mixed, beside, pieces, vec, raise_row))
         mlp_out = group_sum(partials, x_masks)
         stream = middle + mlp_out + vec[5:6]
 
@@ -937,7 +1047,7 @@
     loss_local = jnp.sum(jax.nn.logsumexp(logits, -1) - jnp.sum(logits * target_hot, -1))
     logit_grad = (jax.nn.softmax(logits, -1) - target_hot) / total_images
     logit_low = logit_grad.astype(low_type)
-    head_every = gather_ordered(jnp.concatenate([final_low.astype(wide_type), logit_grad], 1))
+    head_every = gather_rows(jnp.concatenate([final_low.astype(wide_type), logit_grad], 1))
     final_grad = product("nc,dc->nd", logit_low, head_low)
     lead_grad, gain_final, shift_final = final_pull(final_grad)
     upper = jnp.zeros((share_images, SLOTS, model_width), wide_type).at[:, 0].set(lead_grad)
@@ -948,17 +1058,17 @@
     attention_moves, hidden_sums = [None] * LAYERS, [None] * LAYERS
     waiting = None
     for layer in reversed(range(LAYERS)):
-        stream_in, middle, first, qkv, mixed, pieces, vec, raise_row = saved[layer]
+        stream_in, middle, first, qkv, mixed, beside, pieces, vec, raise_row = saved[layer]
         outer, inner = pieces
         outer_down = near_far(upper_low, x_masks)
         inner_down = [swap(outer_down[0], 1)]
         partials, groups, raise_sum = [], [], 0.0
         if waiting is not None:
             waiting, inner_down = together(waiting, inner_down)
-            attention_moves[layer + 1] = Transfer(reduce_all(waiting, turned_masks))
+            attention_moves[layer + 1] = Transfer(reduce_all(waiting, x_masks + y_masks))
         for k in range(len(outer)):
             if k == 1:
-                partials, outer_down = advance(attention_moves[layer + 1 :], (partials, outer_down))
+                partials, outer_down = together(partials, outer_down)
             if k > 0:
                 inner_down.append(swap(outer_down[k], 1))
             kept, sent, active, grad, raise_part = hidden_chain(
@@ -967,18 +1077,28 @@
             partials.append((kept, sent))
             groups.append((outer[k], inner[k], outer_down[k], inner_down[k], active, grad))
             raise_sum = raise_sum + raise_part
-        hidden_grads = hidden_weights(column_tab, groups, (data,) + hidden_packs[0].shape)
+        hidden_grads = hidden_weights(
+            column_tab if layer > 0 else first_tab, groups, (data,) + hidden_packs[0].shape
+        )
         pull = group_sum(partials, x_masks)
-        pull, hidden_grads, head_every = together(pull, hidden_grads, head_every)
-        hidden_sums[layer] = lax.psum_scatter(hidden_grads, "dp", scatter_dimension=0).astype(wide_type)
+        pull, hidden_grads, head_every = advance(
+            attention_moves[layer + 1 :], (pull, hidden_grads, head_every)
+        )
+        if layer > 0:
+            hidden_sums[layer] = lax.psum_scatter(hidden_grads, "dp", scatter_dimension=0)
+        else:
+            hidden_move = Transfer(reduce_deep(hidden_grads, y_masks))
         upper, upper_low, up, joined, tail = attention_chain(
-            upper, pull, middle, stream_in, vec, bias, qkv, attention_halves[layer]
+            upper, pull, middle, stream_in, vec, turned_bias, qkv, attention_halves[layer]
         )
         upper, upper_low, up, joined = advance(
             attention_moves[layer + 1 :], (upper, upper_low, up, joined)
         )
         waiting = attention_weights(
-            turned_tab if layer > 0 else every_tab, first, joined, up, mixed, (devices // 4, pack_rows, pack_width)
+            table(origins(x_masks + y_masks if layer > 0 else y_masks + x_masks)),
+            (first, joined, up, mixed),
+            (beside[0], swap(joined, 1), swap(up, 1), beside[1]),
+            (devices // 4, pack_rows, pack_width),
         )
         vector_rows[layer], shift_rows[layer] = tail[:6], tail[6:]
         raise_rows[layer] = lax.dynamic_update_slice_in_dim(
@@ -999,39 +1119,50 @@
         ]
         + vector_rows
         + shift_rows
-        + raise_rows
-        + [jnp.zeros((1, model_width), wide_type).at[0, 0].set(loss_local)],
+        + raise_rows,
         0,
     )
-    patch_grads = embed_weights(turned, chosen, upper_low, patch_halves[0].shape)
-    patch_move = Transfer(reduce_quarters(patch_grads, turned_masks))
-    attention_move = Transfer(reduce_quarters(waiting, flip_masks))
+    chosen, waiting = advance(attention_moves[1:], (chosen, waiting))
+    patch_grads = embed_weights(
+        origins(x_masks + y_masks), chosen, upper_low, chosen_other, swap(upper_low, 1), patch_halves[0].shape
+    )
+    patch_grads = advance(attention_moves[1:], patch_grads)
+    patch_move = Transfer(reduce_halves(patch_grads, x_masks + y_masks))
+    attention_move = Transfer(reduce_halves(waiting, y_masks + x_masks))
     small_move = Transfer(sum_steps(small))
+    head_every = in_order(head_every)
+    head_sum = head_gradient(head_every[:, :model_width].astype(low_type), head_every[:, model_width:])
+    head_sum = advance([patch_move, attention_move, hidden_move, small_move], head_sum)
     while attention_move.wanted is not None:
-        advance([patch_move, attention_move, small_move] + attention_moves[1:])
-    head_sum = head_gradient(head_every[:, :model_width].astype(low_type), head_every[:, model_width:])
+        advance([patch_move, attention_move, hidden_move, small_move])
     last_blocks = jnp.concatenate(
         [attention_move.result, patch_move.result.reshape(data // sizes()[1], -1, pack_width)], 1
     )
     last_move = Transfer(reduce_z(last_blocks))
+    advance([last_move, hidden_move, small_move])
+    advance([last_move, hidden_move] + attention_moves[1:])
     while last_move.wanted is not None:
         advance([last_move, small_move] + attention_moves[1:])
+    hidden_sums[0] = hidden_move.finish()
     last_sum, small = last_move.result, small_move.finish()
     patch_sum = last_sum[pack_rows:].reshape(patch_weight.shape)
     attention_sums = [last_sum[:pack_rows]] + [m.finish() for m in attention_moves[1:]]
-    joint_sum, output_sum, expand_sum, shrink_sum, shard_sq = unpack_grads(
-        jnp.stack(attention_sums), jnp.stack(hidden_sums), pack_rows, pack_width // 4, local_hidden
-    )
+    expand_sum, shrink_sum, shard_sq = unpack_hidden(hidden_sums)
+    unpacked = [unpack_attention(total) for total in attention_sums]
+    joint_sum = jnp.stack([member[0] for member in unpacked])
+    output_sum = jnp.stack([member[1] for member in unpacked])
+    for member in unpacked:
+        shard_sq = shard_sq + member[2]
     joint_sum = joint_sum.transpose(0, 2, 1, 3)
 
     vector_count = vector_table.shape[0]
     vector_sum = small[:vector_count]
     shift_sum = small[vector_count : vector_count + 2 * LAYERS].reshape(shift_table.shape)
-    raise_sum = small[vector_count + 2 * LAYERS : -1].reshape(raise_table.shape)
-    loss_total = small[-1, 0]
+    raise_sum = small[vector_count + 2 * LAYERS :].reshape(raise_table.shape)
     sharded_sq = shard_sq[0, 0] + jnp.sum(patch_sum * patch_sum)
-    shared_sq = jnp.sum(head_sum * head_sum) + jnp.sum(small[:-1] * small[:-1])
-    total_sq = sum_all(sharded_sq) + shared_sq
+    shared_sq = jnp.sum(head_sum * head_sum) + jnp.sum(small * small)
+    sums = sum_all(jnp.stack([sharded_sq, loss_local]))
+    total_sq, loss_total = sums[0] + shared_sq, sums[1]
     gradient_norm = jnp.sqrt(total_sq)
     factor = jnp.minimum(1.0, clip_limit / (gradient_norm + norm_eps))
     weights_in = (

time: 812 us -> 794 us (0.978)
  starting transfers between devices: 98.7 us -> 114 us
  Pallas kernels: 202 us -> 188 us
  other arithmetic: 82.3 us -> 68.7 us
  local copies, waits for them, and re-layouts: 58.4 us -> 45.1 us
  waiting for transfers between devices: 328 us -> 338 us
    unnamed x276 -> x250, local copies, waits for them, and re-layouts: 34 us -> 15.9 us
    ppermute x84 -> x96, starting transfers between devices: 98.6 us -> 114 us  [move(): return lax.ppermute(values, AXES, pairs)]
    convert_element_type x6 -> x7, other arithmetic: 17.4 us -> 5.6 us  [the longest x2 3.06 us: reduce_halves(): sum((term[half:].astype(wide_type) for term in terms)).astype(low_type)]
    pallas_call x2, Pallas kernels: 35.2 us -> 24.2 us  [attention_forward(): call(functools.partial(attention_forward_kernel, len(halves)), [smem] + [...]
    ppermute x84 -> x96, waiting for transfers between devices: 321 us -> 331 us  [move(): return lax.ppermute(values, AXES, pairs)]
    pallas_call x2, Pallas kernels: 48.4 us -> 39.3 us  [attention_chain(): call(functools.partial(attention_chain_kernel, len(halves)), [smem] + [vm...]
    pallas_call x5 -> x9, Pallas kernels: 30.9 us -> 37.8 us  [the longest x2 23.2 us: attention_weights(): call(attention_weights_kernel, [smem] + [vmem] * 8, [(half_shape, low_typ...]
  transfers between devices with their start and end apart: 88 -> 99, of which waited for: 46 -> 46; matrix products, arithmetic and copies ran while one was open for 9% -> 8% of each run, Pallas kernels for 21% -> 19%
where the time goes in v4:
time: 794 us; the launch traced here: 787 us
  waiting for transfers between devices  338 us (43%)
  Pallas kernels  188 us (24%)
  starting transfers between devices  114 us (14%)
  other arithmetic  68.7 us (9%)
  local copies, waits for them, and re-layouts  45.1 us (6%)
  between operations  23 us (3%)
  matrix products  9.84 us (1%)
    ppermute x96, waiting for transfers between devices, move(): return lax.ppermute(values, AXES, pairs)  331 us
    ppermute x96, starting transfers between devices, move(): return lax.ppermute(values, AXES, pairs)  114 us
    pallas_call x2, Pallas kernels, attention_chain(): call(functools.partial(attention_chain_kernel, len(halves)), [smem] + [vm...  39.3 us
    pallas_call x4, Pallas kernels, hidden_chain(): call(functools.partial(hidden_chain_kernel, len(halves)), [smem] + [vmem]...  33.7 us
    pallas_call x4, Pallas kernels, hidden_forward(): call(functools.partial(hidden_forward_kernel, len(halves)), [smem] + [vme...  25.5 us
    sub x9, other arithmetic, adamw(): weight - rate * (corrected / (jnp.sqrt(scaled) + adam_eps) + decay_rate *...  24.9 us
    pallas_call x2, Pallas kernels, attention_forward(): call(functools.partial(attention_forward_kernel, len(halves)), [smem] + [...  24.2 us
    pallas_call x2, Pallas kernels, attention_weights(): call(attention_weights_kernel, [smem] + [vmem] * 8, [(half_shape, low_typ...  23.2 us
  transfers between devices with their start and end apart: 99, of which 46 were waited for; matrix products, arithmetic and copies ran while one was open for 8% of the time, Pallas kernels for 19%

profile of v4, /device:TPU:0, one launch (start us, length us, event | category | flops | bytes accessed | tf_op | source)
XLA Modules:
  0.0 787.2 jit_solution(6479181034205091974)
XLA Ops:
  32.9 13.5 %collective-permute-done.3 = bf16[224,1024]{1,0:T(8,128)(2,1)S(1)} collective-permute-done((bf16[224,1024]{1,0:T(8,128)(2,1)}, bf16[224,1024]{1,0:T(8,128)(2,1)S(1)}, u32[]{:S(2)}, u32[]{:S(2)}) %collective-permute-start.3) | collective-permute-done | bytes 458784 | tf_op jit(solution)/shard_map/ppermute | solution.py:31
  49.1 10.8 %collective-permute-done.5 = bf16[224,1024]{1,0:T(8,128)(2,1)} collective-permute-done((bf16[224,1024]{1,0:T(8,128)(2,1)S(1)}, bf16[224,1024]{1,0:T(8,128)(2,1)}, u32[]{:S(2)}, u32[]{:S(2)}) %collective-permute-start.5) | collective-permute-done | bytes 458784 | tf_op jit(solution)/shard_map/ppermute | solution.py:31
  72.9 17.7 %collective-permute-done.8 = bf16[128,2048]{1,0:T(8,128)(2,1)} collective-permute-done((bf16[128,2048]{1,0:T(8,128)(2,1)S(1)}, bf16[128,2048]{1,0:T(8,128)(2,1)}, u32[]{:S(2)}, u32[]{:S(2)}) %collective-permute-start.8) | collective-permute-done | bytes 524320 | tf_op jit(solution)/shard_map/ppermute | solution.py:31
  104.3 54.2 %collective-permute-done.10.refs_1_ = bf16[8,96,1024]{2,1,0:T(8,128)(2,1)} collective-permute-done((bf16[8,96,1024]{2,1,0:T(8,128)(2,1)}, bf16[8,96,1024]{2,1,0:T(8,128)(2,1)}, u32[]{:S(2)}, u32[]{:S(2)}) %collective-permute-start.10) | collective-permute-done | bytes 1572896 | tf_op jit(solution)/shard_map/ppermute | solution.py:31
  177.5 12.3 %shard_map.657 = (f32[304,1024]{1,0:T(8,128)S(1)}, bf16[304,1024]{1,0:T(8,128)(2,1)S(1)}, bf16[304,1024]{1,0:T(8,128)(2,1)S(1)}, bf16[3,304,1024]{2,1,0:T(8,128)(2,1)}, bf16[304,1024]{1,0:T(8,128)(2,1)}) custom-call(s32[2,32]{1,0:T(2,128)S(1)} %pad_add_fusion.2.tab_ref, f32[304,1024]{1,0:T(8,128)S(1)} %shard_map.656.stream_ref, ...), custom_call_target="tpu_custom_call" | custom-call | flops 6375342080 | bytes 20971520 | tf_op jit(solution)/shard_map/pallas_call | solution.py:698
  204.4 13.5 %collective-permute-done.19 = bf16[128,2048]{1,0:T(8,128)(2,1)} collective-permute-done((bf16[128,2048]{1,0:T(8,128)(2,1)}, bf16[128,2048]{1,0:T(8,128)(2,1)}, u32[]{:S(2)}, u32[]{:S(2)}) %collective-permute-start.19) | collective-permute-done | bytes 524320 | tf_op jit(solution)/shard_map/ppermute | solution.py:31
  233.5 17.5 %collective-permute-done.25 = bf16[304,1024]{1,0:T(8,128)(2,1)S(1)} collective-permute-done((bf16[304,1024]{1,0:T(8,128)(2,1)S(1)}, bf16[304,1024]{1,0:T(8,128)(2,1)S(1)}, u32[]{:S(2)}, u32[]{:S(2)}) %collective-permute-start.25) | collective-permute-done | bytes 622624 | tf_op jit(solution)/shard_map/ppermute | solution.py:31
  258.4 11.9 %shard_map.660 = (f32[304,1024]{1,0:T(8,128)S(1)}, bf16[304,1024]{1,0:T(8,128)(2,1)S(1)}, bf16[304,1024]{1,0:T(8,128)(2,1)S(1)}, bf16[3,304,1024]{2,1,0:T(8,128)(2,1)}, bf16[304,1024]{1,0:T(8,128)(2,1)S(1)}) custom-call(s32[2,32]{1,0:T(2,128)S(1)} %pad_add_fusion.1.tab_ref, f32[304,1024]{1,0:T(8,128)S(1)} %add_add_fusion.stream_ref, ...), custom_call_target="tpu_custom_call" | custom-call | flops 6375342080 | bytes 20971520 | tf_op jit(solution)/shard_map/pallas_call | solution.py:698
  272.0 10.7 %collective-permute-done.26.refs_1_ = bf16[4,128,2048]{2,1,0:T(8,128)(2,1)} collective-permute-done((bf16[4,128,2048]{2,1,0:T(8,128)(2,1)}, bf16[4,128,2048]{2,1,0:T(8,128)(2,1)}, u32[]{:S(2)}, u32[]{:S(2)}) %collective-permute-start.26) | collective-permute-done | bytes 2097184 | tf_op jit(solution)/shard_map/ppermute | solution.py:31
  311.3 14.6 %collective-permute-done.32 = bf16[304,1024]{1,0:T(8,128)(2,1)S(1)} collective-permute-done((bf16[304,1024]{1,0:T(8,128)(2,1)S(1)}, bf16[304,1024]{1,0:T(8,128)(2,1)S(1)}, u32[]{:S(2)}, u32[]{:S(2)}) %collective-permute-start.32) | collective-permute-done | bytes 622624 | tf_op jit(solution)/shard_map/ppermute | solution.py:31
  342.8 8.9 %shard_map.663 = (f32[304,1024]{1,0:T(8,128)S(1)}, bf16[304,1024]{1,0:T(8,128)(2,1)}, bf16[608,1024]{1,0:T(8,128)(2,1)S(1)}, bf16[608,1024]{1,0:T(8,128)(2,1)}, f32[1,1024]{1,0:T(1,128)S(1)}) custom-call(s32[2,8]{1,0:T(2,128)S(1)} %stack.121.tab_ref, bf16[304,1024]{1,0:T(8,128)(2,1)S(1)} %copy-done.42, bf16[304,1024]{1,0:T(8,128)(2,1)S(1)} %copy-done.44, ...), custom_call_target="tpu_custom_call" | custom-call | flops 6375342080 | bytes 20971520 | tf_op jit(solution)/shard_map/pallas_call | solution.py:780
  377.5 10.0 %shard_map.665 = bf16[8,128,2048]{2,1,0:T(8,128)(2,1)} custom-call(s32[2,8]{1,0:T(2,128)S(1)} %copy-done.51, bf16[304,1024]{1,0:T(8,128)(2,1)S(1)} %copy-done.42, bf16[304,1024]{1,0:T(8,128)(2,1)S(1)} %copy-done.44, bf16[304,1024]{1,0:T(8,128)(2,1)S(1)} %pad.264.down_here_ref.refs_2_, bf16[304,1024]{1,0:T(8,128)(2,1)S(1)} %collective-permute-done.33.down_there_ref.refs_3_, ...), custom_call_target="tpu_custom_call" | custom-call | flops 10200547328 | bytes 20971520 | tf_op jit(solution)/shard_map/pallas_call | solution.py:800
  395.3 20.0 %shard_map.666 = (f32[304,1024]{1,0:T(8,128)S(1)}, bf16[304,1024]{1,0:T(8,128)(2,1)S(1)}, bf16[304,1024]{1,0:T(8,128)(2,1)S(1)}, bf16[3,304,1024]{2,1,0:T(8,128)(2,1)}, f32[8,1024]{1,0:T(8,128)S(1)}) custom-call(s32[2,32]{1,0:T(2,128)S(1)} %pad_add_fusion.1.tab_ref, f32[304,1024]{1,0:T(8,128)S(1)} %copy-done.12, f32[304,1024]{1,0:T(8,128)S(1)} %convert_add_fusion.7.pull_ref, ...), custom_call_target="tpu_custom_call" | custom-call | flops 9563013120 | bytes 31457280 | tf_op jit(solution)/shard_map/pallas_call | solution.py:717
  424.7 11.0 %shard_map.667 = (bf16[8,128,1024]{2,1,0:T(8,128)(2,1)}, bf16[8,128,1024]{2,1,0:T(8,128)(2,1)}) custom-call(s32[2,16]{1,0:T(2,128)S(1)} %pad_add_fusion.tab_ref, bf16[304,1024]{1,0:T(8,128)(2,1)S(1)} %copy-done.38, bf16[3,304,1024]{2,1,0:T(8,128)(2,1)S(1)} %copy-done.27, bf16[304,1024]{1,0:T(8,128)(2,1)S(1)} %get-tuple-element.281.refs_2_, ...), custom_call_target="tpu_custom_call" | custom-call | flops 5100273664 | bytes 16777216 | tf_op jit(solution)/shard_map/pallas_call | solution.py:741
  460.0 10.2 %shard_map.670 = bf16[8,128,2048]{2,1,0:T(8,128)(2,1)} custom-call(s32[2,8]{1,0:T(2,128)S(1)} %stack.127.tab_ref, bf16[304,1024]{1,0:T(8,128)(2,1)S(1)} %copy-done.32, bf16[304,1024]{1,0:T(8,128)(2,1)S(1)} %copy-done.34, bf16[304,1024]{1,0:T(8,128)(2,1)S(1)} %get-tuple-element.285.down_here_ref.refs_2_, ...), custom_call_target="tpu_custom_call" | custom-call | flops 10200547328 | bytes 20971520 | tf_op jit(solution)/shard_map/pallas_call | solution.py:800
  484.1 19.4 %shard_map.671 = (f32[304,1024]{1,0:T(8,128)S(1)}, bf16[304,1024]{1,0:T(8,128)(2,1)S(1)}, bf16[304,1024]{1,0:T(8,128)(2,1)}, bf16[3,304,1024]{2,1,0:T(8,128)(2,1)}, f32[8,1024]{1,0:T(8,128)S(1)}) custom-call(s32[2,32]{1,0:T(2,128)S(1)} %pad_add_fusion.2.tab_ref, f32[304,1024]{1,0:T(8,128)S(1)} %get-tuple-element.305.upper_ref, ...), custom_call_target="tpu_custom_call" | custom-call | flops 9563013120 | bytes 31457280 | tf_op jit(solution)/shard_map/pallas_call | solution.py:717
  516.8 12.2 %shard_map.672 = (bf16[8,128,1024]{2,1,0:T(8,128)(2,1)}, bf16[8,128,1024]{2,1,0:T(8,128)(2,1)}) custom-call(s32[2,16]{1,0:T(2,128)S(1)} %pad_add_fusion.3.tab_ref, bf16[304,1024]{1,0:T(8,128)(2,1)S(1)} %copy-done.30, bf16[3,304,1024]{2,1,0:T(8,128)(2,1)S(1)} %copy-done.26, bf16[304,1024]{1,0:T(8,128)(2,1)} %get-tuple-element.313.refs_2_, ...), custom_call_target="tpu_custom_call" | custom-call | flops 5100273664 | bytes 16777216 | tf_op jit(solution)/shard_map/pallas_call | solution.py:741
  544.0 11.0 %shard_map.673 = (bf16[8,96,1024]{2,1,0:T(8,128)(2,1)S(1)}, bf16[8,96,1024]{2,1,0:T(8,128)(2,1)}) custom-call(s32[16]{0:T(128)S(1)} %get-tuple-element.412.tab_ref, bf16[304,3072]{1,0:T(8,128)(2,1)} %pad.38.chosen_ref, bf16[304,1024]{1,0:T(8,128)(2,1)S(1)} %copy-done.48, bf16[304,3072]{1,0:T(8,128)(2,1)} %collective-permute-done.63.chosen_other, ...), custom_call_target="tpu_custom_call" | custom-call | flops 3825205248 | bytes 12582912 | tf_op jit(solution)/shard_map/pallas_call | solution.py:680
  576.8 9.4 %collective-permute-done.69 = bf16[78,1024]{1,0:T(8,128)(2,1)S(1)} collective-permute-done((bf16[78,1024]{1,0:T(8,128)(2,1)S(1)}, bf16[78,1024]{1,0:T(8,128)(2,1)S(1)}, u32[]{:S(2)}, u32[]{:S(2)}) %collective-permute-start.69) | collective-permute-done | bytes 159776 | tf_op jit(solution)/shard_map/ppermute | solution.py:31
  586.2 19.3 %collective-permute-done.65 = bf16[8,96,1024]{2,1,0:T(8,128)(2,1)} collective-permute-done((bf16[8,96,1024]{2,1,0:T(8,128)(2,1)}, bf16[8,96,1024]{2,1,0:T(8,128)(2,1)}, u32[]{:S(2)}, u32[]{:S(2)}) %collective-permute-start.65) | collective-permute-done | bytes 1572896 | tf_op jit(solution)/shard_map/ppermute | solution.py:31
  624.4 23.6 %collective-permute-done.74 = bf16[78,1024]{1,0:T(8,128)(2,1)S(1)} collective-permute-done((bf16[78,1024]{1,0:T(8,128)(2,1)S(1)}, bf16[78,1024]{1,0:T(8,128)(2,1)S(1)}, u32[]{:S(2)}, u32[]{:S(2)}) %collective-permute-start.74) | collective-permute-done | bytes 159776 | tf_op jit(solution)/shard_map/ppermute | solution.py:31
  667.8 14.4 %collective-permute-done.75 = bf16[224,1024]{1,0:T(8,128)(2,1)S(1)} collective-permute-done((bf16[224,1024]{1,0:T(8,128)(2,1)S(1)}, bf16[224,1024]{1,0:T(8,128)(2,1)S(1)}, u32[]{:S(2)}, u32[]{:S(2)}) %collective-permute-start.75) | collective-permute-done | bytes 458784 | tf_op jit(solution)/shard_map/ppermute | solution.py:31
  696.1 10.7 %collective-permute-start.85 = (bf16[224,1024]{1,0:T(8,128)(2,1)}, bf16[224,1024]{1,0:T(8,128)(2,1)}, u32[]{:S(2)}, u32[]{:S(2)}) collective-permute-start(bf16[224,1024]{1,0:T(8,128)(2,1)} %get-tuple-element.424), channel_id=1, source_target_pairs={{0,8},{1,9},{2,10},{3,11},{4,12},{5,13},{6,14},{7,15},{8,16},{9,17... | collective-permute-start | bytes 1376264 | tf_op jit(solution)/shard_map/ppermute | solution.py:31
  758.3 11.4 %multiply_subtract_fusion = (f32[1025,1000]{1,0:T(8,128)}, f32[1025,1000]{1,0:T(8,128)}, f32[1025,1000]{1,0:T(8,128)}) fusion(f32[1025,1000]{1,0:T(8,128)} %param.56, f32[1025,1000]{1,0:T(8,128)} %copy-done.2, f32[]{:T(128)S(6)} %min.3, f32[1025,1000]{1,0:T(8,128)} %param.65, f32[1025,1000]{1,0:T(8,128)} %param.74), kind=kLoop, calls=%fused_computation.10 | loop fusion | flops 16400000 | bytes 28700004 | tf_op jit(solution)/shard_map/sub | solution.py:898
  (624 shorter events, 396.2 us)
Async XLA Ops:
  7.2 190.9 %all-gather.3.cloned.1.call-start = ((), (), s32[]{:S(2)}) async-start(), calls=%async_computation.1 | async-start | bytes 4718592 | tf_op jit(solution)/shard_map/all_gather | solution.py:954
  60.8 196.5 %all-gather.5.cloned.1.call-start = ((), (), s32[]{:S(2)}) async-start(), calls=%async_computation.2 | async-start | bytes 8650752 | tf_op jit(solution)/shard_map/all_gather | solution.py:956
  61.6 653.7 %reduce-scatter.2.cloned.1.call-start = ((), (), s32[]{:S(2)}) async-start(), calls=%async_computation.3 | async-start | bytes 4718592 | tf_op jit(solution)/shard_map/reduce_scatter | solution.py:1088
  64.5 34.0 %collective-permute-start.7 = (bf16[4,128,1024]{2,1,0:T(8,128)(2,1)S(1)}, bf16[4,128,1024]{2,1,0:T(8,128)(2,1)S(1)}, u32[]{:S(2)}, u32[]{:S(2)}) collective-permute-start(bf16[4,128,1024]{2,1,0:T(8,128)(2,1)S(1)} %slice.344), channel_id=1, source_target_pairs={{0,4},{1,5},{2,6},{3,7},{4,0},{5,1},{6,2},{7,3},{8,12},{9,13},{10,... | collective-permute-start | bytes 3145736 | tf_op jit(solution)/shard_map/ppermute | solution.py:31
  66.0 32.4 %collective-permute-start.6 = (bf16[4,96,1024]{2,1,0:T(8,128)(2,1)S(1)}, bf16[4,96,1024]{2,1,0:T(8,128)(2,1)S(1)}, u32[]{:S(2)}, u32[]{:S(2)}) collective-permute-start(bf16[4,96,1024]{2,1,0:T(8,128)(2,1)S(1)} %pad_maximum_fusion.3), channel_id=1, source_target_pairs={{0,2},{1,3},{2,0},{3,1},{4,6},{5,7},{6,4},{7,5},{8,10},{9,11},{10,... | collective-permute-start | bytes 2359304 | tf_op jit(solution)/shard_map/ppermute | solution.py:31
  70.6 27.9 %collective-permute-start.9 = (bf16[128,2048]{1,0:T(8,128)(2,1)S(1)}, bf16[128,2048]{1,0:T(8,128)(2,1)}, u32[]{:S(2)}, u32[]{:S(2)}) collective-permute-start(bf16[128,2048]{1,0:T(8,128)(2,1)S(1)} %get-tuple-element.440), channel_id=1, source_target_pairs={{8,0},{9,1},{10,2},{11,3},{12,4},{13,5},{14,6},{15,7},{16,8},{17,9... | collective-permute-start | bytes 1572872 | tf_op jit(solution)/shard_map/ppermute | solution.py:31
  99.5 59.0 %collective-permute-start.12 = (bf16[8,128,1024]{2,1,0:T(8,128)(2,1)}, bf16[8,128,1024]{2,1,0:T(8,128)(2,1)}, u32[]{:S(2)}, u32[]{:S(2)}) collective-permute-start(bf16[8,128,1024]{2,1,0:T(8,128)(2,1)} %constant_dynamic-update-slice_fusion.2.refs_0_), channel_id=1, source_target_pairs={{0,2},{1,3},{2,0},{3,1},{4,6},{5,7},{6,4},{7,5},{8,10},{9,11},{10,... | collective-permute-start | bytes 6291464 | tf_op jit(solution)/shard_map/ppermute | solution.py:31
  101.1 57.4 %collective-permute-start.13 = (bf16[8,128,1024]{2,1,0:T(8,128)(2,1)}, bf16[8,128,1024]{2,1,0:T(8,128)(2,1)}, u32[]{:S(2)}, u32[]{:S(2)}) collective-permute-start(bf16[8,128,1024]{2,1,0:T(8,128)(2,1)} %constant_dynamic-update-slice_fusion.2.refs_0_), channel_id=1, source_target_pairs={{0,1},{1,0},{2,3},{3,2},{4,5},{5,4},{6,7},{7,6},{8,9},{9,8},{10,11... | collective-permute-start | bytes 6291464 | tf_op jit(solution)/shard_map/ppermute | solution.py:31
  102.9 55.5 %collective-permute-start.10 = (bf16[8,96,1024]{2,1,0:T(8,128)(2,1)}, bf16[8,96,1024]{2,1,0:T(8,128)(2,1)}, u32[]{:S(2)}, u32[]{:S(2)}) collective-permute-start(bf16[8,96,1024]{2,1,0:T(8,128)(2,1)} %constant_dynamic-update-slice_fusion.refs_0_), channel_id=1, source_target_pairs={{0,4},{1,5},{2,6},{3,7},{4,0},{5,1},{6,2},{7,3},{8,12},{9,13},{10,... | collective-permute-start | bytes 4718600 | tf_op jit(solution)/shard_map/ppermute | solution.py:31
  103.5 55.0 %collective-permute-start.11 = (bf16[8,96,1024]{2,1,0:T(8,128)(2,1)}, bf16[8,96,1024]{2,1,0:T(8,128)(2,1)}, u32[]{:S(2)}, u32[]{:S(2)}) collective-permute-start(bf16[8,96,1024]{2,1,0:T(8,128)(2,1)} %constant_dynamic-update-slice_fusion.refs_0_), channel_id=1, source_target_pairs={{0,1},{1,0},{2,3},{3,2},{4,5},{5,4},{6,7},{7,6},{8,9},{9,8},{10,11... | collective-permute-start | bytes 4718600 | tf_op jit(solution)/shard_map/ppermute | solution.py:31
  230.1 52.6 %collective-permute-start.26 = (bf16[4,128,2048]{2,1,0:T(8,128)(2,1)}, bf16[4,128,2048]{2,1,0:T(8,128)(2,1)}, u32[]{:S(2)}, u32[]{:S(2)}) collective-permute-start(bf16[4,128,2048]{2,1,0:T(8,128)(2,1)} %pad_maximum_fusion.refs_0_), channel_id=1, source_target_pairs={{0,4},{1,5},{2,6},{3,7},{4,0},{5,1},{6,2},{7,3},{8,12},{9,13},{10,... | collective-permute-start | bytes 6291464 | tf_op jit(solution)/shard_map/ppermute | solution.py:31
  457.7 47.4 %collective-permute-start.56 = (bf16[4,128,1024]{2,1,0:T(8,128)(2,1)}, bf16[4,128,1024]{2,1,0:T(8,128)(2,1)}, u32[]{:S(2)}, u32[]{:S(2)}) collective-permute-start(bf16[4,128,1024]{2,1,0:T(8,128)(2,1)} %get-tuple-element.435), channel_id=1, source_target_pairs={{0,4},{1,5},{2,6},{3,7},{4,0},{5,1},{6,2},{7,3},{8,12},{9,13},{10,... | collective-permute-start | bytes 3145736 | tf_op jit(solution)/shard_map/ppermute | solution.py:31
  505.6 38.4 %collective-permute-start.63 = (bf16[304,3072]{1,0:T(8,128)(2,1)}, bf16[304,3072]{1,0:T(8,128)(2,1)}, u32[]{:S(2)}, u32[]{:S(2)}) collective-permute-start(bf16[304,3072]{1,0:T(8,128)(2,1)} %pad.38.chosen_ref), channel_id=1, source_target_pairs={{0,1},{1,0},{2,3},{3,2},{4,5},{5,4},{6,7},{7,6},{8,9},{9,8},{10,11... | collective-permute-start | bytes 5603336 | tf_op jit(solution)/shard_map/ppermute | solution.py:31
  513.7 30.3 %collective-permute-start.64 = (bf16[304,1024]{1,0:T(8,128)(2,1)}, bf16[304,1024]{1,0:T(8,128)(2,1)S(1)}, u32[]{:S(2)}, u32[]{:S(2)}) collective-permute-start(bf16[304,1024]{1,0:T(8,128)(2,1)} %copy-done.47), channel_id=1, source_target_pairs={{0,1},{1,0},{2,3},{3,2},{4,5},{5,4},{6,7},{7,6},{8,9},{9,8},{10,11... | collective-permute-start | bytes 1867784 | tf_op jit(solution)/shard_map/ppermute | solution.py:31
  536.9 68.5 %collective-permute-start.66 = (bf16[8,128,1024]{2,1,0:T(8,128)(2,1)}, bf16[8,128,1024]{2,1,0:T(8,128)(2,1)}, u32[]{:S(2)}, u32[]{:S(2)}) collective-permute-start(bf16[8,128,1024]{2,1,0:T(8,128)(2,1)} %get-tuple-element.325), channel_id=1, source_target_pairs={{0,2},{1,3},{2,0},{3,1},{4,6},{5,7},{6,4},{7,5},{8,10},{9,11},{10,... | collective-permute-start | bytes 6291464 | tf_op jit(solution)/shard_map/ppermute | solution.py:31
  555.1 50.4 %collective-permute-start.65 = (bf16[8,96,1024]{2,1,0:T(8,128)(2,1)}, bf16[8,96,1024]{2,1,0:T(8,128)(2,1)}, u32[]{:S(2)}, u32[]{:S(2)}) collective-permute-start(bf16[8,96,1024]{2,1,0:T(8,128)(2,1)} %get-tuple-element.324), channel_id=1, source_target_pairs={{0,4},{1,5},{2,6},{3,7},{4,0},{5,1},{6,2},{7,3},{8,12},{9,13},{10,... | collective-permute-start | bytes 4718600 | tf_op jit(solution)/shard_map/ppermute | solution.py:31
  557.3 28.8 %collective-permute-start.67 = (bf16[2,128,2048]{2,1,0:T(8,128)(2,1)}, bf16[2,128,2048]{2,1,0:T(8,128)(2,1)}, u32[]{:S(2)}, u32[]{:S(2)}) collective-permute-start(bf16[2,128,2048]{2,1,0:T(8,128)(2,1)} %get-tuple-element.422), channel_id=1, source_target_pairs={{0,8},{1,9},{2,10},{3,11},{4,12},{5,13},{6,14},{7,15}} | collective-permute-start | bytes 3145736 | tf_op jit(solution)/shard_map/ppermute | solution.py:31
  607.1 40.9 %collective-permute-start.71 = (bf16[4,128,1024]{2,1,0:T(8,128)(2,1)S(1)}, bf16[4,128,1024]{2,1,0:T(8,128)(2,1)S(1)}, u32[]{:S(2)}, u32[]{:S(2)}) collective-permute-start(bf16[4,128,1024]{2,1,0:T(8,128)(2,1)S(1)} %add_convert_fusion.2), channel_id=1, source_target_pairs={{0,4},{1,5},{2,6},{3,7},{4,0},{5,1},{6,2},{7,3},{8,12},{9,13},{10,... | collective-permute-start | bytes 3145736 | tf_op jit(solution)/shard_map/ppermute | solution.py:31
  609.7 38.3 %collective-permute-start.72 = (bf16[2,128,2048]{2,1,0:T(8,128)(2,1)S(1)}, bf16[2,128,2048]{2,1,0:T(8,128)(2,1)S(1)}, u32[]{:S(2)}, u32[]{:S(2)}) collective-permute-start(bf16[2,128,2048]{2,1,0:T(8,128)(2,1)S(1)} %get-tuple-element.420), channel_id=1, source_target_pairs={{0,8},{1,9},{2,10},{3,11},{4,12},{5,13},{6,14},{7,15},{8,16},{9,17... | collective-permute-start | bytes 3145736 | tf_op jit(solution)/shard_map/ppermute | solution.py:31
  615.2 32.7 %collective-permute-start.73 = (bf16[2,128,2048]{2,1,0:T(8,128)(2,1)S(1)}, bf16[2,128,2048]{2,1,0:T(8,128)(2,1)S(1)}, u32[]{:S(2)}, u32[]{:S(2)}) collective-permute-start(bf16[2,128,2048]{2,1,0:T(8,128)(2,1)S(1)} %get-tuple-element.419), channel_id=1, source_target_pairs={{16,8},{17,9},{18,10},{19,11},{20,12},{21,13},{22,14},{23,15},{24,... | collective-permute-start | bytes 3145736 | tf_op jit(solution)/shard_map/ppermute | solution.py:31
  617.4 30.5 %collective-permute-start.70 = (bf16[4,96,1024]{2,1,0:T(8,128)(2,1)S(1)}, bf16[4,96,1024]{2,1,0:T(8,128)(2,1)S(1)}, u32[]{:S(2)}, u32[]{:S(2)}) collective-permute-start(bf16[4,96,1024]{2,1,0:T(8,128)(2,1)S(1)} %add_convert_fusion.4), channel_id=1, source_target_pairs={{0,2},{1,3},{2,0},{3,1},{4,6},{5,7},{6,4},{7,5},{8,10},{9,11},{10,... | collective-permute-start | bytes 2359304 | tf_op jit(solution)/shard_map/ppermute | solution.py:31
  619.6 28.4 %collective-permute-start.74 = (bf16[78,1024]{1,0:T(8,128)(2,1)S(1)}, bf16[78,1024]{1,0:T(8,128)(2,1)S(1)}, u32[]{:S(2)}, u32[]{:S(2)}) collective-permute-start(bf16[78,1024]{1,0:T(8,128)(2,1)S(1)} %add_convert_fusion.20), channel_id=1, source_target_pairs={{0,16},{1,17},{2,18},{3,19},{4,20},{5,21},{6,22},{7,23},{8,24},{9,... | collective-permute-start | bytes 479240 | tf_op jit(solution)/shard_map/ppermute | solution.py:31
  648.8 34.1 %collective-permute-start.77 = (bf16[2,128,2048]{2,1,0:T(8,128)(2,1)S(1)}, bf16[2,128,2048]{2,1,0:T(8,128)(2,1)S(1)}, u32[]{:S(2)}, u32[]{:S(2)}) collective-permute-start(bf16[2,128,2048]{2,1,0:T(8,128)(2,1)S(1)} %get-tuple-element.418), channel_id=1, source_target_pairs={{0,8},{1,9},{2,10},{3,11},{4,12},{5,13},{6,14},{7,15},{8,16},{9,17... | collective-permute-start | bytes 3145736 | tf_op jit(solution)/shard_map/ppermute | solution.py:31
  650.1 32.8 %collective-permute-start.78 = (bf16[2,128,2048]{2,1,0:T(8,128)(2,1)S(1)}, bf16[2,128,2048]{2,1,0:T(8,128)(2,1)S(1)}, u32[]{:S(2)}, u32[]{:S(2)}) collective-permute-start(bf16[2,128,2048]{2,1,0:T(8,128)(2,1)S(1)} %get-tuple-element.417), channel_id=1, source_target_pairs={{8,0},{9,1},{10,2},{11,3},{12,4},{13,5},{14,6},{15,7},{16,8},{17,9... | collective-permute-start | bytes 3145736 | tf_op jit(solution)/shard_map/ppermute | solution.py:31
  (198 other events, 2395.8 us)
Sparse Core Ops, SparseCore 0:
  60.9 101.7 all-gather.2
  166.2 91.1 all-gather.4
  511.9 107.6 reduce-scatter.1

commit v5 on v4

--- a/solution.py
+++ b/solution.py
@@ -1034,7 +1034,7 @@
         mlp_out = group_sum(partials, x_masks)
         stream = middle + mlp_out + vec[5:6]
 
-    lead_rows = stream[:real_rows].reshape(share_images, SLOTS, model_width)[:, 0]
+    lead_rows = stream[:real_rows:SLOTS]
     final_out, final_pull = jax.vjp(
         layer_norm, lead_rows, vector_table[SLOTS + 2], vector_table[SLOTS + 3]
     )
@@ -1050,8 +1050,10 @@
     head_every = gather_rows(jnp.concatenate([final_low.astype(wide_type), logit_grad], 1))
     final_grad = product("nc,dc->nd", logit_low, head_low)
     lead_grad, gain_final, shift_final = final_pull(final_grad)
-    upper = jnp.zeros((share_images, SLOTS, model_width), wide_type).at[:, 0].set(lead_grad)
-    upper = jnp.pad(upper.reshape(real_rows, model_width), ((0, rows - real_rows), (0, 0)))
+    last_row = (share_images - 1) * SLOTS + 1
+    upper = lax.pad(
+        lead_grad, jnp.zeros((), wide_type), ((0, rows - last_row, SLOTS - 1), (0, 0, 0))
+    )
     upper_low = upper.astype(low_type)
 
     vector_rows, shift_rows, raise_rows = [None] * LAYERS, [None] * LAYERS, [None] * LAYERS

time: 794 us -> 795 us (level)
    unnamed x250 -> x257, local copies, waits for them, and re-layouts: 15.9 us -> 17.9 us
where the time goes in v5:
time: 795 us; the launch traced here: 788 us
  waiting for transfers between devices  338 us (43%)
  Pallas kernels  188 us (24%)
  starting transfers between devices  116 us (15%)
  other arithmetic  68.3 us (9%)
  local copies, waits for them, and re-layouts  45.4 us (6%)
  between operations  23 us (3%)
  matrix products  9.84 us (1%)
    ppermute x96, waiting for transfers between devices, move(): return lax.ppermute(values, AXES, pairs)  331 us
    ppermute x96, starting transfers between devices, move(): return lax.ppermute(values, AXES, pairs)  116 us
    pallas_call x2, Pallas kernels, attention_chain(): call(functools.partial(attention_chain_kernel, len(halves)), [smem] + [vm...  39.3 us
    pallas_call x4, Pallas kernels, hidden_chain(): call(functools.partial(hidden_chain_kernel, len(halves)), [smem] + [vmem]...  33.7 us
    pallas_call x4, Pallas kernels, hidden_forward(): call(functools.partial(hidden_forward_kernel, len(halves)), [smem] + [vme...  25.5 us
    sub x9, other arithmetic, adamw(): weight - rate * (corrected / (jnp.sqrt(scaled) + adam_eps) + decay_rate *...  24.9 us
    pallas_call x2, Pallas kernels, attention_forward(): call(functools.partial(attention_forward_kernel, len(halves)), [smem] + [...  24.1 us
    pallas_call x2, Pallas kernels, attention_weights(): call(attention_weights_kernel, [smem] + [vmem] * 8, [(half_shape, low_typ...  22.9 us
  transfers between devices with their start and end apart: 99, of which 46 were waited for; matrix products, arithmetic and copies ran while one was open for 8% of the time, Pallas kernels for 19%

profile of v5, /device:TPU:0, one launch (start us, length us, event | category | flops | bytes accessed | tf_op | source)
XLA Modules:
  0.0 787.8 jit_solution(12002645286259435480)
XLA Ops:
  32.9 13.5 %collective-permute-done.3 = bf16[224,1024]{1,0:T(8,128)(2,1)S(1)} collective-permute-done((bf16[224,1024]{1,0:T(8,128)(2,1)}, bf16[224,1024]{1,0:T(8,128)(2,1)S(1)}, u32[]{:S(2)}, u32[]{:S(2)}) %collective-permute-start.3) | collective-permute-done | bytes 458784 | tf_op jit(solution)/shard_map/ppermute | solution.py:31
  49.2 10.8 %collective-permute-done.5 = bf16[224,1024]{1,0:T(8,128)(2,1)} collective-permute-done((bf16[224,1024]{1,0:T(8,128)(2,1)S(1)}, bf16[224,1024]{1,0:T(8,128)(2,1)}, u32[]{:S(2)}, u32[]{:S(2)}) %collective-permute-start.5) | collective-permute-done | bytes 458784 | tf_op jit(solution)/shard_map/ppermute | solution.py:31
  73.0 17.6 %collective-permute-done.8 = bf16[128,2048]{1,0:T(8,128)(2,1)} collective-permute-done((bf16[128,2048]{1,0:T(8,128)(2,1)S(1)}, bf16[128,2048]{1,0:T(8,128)(2,1)}, u32[]{:S(2)}, u32[]{:S(2)}) %collective-permute-start.8) | collective-permute-done | bytes 524320 | tf_op jit(solution)/shard_map/ppermute | solution.py:31
  104.4 54.1 %collective-permute-done.10.refs_1_ = bf16[8,96,1024]{2,1,0:T(8,128)(2,1)} collective-permute-done((bf16[8,96,1024]{2,1,0:T(8,128)(2,1)}, bf16[8,96,1024]{2,1,0:T(8,128)(2,1)}, u32[]{:S(2)}, u32[]{:S(2)}) %collective-permute-start.10) | collective-permute-done | bytes 1572896 | tf_op jit(solution)/shard_map/ppermute | solution.py:31
  177.5 12.3 %shard_map.657 = (f32[304,1024]{1,0:T(8,128)S(1)}, bf16[304,1024]{1,0:T(8,128)(2,1)S(1)}, bf16[304,1024]{1,0:T(8,128)(2,1)S(1)}, bf16[3,304,1024]{2,1,0:T(8,128)(2,1)}, bf16[304,1024]{1,0:T(8,128)(2,1)}) custom-call(s32[2,32]{1,0:T(2,128)S(1)} %pad_add_fusion.2.tab_ref, f32[304,1024]{1,0:T(8,128)S(1)} %shard_map.656.stream_ref, ...), custom_call_target="tpu_custom_call" | custom-call | flops 6375342080 | bytes 20971520 | tf_op jit(solution)/shard_map/pallas_call | solution.py:698
  204.4 13.6 %collective-permute-done.19 = bf16[128,2048]{1,0:T(8,128)(2,1)} collective-permute-done((bf16[128,2048]{1,0:T(8,128)(2,1)}, bf16[128,2048]{1,0:T(8,128)(2,1)}, u32[]{:S(2)}, u32[]{:S(2)}) %collective-permute-start.19) | collective-permute-done | bytes 524320 | tf_op jit(solution)/shard_map/ppermute | solution.py:31
  233.7 17.5 %collective-permute-done.25 = bf16[304,1024]{1,0:T(8,128)(2,1)S(1)} collective-permute-done((bf16[304,1024]{1,0:T(8,128)(2,1)S(1)}, bf16[304,1024]{1,0:T(8,128)(2,1)S(1)}, u32[]{:S(2)}, u32[]{:S(2)}) %collective-permute-start.25) | collective-permute-done | bytes 622624 | tf_op jit(solution)/shard_map/ppermute | solution.py:31
  258.7 11.9 %shard_map.660 = (f32[304,1024]{1,0:T(8,128)S(1)}, bf16[304,1024]{1,0:T(8,128)(2,1)S(1)}, bf16[304,1024]{1,0:T(8,128)(2,1)S(1)}, bf16[3,304,1024]{2,1,0:T(8,128)(2,1)}, bf16[304,1024]{1,0:T(8,128)(2,1)S(1)}) custom-call(s32[2,32]{1,0:T(2,128)S(1)} %pad_add_fusion.1.tab_ref, f32[304,1024]{1,0:T(8,128)S(1)} %add_add_fusion.1.stream_ref, ...), custom_call_target="tpu_custom_call" | custom-call | flops 6375342080 | bytes 20971520 | tf_op jit(solution)/shard_map/pallas_call | solution.py:698
  272.3 10.7 %collective-permute-done.26.refs_1_ = bf16[4,128,2048]{2,1,0:T(8,128)(2,1)} collective-permute-done((bf16[4,128,2048]{2,1,0:T(8,128)(2,1)}, bf16[4,128,2048]{2,1,0:T(8,128)(2,1)}, u32[]{:S(2)}, u32[]{:S(2)}) %collective-permute-start.26) | collective-permute-done | bytes 2097184 | tf_op jit(solution)/shard_map/ppermute | solution.py:31
  311.5 14.6 %collective-permute-done.32 = bf16[304,1024]{1,0:T(8,128)(2,1)S(1)} collective-permute-done((bf16[304,1024]{1,0:T(8,128)(2,1)S(1)}, bf16[304,1024]{1,0:T(8,128)(2,1)S(1)}, u32[]{:S(2)}, u32[]{:S(2)}) %collective-permute-start.32) | collective-permute-done | bytes 622624 | tf_op jit(solution)/shard_map/ppermute | solution.py:31
  343.0 8.9 %shard_map.663 = (f32[304,1024]{1,0:T(8,128)S(1)}, bf16[304,1024]{1,0:T(8,128)(2,1)}, bf16[608,1024]{1,0:T(8,128)(2,1)S(1)}, bf16[608,1024]{1,0:T(8,128)(2,1)}, f32[1,1024]{1,0:T(1,128)S(1)}) custom-call(s32[2,8]{1,0:T(2,128)S(1)} %stack.121.tab_ref, bf16[304,1024]{1,0:T(8,128)(2,1)S(1)} %copy-done.43, bf16[304,1024]{1,0:T(8,128)(2,1)S(1)} %copy-done.46, ...), custom_call_target="tpu_custom_call" | custom-call | flops 6375342080 | bytes 20971520 | tf_op jit(solution)/shard_map/pallas_call | solution.py:780
  378.4 10.0 %shard_map.665 = bf16[8,128,2048]{2,1,0:T(8,128)(2,1)} custom-call(s32[2,8]{1,0:T(2,128)S(1)} %copy-done.56, bf16[304,1024]{1,0:T(8,128)(2,1)S(1)} %copy-done.44, bf16[304,1024]{1,0:T(8,128)(2,1)S(1)} %copy-done.47, bf16[304,1024]{1,0:T(8,128)(2,1)S(1)} %convert_element_type.314.down_here_ref.refs_2_, ...), custom_call_target="tpu_custom_call" | custom-call | flops 10200547328 | bytes 20971520 | tf_op jit(solution)/shard_map/pallas_call | solution.py:800
  396.3 20.0 %shard_map.666 = (f32[304,1024]{1,0:T(8,128)S(1)}, bf16[304,1024]{1,0:T(8,128)(2,1)S(1)}, bf16[304,1024]{1,0:T(8,128)(2,1)S(1)}, bf16[3,304,1024]{2,1,0:T(8,128)(2,1)}, f32[8,1024]{1,0:T(8,128)S(1)}) custom-call(s32[2,32]{1,0:T(2,128)S(1)} %pad_add_fusion.1.tab_ref, f32[304,1024]{1,0:T(8,128)S(1)} %pad.38.upper_ref, ...), custom_call_target="tpu_custom_call" | custom-call | flops 9563013120 | bytes 31457280 | tf_op jit(solution)/shard_map/pallas_call | solution.py:717
  425.6 11.0 %shard_map.667 = (bf16[8,128,1024]{2,1,0:T(8,128)(2,1)}, bf16[8,128,1024]{2,1,0:T(8,128)(2,1)}) custom-call(s32[2,16]{1,0:T(2,128)S(1)} %pad_add_fusion.tab_ref, bf16[304,1024]{1,0:T(8,128)(2,1)S(1)} %copy-done.39, bf16[3,304,1024]{2,1,0:T(8,128)(2,1)S(1)} %copy-done.28, bf16[304,1024]{1,0:T(8,128)(2,1)S(1)} %get-tuple-element.269.refs_2_, ...), custom_call_target="tpu_custom_call" | custom-call | flops 5100273664 | bytes 16777216 | tf_op jit(solution)/shard_map/pallas_call | solution.py:741
  461.0 10.2 %shard_map.670 = bf16[8,128,2048]{2,1,0:T(8,128)(2,1)} custom-call(s32[2,8]{1,0:T(2,128)S(1)} %stack.127.tab_ref, bf16[304,1024]{1,0:T(8,128)(2,1)S(1)} %copy-done.33, bf16[304,1024]{1,0:T(8,128)(2,1)S(1)} %copy-done.35, bf16[304,1024]{1,0:T(8,128)(2,1)S(1)} %get-tuple-element.273.down_here_ref.refs_2_, ...), custom_call_target="tpu_custom_call" | custom-call | flops 10200547328 | bytes 20971520 | tf_op jit(solution)/shard_map/pallas_call | solution.py:800
  485.0 19.4 %shard_map.671 = (f32[304,1024]{1,0:T(8,128)S(1)}, bf16[304,1024]{1,0:T(8,128)(2,1)S(1)}, bf16[304,1024]{1,0:T(8,128)(2,1)}, bf16[3,304,1024]{2,1,0:T(8,128)(2,1)}, f32[8,1024]{1,0:T(8,128)S(1)}) custom-call(s32[2,32]{1,0:T(2,128)S(1)} %pad_add_fusion.2.tab_ref, f32[304,1024]{1,0:T(8,128)S(1)} %get-tuple-element.293.upper_ref, ...), custom_call_target="tpu_custom_call" | custom-call | flops 9563013120 | bytes 31457280 | tf_op jit(solution)/shard_map/pallas_call | solution.py:717
  517.7 11.9 %shard_map.672 = (bf16[8,128,1024]{2,1,0:T(8,128)(2,1)}, bf16[8,128,1024]{2,1,0:T(8,128)(2,1)}) custom-call(s32[2,16]{1,0:T(2,128)S(1)} %pad_add_fusion.3.tab_ref, bf16[304,1024]{1,0:T(8,128)(2,1)S(1)} %copy-done.31, bf16[3,304,1024]{2,1,0:T(8,128)(2,1)S(1)} %copy-done.27, bf16[304,1024]{1,0:T(8,128)(2,1)} %get-tuple-element.301.refs_2_, ...), custom_call_target="tpu_custom_call" | custom-call | flops 5100273664 | bytes 16777216 | tf_op jit(solution)/shard_map/pallas_call | solution.py:741
  545.0 11.0 %shard_map.673 = (bf16[8,96,1024]{2,1,0:T(8,128)(2,1)S(1)}, bf16[8,96,1024]{2,1,0:T(8,128)(2,1)}) custom-call(s32[16]{0:T(128)S(1)} %get-tuple-element.400.tab_ref, bf16[304,3072]{1,0:T(8,128)(2,1)} %pad.34.chosen_ref, bf16[304,1024]{1,0:T(8,128)(2,1)S(1)} %copy-done.53, bf16[304,3072]{1,0:T(8,128)(2,1)} %collective-permute-done.63.chosen_other, ...), custom_call_target="tpu_custom_call" | custom-call | flops 3825205248 | bytes 12582912 | tf_op jit(solution)/shard_map/pallas_call | solution.py:680
  577.7 9.4 %collective-permute-done.69 = bf16[78,1024]{1,0:T(8,128)(2,1)S(1)} collective-permute-done((bf16[78,1024]{1,0:T(8,128)(2,1)S(1)}, bf16[78,1024]{1,0:T(8,128)(2,1)S(1)}, u32[]{:S(2)}, u32[]{:S(2)}) %collective-permute-start.69) | collective-permute-done | bytes 159776 | tf_op jit(solution)/shard_map/ppermute | solution.py:31
  587.1 18.0 %collective-permute-done.65 = bf16[8,96,1024]{2,1,0:T(8,128)(2,1)} collective-permute-done((bf16[8,96,1024]{2,1,0:T(8,128)(2,1)}, bf16[8,96,1024]{2,1,0:T(8,128)(2,1)}, u32[]{:S(2)}, u32[]{:S(2)}) %collective-permute-start.65) | collective-permute-done | bytes 1572896 | tf_op jit(solution)/shard_map/ppermute | solution.py:31
  624.3 23.7 %collective-permute-done.74 = bf16[78,1024]{1,0:T(8,128)(2,1)S(1)} collective-permute-done((bf16[78,1024]{1,0:T(8,128)(2,1)S(1)}, bf16[78,1024]{1,0:T(8,128)(2,1)S(1)}, u32[]{:S(2)}, u32[]{:S(2)}) %collective-permute-start.74) | collective-permute-done | bytes 159776 | tf_op jit(solution)/shard_map/ppermute | solution.py:31
  667.8 14.9 %collective-permute-done.75 = bf16[224,1024]{1,0:T(8,128)(2,1)S(1)} collective-permute-done((bf16[224,1024]{1,0:T(8,128)(2,1)S(1)}, bf16[224,1024]{1,0:T(8,128)(2,1)S(1)}, u32[]{:S(2)}, u32[]{:S(2)}) %collective-permute-start.75) | collective-permute-done | bytes 458784 | tf_op jit(solution)/shard_map/ppermute | solution.py:31
  696.7 11.2 %collective-permute-start.85 = (bf16[224,1024]{1,0:T(8,128)(2,1)}, bf16[224,1024]{1,0:T(8,128)(2,1)}, u32[]{:S(2)}, u32[]{:S(2)}) collective-permute-start(bf16[224,1024]{1,0:T(8,128)(2,1)} %get-tuple-element.412), channel_id=1, source_target_pairs={{0,8},{1,9},{2,10},{3,11},{4,12},{5,13},{6,14},{7,15},{8,16},{9,17... | collective-permute-start | bytes 1376264 | tf_op jit(solution)/shard_map/ppermute | solution.py:31
  758.9 11.4 %multiply_subtract_fusion = (f32[1025,1000]{1,0:T(8,128)}, f32[1025,1000]{1,0:T(8,128)}, f32[1025,1000]{1,0:T(8,128)}) fusion(f32[1025,1000]{1,0:T(8,128)} %param.54, f32[1025,1000]{1,0:T(8,128)} %copy-done.2, f32[]{:T(128)S(6)} %min.3, f32[1025,1000]{1,0:T(8,128)} %param.63, f32[1025,1000]{1,0:T(8,128)} %param.72), kind=kLoop, calls=%fused_computation.10 | loop fusion | flops 16400000 | bytes 28700004 | tf_op jit(solution)/shard_map/sub | solution.py:898
  (629 shorter events, 397.2 us)
Async XLA Ops:
  7.2 190.9 %all-gather.3.cloned.1.call-start = ((), (), s32[]{:S(2)}) async-start(), calls=%async_computation.1 | async-start | bytes 4718592 | tf_op jit(solution)/shard_map/all_gather | solution.py:954
  60.8 196.8 %all-gather.5.cloned.1.call-start = ((), (), s32[]{:S(2)}) async-start(), calls=%async_computation.2 | async-start | bytes 8650752 | tf_op jit(solution)/shard_map/all_gather | solution.py:956
  61.6 654.8 %reduce-scatter.2.cloned.1.call-start = ((), (), s32[]{:S(2)}) async-start(), calls=%async_computation.3 | async-start | bytes 4718592 | tf_op jit(solution)/shard_map/reduce_scatter | solution.py:1090
  64.5 34.0 %collective-permute-start.7 = (bf16[4,128,1024]{2,1,0:T(8,128)(2,1)S(1)}, bf16[4,128,1024]{2,1,0:T(8,128)(2,1)S(1)}, u32[]{:S(2)}, u32[]{:S(2)}) collective-permute-start(bf16[4,128,1024]{2,1,0:T(8,128)(2,1)S(1)} %slice.321), channel_id=1, source_target_pairs={{0,4},{1,5},{2,6},{3,7},{4,0},{5,1},{6,2},{7,3},{8,12},{9,13},{10,... | collective-permute-start | bytes 3145736 | tf_op jit(solution)/shard_map/ppermute | solution.py:31
  66.1 32.4 %collective-permute-start.6 = (bf16[4,96,1024]{2,1,0:T(8,128)(2,1)S(1)}, bf16[4,96,1024]{2,1,0:T(8,128)(2,1)S(1)}, u32[]{:S(2)}, u32[]{:S(2)}) collective-permute-start(bf16[4,96,1024]{2,1,0:T(8,128)(2,1)S(1)} %pad_maximum_fusion.3), channel_id=1, source_target_pairs={{0,2},{1,3},{2,0},{3,1},{4,6},{5,7},{6,4},{7,5},{8,10},{9,11},{10,... | collective-permute-start | bytes 2359304 | tf_op jit(solution)/shard_map/ppermute | solution.py:31
  70.6 27.8 %collective-permute-start.9 = (bf16[128,2048]{1,0:T(8,128)(2,1)S(1)}, bf16[128,2048]{1,0:T(8,128)(2,1)}, u32[]{:S(2)}, u32[]{:S(2)}) collective-permute-start(bf16[128,2048]{1,0:T(8,128)(2,1)S(1)} %get-tuple-element.426), channel_id=1, source_target_pairs={{8,0},{9,1},{10,2},{11,3},{12,4},{13,5},{14,6},{15,7},{16,8},{17,9... | collective-permute-start | bytes 1572872 | tf_op jit(solution)/shard_map/ppermute | solution.py:31
  99.5 59.0 %collective-permute-start.12 = (bf16[8,128,1024]{2,1,0:T(8,128)(2,1)}, bf16[8,128,1024]{2,1,0:T(8,128)(2,1)}, u32[]{:S(2)}, u32[]{:S(2)}) collective-permute-start(bf16[8,128,1024]{2,1,0:T(8,128)(2,1)} %constant_dynamic-update-slice_fusion.2.refs_0_), channel_id=1, source_target_pairs={{0,2},{1,3},{2,0},{3,1},{4,6},{5,7},{6,4},{7,5},{8,10},{9,11},{10,... | collective-permute-start | bytes 6291464 | tf_op jit(solution)/shard_map/ppermute | solution.py:31
  101.1 57.4 %collective-permute-start.13 = (bf16[8,128,1024]{2,1,0:T(8,128)(2,1)}, bf16[8,128,1024]{2,1,0:T(8,128)(2,1)}, u32[]{:S(2)}, u32[]{:S(2)}) collective-permute-start(bf16[8,128,1024]{2,1,0:T(8,128)(2,1)} %constant_dynamic-update-slice_fusion.2.refs_0_), channel_id=1, source_target_pairs={{0,1},{1,0},{2,3},{3,2},{4,5},{5,4},{6,7},{7,6},{8,9},{9,8},{10,11... | collective-permute-start | bytes 6291464 | tf_op jit(solution)/shard_map/ppermute | solution.py:31
  102.9 55.5 %collective-permute-start.10 = (bf16[8,96,1024]{2,1,0:T(8,128)(2,1)}, bf16[8,96,1024]{2,1,0:T(8,128)(2,1)}, u32[]{:S(2)}, u32[]{:S(2)}) collective-permute-start(bf16[8,96,1024]{2,1,0:T(8,128)(2,1)} %constant_dynamic-update-slice_fusion.refs_0_), channel_id=1, source_target_pairs={{0,4},{1,5},{2,6},{3,7},{4,0},{5,1},{6,2},{7,3},{8,12},{9,13},{10,... | collective-permute-start | bytes 4718600 | tf_op jit(solution)/shard_map/ppermute | solution.py:31
  103.5 55.0 %collective-permute-start.11 = (bf16[8,96,1024]{2,1,0:T(8,128)(2,1)}, bf16[8,96,1024]{2,1,0:T(8,128)(2,1)}, u32[]{:S(2)}, u32[]{:S(2)}) collective-permute-start(bf16[8,96,1024]{2,1,0:T(8,128)(2,1)} %constant_dynamic-update-slice_fusion.refs_0_), channel_id=1, source_target_pairs={{0,1},{1,0},{2,3},{3,2},{4,5},{5,4},{6,7},{7,6},{8,9},{9,8},{10,11... | collective-permute-start | bytes 4718600 | tf_op jit(solution)/shard_map/ppermute | solution.py:31
  230.1 52.8 %collective-permute-start.26 = (bf16[4,128,2048]{2,1,0:T(8,128)(2,1)}, bf16[4,128,2048]{2,1,0:T(8,128)(2,1)}, u32[]{:S(2)}, u32[]{:S(2)}) collective-permute-start(bf16[4,128,2048]{2,1,0:T(8,128)(2,1)} %pad_maximum_fusion.refs_0_), channel_id=1, source_target_pairs={{0,4},{1,5},{2,6},{3,7},{4,0},{5,1},{6,2},{7,3},{8,12},{9,13},{10,... | collective-permute-start | bytes 6291464 | tf_op jit(solution)/shard_map/ppermute | solution.py:31
  458.7 47.4 %collective-permute-start.56 = (bf16[4,128,1024]{2,1,0:T(8,128)(2,1)}, bf16[4,128,1024]{2,1,0:T(8,128)(2,1)}, u32[]{:S(2)}, u32[]{:S(2)}) collective-permute-start(bf16[4,128,1024]{2,1,0:T(8,128)(2,1)} %get-tuple-element.423), channel_id=1, source_target_pairs={{0,4},{1,5},{2,6},{3,7},{4,0},{5,1},{6,2},{7,3},{8,12},{9,13},{10,... | collective-permute-start | bytes 3145736 | tf_op jit(solution)/shard_map/ppermute | solution.py:31
  506.6 38.4 %collective-permute-start.63 = (bf16[304,3072]{1,0:T(8,128)(2,1)}, bf16[304,3072]{1,0:T(8,128)(2,1)}, u32[]{:S(2)}, u32[]{:S(2)}) collective-permute-start(bf16[304,3072]{1,0:T(8,128)(2,1)} %pad.34.chosen_ref), channel_id=1, source_target_pairs={{0,1},{1,0},{2,3},{3,2},{4,5},{5,4},{6,7},{7,6},{8,9},{9,8},{10,11... | collective-permute-start | bytes 5603336 | tf_op jit(solution)/shard_map/ppermute | solution.py:31
  514.7 30.3 %collective-permute-start.64 = (bf16[304,1024]{1,0:T(8,128)(2,1)}, bf16[304,1024]{1,0:T(8,128)(2,1)S(1)}, u32[]{:S(2)}, u32[]{:S(2)}) collective-permute-start(bf16[304,1024]{1,0:T(8,128)(2,1)} %copy-done.52), channel_id=1, source_target_pairs={{0,1},{1,0},{2,3},{3,2},{4,5},{5,4},{6,7},{7,6},{8,9},{9,8},{10,11... | collective-permute-start | bytes 1867784 | tf_op jit(solution)/shard_map/ppermute | solution.py:31
  537.9 67.2 %collective-permute-start.66 = (bf16[8,128,1024]{2,1,0:T(8,128)(2,1)}, bf16[8,128,1024]{2,1,0:T(8,128)(2,1)}, u32[]{:S(2)}, u32[]{:S(2)}) collective-permute-start(bf16[8,128,1024]{2,1,0:T(8,128)(2,1)} %get-tuple-element.313), channel_id=1, source_target_pairs={{0,2},{1,3},{2,0},{3,1},{4,6},{5,7},{6,4},{7,5},{8,10},{9,11},{10,... | collective-permute-start | bytes 6291464 | tf_op jit(solution)/shard_map/ppermute | solution.py:31
  556.1 49.0 %collective-permute-start.65 = (bf16[8,96,1024]{2,1,0:T(8,128)(2,1)}, bf16[8,96,1024]{2,1,0:T(8,128)(2,1)}, u32[]{:S(2)}, u32[]{:S(2)}) collective-permute-start(bf16[8,96,1024]{2,1,0:T(8,128)(2,1)} %get-tuple-element.312), channel_id=1, source_target_pairs={{0,4},{1,5},{2,6},{3,7},{4,0},{5,1},{6,2},{7,3},{8,12},{9,13},{10,... | collective-permute-start | bytes 4718600 | tf_op jit(solution)/shard_map/ppermute | solution.py:31
  558.2 28.9 %collective-permute-start.67 = (bf16[2,128,2048]{2,1,0:T(8,128)(2,1)}, bf16[2,128,2048]{2,1,0:T(8,128)(2,1)}, u32[]{:S(2)}, u32[]{:S(2)}) collective-permute-start(bf16[2,128,2048]{2,1,0:T(8,128)(2,1)} %get-tuple-element.410), channel_id=1, source_target_pairs={{0,8},{1,9},{2,10},{3,11},{4,12},{5,13},{6,14},{7,15}} | collective-permute-start | bytes 3145736 | tf_op jit(solution)/shard_map/ppermute | solution.py:31
  606.7 41.2 %collective-permute-start.71 = (bf16[4,128,1024]{2,1,0:T(8,128)(2,1)S(1)}, bf16[4,128,1024]{2,1,0:T(8,128)(2,1)S(1)}, u32[]{:S(2)}, u32[]{:S(2)}) collective-permute-start(bf16[4,128,1024]{2,1,0:T(8,128)(2,1)S(1)} %add_convert_fusion.2), channel_id=1, source_target_pairs={{0,4},{1,5},{2,6},{3,7},{4,0},{5,1},{6,2},{7,3},{8,12},{9,13},{10,... | collective-permute-start | bytes 3145736 | tf_op jit(solution)/shard_map/ppermute | solution.py:31
  609.4 38.6 %collective-permute-start.72 = (bf16[2,128,2048]{2,1,0:T(8,128)(2,1)S(1)}, bf16[2,128,2048]{2,1,0:T(8,128)(2,1)S(1)}, u32[]{:S(2)}, u32[]{:S(2)}) collective-permute-start(bf16[2,128,2048]{2,1,0:T(8,128)(2,1)S(1)} %get-tuple-element.408), channel_id=1, source_target_pairs={{0,8},{1,9},{2,10},{3,11},{4,12},{5,13},{6,14},{7,15},{8,16},{9,17... | collective-permute-start | bytes 3145736 | tf_op jit(solution)/shard_map/ppermute | solution.py:31
  616.4 31.6 %collective-permute-start.73 = (bf16[2,128,2048]{2,1,0:T(8,128)(2,1)S(1)}, bf16[2,128,2048]{2,1,0:T(8,128)(2,1)S(1)}, u32[]{:S(2)}, u32[]{:S(2)}) collective-permute-start(bf16[2,128,2048]{2,1,0:T(8,128)(2,1)S(1)} %get-tuple-element.407), channel_id=1, source_target_pairs={{16,8},{17,9},{18,10},{19,11},{20,12},{21,13},{22,14},{23,15},{24,... | collective-permute-start | bytes 3145736 | tf_op jit(solution)/shard_map/ppermute | solution.py:31
  618.6 29.4 %collective-permute-start.70 = (bf16[4,96,1024]{2,1,0:T(8,128)(2,1)S(1)}, bf16[4,96,1024]{2,1,0:T(8,128)(2,1)S(1)}, u32[]{:S(2)}, u32[]{:S(2)}) collective-permute-start(bf16[4,96,1024]{2,1,0:T(8,128)(2,1)S(1)} %add_convert_fusion.4), channel_id=1, source_target_pairs={{0,2},{1,3},{2,0},{3,1},{4,6},{5,7},{6,4},{7,5},{8,10},{9,11},{10,... | collective-permute-start | bytes 2359304 | tf_op jit(solution)/shard_map/ppermute | solution.py:31
  620.2 27.8 %collective-permute-start.74 = (bf16[78,1024]{1,0:T(8,128)(2,1)S(1)}, bf16[78,1024]{1,0:T(8,128)(2,1)S(1)}, u32[]{:S(2)}, u32[]{:S(2)}) collective-permute-start(bf16[78,1024]{1,0:T(8,128)(2,1)S(1)} %add_convert_fusion.20), channel_id=1, source_target_pairs={{0,16},{1,17},{2,18},{3,19},{4,20},{5,21},{6,22},{7,23},{8,24},{9,... | collective-permute-start | bytes 479240 | tf_op jit(solution)/shard_map/ppermute | solution.py:31
  648.8 34.7 %collective-permute-start.77 = (bf16[2,128,2048]{2,1,0:T(8,128)(2,1)S(1)}, bf16[2,128,2048]{2,1,0:T(8,128)(2,1)S(1)}, u32[]{:S(2)}, u32[]{:S(2)}) collective-permute-start(bf16[2,128,2048]{2,1,0:T(8,128)(2,1)S(1)} %get-tuple-element.406), channel_id=1, source_target_pairs={{0,8},{1,9},{2,10},{3,11},{4,12},{5,13},{6,14},{7,15},{8,16},{9,17... | collective-permute-start | bytes 3145736 | tf_op jit(solution)/shard_map/ppermute | solution.py:31
  650.1 33.3 %collective-permute-start.78 = (bf16[2,128,2048]{2,1,0:T(8,128)(2,1)S(1)}, bf16[2,128,2048]{2,1,0:T(8,128)(2,1)S(1)}, u32[]{:S(2)}, u32[]{:S(2)}) collective-permute-start(bf16[2,128,2048]{2,1,0:T(8,128)(2,1)S(1)} %get-tuple-element.405), channel_id=1, source_target_pairs={{8,0},{9,1},{10,2},{11,3},{12,4},{13,5},{14,6},{15,7},{16,8},{17,9... | collective-permute-start | bytes 3145736 | tf_op jit(solution)/shard_map/ppermute | solution.py:31
  (202 other events, 2420.7 us)
Sparse Core Ops, SparseCore 0:
  61.0 101.7 all-gather.2
  166.2 91.4 all-gather.4
  512.8 106.5 reduce-scatter.1
